TPU v7x, 128 devices: a whole 4x4x4 slice. The times are simulated.
128 devices in a mesh: row: 16 (over x, z_lo, core), col: 8 (over z_hi, y).
Axes of the slice: x: 4, y: 4, z: 4 (z_hi: 2, z_lo: 2; z = z_hi * 2 + z_lo), core: 2. Of those that a mesh axis runs over, the one named last changes fastest.
Arguments:
- alignment: bfloat16 [640, 512, 256], P('col', 'row'), may hold values from -6 to 6
- pairwise: bfloat16 [512, 512, 128], P('row', 'col'), may hold values from -6 to 6
- residue_mask: int32 [512], replicated, may hold values 0 or 1
- sequence_mask: int32 [640], replicated, may hold values 0 or 1
- attention_input_weight: bfloat16 [256, 4, 256], replicated, may hold values from -0.375 to 0.375
- attention_output_weight: bfloat16 [256, 256], replicated, may hold values from -1 to 1
- bias_project: bfloat16 [128, 8], replicated, may hold values from -100 to 100
- outer_factor_weight: bfloat16 [256, 2, 32], replicated, may hold values from -0.375 to 0.375
- outer_output: bfloat16 [1024, 128], replicated, may hold values from -1 to 1
- tri_project: bfloat16 [128, 4, 128], replicated, may hold values from -0.5 to 0.5
- tri_gate: bfloat16 [128, 128], replicated, may hold values from -0.5 to 0.5
- tri_output: bfloat16 [128, 128], replicated, may hold values from -0.5 to 0.5
Outputs:
- alignment_output: bfloat16 [640, 512, 256], P('col', 'row')
- pair_output_state: bfloat16 [512, 512, 128], P('row', 'col')
All inputs are finite; a program needn't handle non-finite values.
Results may differ from a plain program's by a relative error of at most 0.017.
Values may be sent and summed in bfloat16 or wider, within the bound.
No kernel may reach another device: no remote copies, remote signals or barrier semaphores. Data moves between devices by JAX's collectives and lax.ppermute only.
A program may use at most 128 MiB of HBM per device.

v0:
```python
import jax
import jax.numpy as jnp
from jax import lax
from jax.sharding import PartitionSpec as P

EPS = 1e-05
BIG = 1000000000.0


def from_root(value, axis, source):
    kept = jnp.where(lax.axis_index(axis) == source, value, 0).astype(value.dtype)
    return lax.psum(kept, axis)


def normalize_layer(inputs):
    inputs = inputs.astype(jnp.float32)
    centered = inputs - jnp.mean(inputs, axis=-1, keepdims=True)
    variance = jnp.mean(centered * centered, axis=-1, keepdims=True)
    return centered * lax.rsqrt(variance + EPS)


def project_alignment(evoformer_block_fn, attention_input_weight, per_head_width):
    sequence_count, residue_length, alignment_channel_width = evoformer_block_fn.shape
    normalized_input = normalize_layer(evoformer_block_fn).astype(jnp.bfloat16)
    projected_rows = jnp.dot(
        normalized_input.reshape(sequence_count * residue_length, alignment_channel_width),
        attention_input_weight.reshape(alignment_channel_width, 4 * alignment_channel_width),
        preferred_element_type=jnp.float32,
    ).reshape(sequence_count, residue_length, 4, alignment_channel_width)
    query_rows = (projected_rows[:, :, 0] * per_head_width ** (-0.5)).astype(jnp.bfloat16)
    key_portion = projected_rows[:, :, 1].astype(jnp.bfloat16)
    value_portion = projected_rows[:, :, 2].astype(jnp.bfloat16)
    gate_activation = jax.nn.sigmoid(projected_rows[:, :, 3])
    return (query_rows, key_portion, value_portion, gate_activation)


def attend(
    query_rows,
    key_portion,
    value_portion,
    gate_activation,
    bias_block,
    key_penalty,
    number_of_heads,
):
    sequence_count, number_of_queries, alignment_channel_width = query_rows.shape
    key_count = key_portion.shape[1]
    per_head_width = alignment_channel_width // number_of_heads
    query_heads = query_rows.reshape(
        sequence_count, number_of_queries, number_of_heads, per_head_width
    )
    key_heads = key_portion.reshape(sequence_count, key_count, number_of_heads, per_head_width)
    value_heads = value_portion.reshape(sequence_count, key_count, number_of_heads, per_head_width)
    scores = jnp.einsum(
        "sihd,sjhd->shij", query_heads, key_heads, preferred_element_type=jnp.float32
    )
    scores = scores + bias_block.astype(jnp.float32)[None] + key_penalty[None, None, None, :]
    scores = scores - jnp.max(scores, axis=-1, keepdims=True)
    exponent = jnp.exp(scores)
    weights = (exponent / jnp.sum(exponent, axis=-1, keepdims=True)).astype(jnp.bfloat16)
    weighted_value_mix = jnp.einsum(
        "shij,sjhd->sihd", weights, value_heads, preferred_element_type=jnp.float32
    )
    return (
        weighted_value_mix.reshape(sequence_count, number_of_queries, alignment_channel_width)
        * gate_activation
    ).astype(jnp.bfloat16)


def body(
    alignment,
    pairwise,
    residue_mask,
    sequence_mask,
    attention_input_weight,
    attention_output_weight,
    bias_project,
    outer_factor_weight,
    outer_output,
    tri_project,
    tri_gate,
    tri_output,
):
    row_count = lax.axis_size("row")
    col_count = lax.axis_size("col")
    row_index = lax.axis_index("row")
    col_index = lax.axis_index("col")
    row_ratio = row_count // col_count
    sequence_local_part, device_local_rows, alignment_channel_width = alignment.shape
    columns = pairwise.shape[1]
    channels = pairwise.shape[2]
    number_of_heads = bias_project.shape[1]
    per_head_width = alignment_channel_width // number_of_heads
    outer_mean_width = outer_factor_weight.shape[2]
    hidden = tri_project.shape[2]
    res_live = residue_mask.astype(jnp.float32)
    seq_live = sequence_mask.astype(jnp.float32)
    row_live = lax.dynamic_slice_in_dim(res_live, row_index * device_local_rows, device_local_rows)
    col_live = lax.dynamic_slice_in_dim(res_live, col_index * columns, columns)
    seq_mine = lax.dynamic_slice_in_dim(
        seq_live, col_index * sequence_local_part, sequence_local_part
    )
    key_penalty = (res_live - 1.0) * BIG
    pair_normed = normalize_layer(pairwise).astype(jnp.bfloat16)
    bias_local = jnp.einsum(
        "ijc,ch->hij", pair_normed, bias_project, preferred_element_type=jnp.float32
    ).astype(jnp.bfloat16)
    bias_rows = lax.all_gather(bias_local, "col", axis=2, tiled=True)
    complete_sequences = lax.all_to_all(alignment, "row", split_axis=0, concat_axis=1, tiled=True)
    bias_every = lax.all_gather(bias_rows, "row", axis=1, tiled=True)
    query_rows, key_portion, value_portion, gate_activation = project_alignment(
        complete_sequences, attention_input_weight, per_head_width
    )

    def attend_one(operands):
        query_one, key_one, value_one, single_gate_value = operands
        return attend(
            query_one[None],
            key_one[None],
            value_one[None],
            single_gate_value[None],
            bias_every,
            key_penalty,
            number_of_heads,
        )[0]

    seq_results = lax.map(attend_one, (query_rows, key_portion, value_portion, gate_activation))
    attention_result_rows = lax.all_to_all(
        seq_results, "row", split_axis=1, concat_axis=0, tiled=True
    )
    alignment_flattened = attention_result_rows.reshape(
        sequence_local_part * device_local_rows, alignment_channel_width
    )
    alignment_output = (
        alignment.astype(jnp.float32)
        + jnp.dot(
            alignment_flattened, attention_output_weight, preferred_element_type=jnp.float32
        ).reshape(sequence_local_part, device_local_rows, alignment_channel_width)
    ).astype(jnp.bfloat16)
    alignment_second_copy = normalize_layer(alignment_output).astype(jnp.bfloat16)
    outer_factor_pair = jnp.dot(
        alignment_second_copy.reshape(
            sequence_local_part * device_local_rows, alignment_channel_width
        ),
        outer_factor_weight.reshape(alignment_channel_width, 2 * outer_mean_width),
        preferred_element_type=jnp.float32,
    ).reshape(sequence_local_part, device_local_rows, 2, outer_mean_width)
    live_here = (seq_mine[:, None] * row_live[None, :])[:, :, None]
    left_outer = (outer_factor_pair[:, :, 0] * live_here).astype(jnp.bfloat16)
    right_outer = (outer_factor_pair[:, :, 1] * live_here).astype(jnp.bfloat16)
    left_every, right_every = (
        lax.all_gather(left_outer, "col", axis=0, tiled=True),
        lax.all_gather(right_outer, "col", axis=0, tiled=True),
    )
    right_parts = [
        from_root(right_every, "row", col_index * row_ratio + offset) for offset in range(row_ratio)
    ]
    right_cols = jnp.concatenate(right_parts, axis=1)
    sequence_total_count = left_every.shape[0]
    outer_block = lax.dot_general(
        left_every.reshape(sequence_total_count, device_local_rows * outer_mean_width),
        right_cols.reshape(sequence_total_count, columns * outer_mean_width),
        (((0,), (0,)), ((), ())),
        preferred_element_type=jnp.float32,
    )
    outer_block = outer_block.astype(jnp.bfloat16).reshape(
        device_local_rows, outer_mean_width, columns, outer_mean_width
    )
    opm_update = jnp.einsum(
        "iajb,abz->ijz",
        outer_block,
        outer_output.reshape(outer_mean_width, outer_mean_width, channels),
        preferred_element_type=jnp.float32,
    )
    counts = jnp.sum(seq_live) * row_live[:, None] * col_live[None, :]
    opm_update = opm_update / jnp.maximum(counts, 1.0)[:, :, None]
    pair_mid = (pairwise.astype(jnp.float32) + opm_update).astype(jnp.bfloat16)
    tri_normed = normalize_layer(pair_mid).astype(jnp.bfloat16)
    flat_normed = tri_normed.reshape(device_local_rows * columns, channels)
    pair_plane = row_live[:, None] * col_live[None, :]
    tri_terms = jnp.dot(
        flat_normed, tri_project.reshape(channels, 4 * hidden), preferred_element_type=jnp.float32
    ).reshape(device_local_rows, columns, 4, hidden)
    pair_live = pair_plane[:, :, None]
    left_tri = (jax.nn.sigmoid(tri_terms[:, :, 0]) * tri_terms[:, :, 1] * pair_live).astype(
        jnp.bfloat16
    )
    right_tri = (jax.nn.sigmoid(tri_terms[:, :, 2]) * tri_terms[:, :, 3] * pair_live).astype(
        jnp.bfloat16
    )
    right_tall = lax.all_gather(right_tri, "row", axis=0, tiled=True)
    right_mine = lax.all_to_all(right_tall, "col", split_axis=0, concat_axis=1, tiled=True)
    combined = jnp.einsum(
        "ikc,jkc->ijc",
        lax.all_gather(left_tri, "col", axis=1, tiled=True),
        right_mine,
        preferred_element_type=jnp.float32,
    )
    tri_result = normalize_layer(combined).astype(jnp.bfloat16)
    update_tri = jnp.dot(
        tri_result.reshape(device_local_rows * columns, hidden),
        tri_output,
        preferred_element_type=jnp.float32,
    ).reshape(device_local_rows, columns, channels)
    gate_out = jax.nn.sigmoid(
        jnp.dot(flat_normed, tri_gate, preferred_element_type=jnp.float32)
    ).reshape(device_local_rows, columns, channels)
    pair_output_state = (pair_mid.astype(jnp.float32) + gate_out * update_tri).astype(jnp.bfloat16)
    return (alignment_output, pair_output_state)


def solution(mesh):
    placed = (
        P("col", "row", None),
        P("row", "col", None),
        P(),
        P(),
        P(),
        P(),
        P(),
        P(),
        P(),
        P(),
        P(),
        P(),
    )
    return jax.shard_map(
        body,
        mesh=mesh,
        in_specs=placed,
        out_specs=(P("col", "row", None), P("row", "col", None)),
        check_vma=False,
    )
```

profile of v0, /device:TPU:1, one launch (start us, length us, event | category | flops | bytes accessed | tf_op | source)
XLA Modules:
  0.0 929.5 jit_solution(182526649603953731)
XLA Ops:
  7.2 1.4 convert_reduce_fusion.2
  8.7 1.7 fusion.46
  10.4 1.8 fusion.43
  12.3 33.4 %all_gather.18 = bf16[8,32,512]{1,0,2:T(8,128)(2,1)S(1)} all-gather(bf16[8,32,64]{1,0,2:T(8,128)(2,1)S(1)} %copy.85), channel_id=1, replica_groups=mesh['row'=16,'col'=8] {'col'}, dimensions={2}, use_global_device_ids=true | all-gather | bytes 294912 | tf_op jit(solution)/shard_map/all_gather | solution.py:108
  45.7 1.7 copy.86
  47.4 10.9 %all-to-all-start = ((bf16[80,32,256]{2,1,0:T(8,128)(2,1)}), bf16[80,32,256]{2,1,0:T(8,128)(2,1)S(1)}, u32[]{:S(2)}, u32[]{:S(2)}) async-start(bf16[80,32,256]{2,1,0:T(8,128)(2,1)} %param.14), calls=%async_computation | async-start | bytes 2621440 | tf_op jit(solution)/shard_map/all_to_all | solution.py:109
  58.6 24.0 %all-to-all-done = bf16[80,32,256]{2,1,0:T(8,128)(2,1)S(1)} async-done(((bf16[80,32,256]{2,1,0:T(8,128)(2,1)}), bf16[80,32,256]{2,1,0:T(8,128)(2,1)S(1)}, u32[]{:S(2)}, u32[]{:S(2)}) %all-to-all-start) | async-done | bytes 1310752 | tf_op jit(solution)/shard_map/all_to_all | solution.py:109
  83.8 0.8 fusion.22
  84.8 1.6 fusion.75
  86.4 1.2 slice_bitcast_fusion.2
  87.6 2.6 fusion.15
  90.3 10.9 %all-gather.6.cloned.1.call-done = bf16[8,512,512]{2,0,1:T(8,128)(2,1)} async-done(((bf16[8,32,512]{2,0,1:T(8,128)(2,1)}), bf16[8,512,512]{2,0,1:T(8,128)(2,1)}) %all-gather.6.cloned.1.call-update) | async-done | bytes 4194320 | tf_op jit(solution)/shard_map/all_gather | solution.py:110
  101.1 7.6 copy.90
  108.7 71.6 %while.10 = (s32[]{:T(128)}, bf16[5,512,256]{1,2,0:T(8,128)(2,1)}, bf16[5,512,256]{2,1,0:T(8,128)(2,1)S(1)}, bf16[5,512,256]{2,1,0:T(8,128)(2,1)}, bf16[5,512,25...) while((s32[]{:T(128)}, bf16[5,512,256]{1,2,0:T(8,128)(2,1)}, ...), condition=%wide.region_7.8_spmd, body=%wide.region_4.7_spmd.sunk | while | flops 425989120 | bytes 16814696 | solution.py:127
  108.7 1.1 constant_dynamic-slice_fusion.9
  110.1 4.8 fusion.105
  115.1 5.8 fusion.106
  120.9 1.1 constant_dynamic-slice_fusion.7
  122.2 0.8 constant_dynamic-update-slice_fusion.2
  123.0 1.1 constant_dynamic-slice_fusion.9
  124.4 4.8 fusion.105
  129.4 5.8 fusion.106
  135.2 1.1 constant_dynamic-slice_fusion.7
  137.3 1.1 constant_dynamic-slice_fusion.9
  138.7 4.8 fusion.105
  143.7 5.8 fusion.106
  149.5 1.1 constant_dynamic-slice_fusion.7
  150.8 0.8 constant_dynamic-update-slice_fusion.2
  151.6 1.1 constant_dynamic-slice_fusion.9
  153.0 4.8 fusion.105
  158.0 5.8 fusion.106
  163.9 1.1 constant_dynamic-slice_fusion.7
  165.2 0.8 constant_dynamic-update-slice_fusion.2
  166.0 1.1 constant_dynamic-slice_fusion.9
  167.3 4.8 fusion.105
  172.3 5.8 fusion.106
  178.2 1.1 constant_dynamic-slice_fusion.7
  179.5 0.8 constant_dynamic-update-slice_fusion.2
  180.3 4.3 copy.92
  184.6 4.3 all-to-all-start.1
  190.7 25.2 %all-to-all-done.1 = bf16[5,512,256]{2,0,1:T(8,128)(2,1)S(1)} async-done(((bf16[5,512,256]{2,0,1:T(8,128)(2,1)}), bf16[5,512,256]{2,0,1:T(8,128)(2,1)S(1)}, u32[]{:S(2)}, u32[]{:S(2)}) %all-to-all-start.1) | async-done | bytes 1310752 | tf_op jit(solution)/shard_map/all_to_all | solution.py:128
  216.3 1.9 convert_reduce_fusion
  219.1 0.9 fusion.28
  220.0 1.5 fusion.31
  222.3 80.2 %all-gather.10.cloned.1.call-done = bf16[640,32,32]{2,1,0:T(8,128)(2,1)} async-done(((bf16[80,32,32]{2,1,0:T(8,128)(2,1)}), bf16[640,32,32]{2,1,0:T(8,128)(2,1)}) %all-gather.10.cloned.1.call-update) | async-done | bytes 1310736 | tf_op jit(solution)/shard_map/all_gather | solution.py:153
  302.4 7.1 broadcast_select_fusion.1
  310.7 72.2 %all-gather.8.cloned.1.call-done = bf16[640,32,32]{2,1,0:T(8,128)(2,1)} async-done(((bf16[80,32,32]{2,1,0:T(8,128)(2,1)}), bf16[640,32,32]{2,1,0:T(8,128)(2,1)}) %all-gather.8.cloned.1.call-update) | async-done | bytes 1310736 | tf_op jit(solution)/shard_map/all_gather | solution.py:152
  382.8 7.5 copy.96
  390.4 229.7 %all-reduce.3.cloned.1.call-done = (bf16[640,32,32]{2,1,0:T(8,128)(2,1)}, bf16[640,32,32]{2,1,0:T(8,128)(2,1)}) async-done(((bf16[640,32,32]{2,1,0:T(8,128)(2,1)}, bf16[640,32,32]{2,1,0:T(8,128)(2,1)}), (bf16[640,32,32]{2,1,0:T(8,128)(2,1)}, bf16[640,32,32]{2,1,0:T(8,128)(2,1)})) %all-reduce.3.cloned.1.call-update) | async-done | bytes 2621456 | tf_op jit(solution)/shard_map/psum | solution.py:12
  620.1 6.7 copy.97
  626.8 6.7 copy.98
  633.8 1.0 copy-done.3
  634.8 5.0 convolution_convert_fusion
  639.8 19.5 %reshape.302 = bf16[32,32,64,32]{3,2,1,0:T(8,128)(2,1)} reshape(bf16[1024,2048]{1,0:T(8,128)(2,1)} %convolution_convert_fusion) | data formatting | bytes 8388608 | tf_op jit(solution)/shard_map/reshape | solution.py:166
  659.4 9.5 %convert_reduce_fusion.1 = (f32[32,64]{1,0:T(8,128)S(1)}, bf16[32,64,128]{2,1,0:T(8,128)(2,1)S(1)}) fusion(f32[32,64]{1,0:T(8,128)S(1)} %get-tuple-element.110, bf16[32,32,64,32]{3,2,1,0:T(8,128)(2,1)} %reshape.302, bf16[32,32,128,1]{2,1,0,3:T(8,128)(2,1)S(1)} %bitcast.219, bf16[32,64,128]{2,1,0:T(8,128)(2,1)S(1)} %copy-done.2), kind=kOutput, calls=%fused_computation.51 | convolution fusion | flops 538441728 | bytes 5521408 | tf_op jit(solution)/shard_map/iajb,abz->ijz/dot_general | solution.py:169
  670.8 1.6 fusion.50
  673.1 53.4 %all-gather.12.cloned.1.call-done = bf16[512,64,128]{2,1,0:T(8,128)(2,1)} async-done(((bf16[32,64,128]{2,1,0:T(8,128)(2,1)}), bf16[512,64,128]{2,1,0:T(8,128)(2,1)}) %all-gather.12.cloned.1.call-update) | async-done | bytes 8388624 | tf_op jit(solution)/shard_map/all_gather | solution.py:191
  726.4 6.7 all-to-all-start.2
  733.6 149.4 %all-gather.14.cloned.1.call-done = bf16[32,512,128]{2,1,0:T(8,128)(2,1)} async-done(((bf16[32,64,128]{2,1,0:T(8,128)(2,1)}), bf16[32,512,128]{2,1,0:T(8,128)(2,1)}) %all-gather.14.cloned.1.call-update) | async-done | bytes 4194320 | tf_op jit(solution)/shard_map/all_gather | solution.py:195
  883.0 8.0 copy.107
  891.0 9.6 %copy.103 = bf16[64,8,64,128]{3,2,1,0:T(8,128)(2,1)} copy(bf16[64,8,64,128]{3,2,0,1:T(8,128)(2,1)} %bitcast.49) | data formatting | bytes 16777216 | tf_op jit(solution)/shard_map/all_to_all | solution.py:192
  900.6 12.6 %copy.106 = bf16[64,512,128]{1,0,2:T(8,128)(2,1)} copy(bf16[64,512,128]{2,1,0:T(8,128)(2,1)} %bitcast.220) | data formatting | bytes 16777216 | tf_op jit(solution)/shard_map/all_to_all | solution.py:192
  913.2 6.9 bitcast_reduce_fusion
  920.9 1.3 fusion.36
  (99 shorter events, 14.8 us)
Async XLA Ops:
  7.2 652.2 %copy-start = (bf16[1024,128]{1,0:T(8,128)(2,1)S(1)}, bf16[1024,128]{1,0:T(8,128)(2,1)}, u32[]{:S(2)}) copy-start(bf16[1024,128]{1,0:T(8,128)(2,1)} %param.22) | copy-start | bytes 786436
  7.2 93.9 %all-gather.6.cloned.1.call-start = ((), (), s32[]{:S(2)}) async-start(), calls=%async_computation.3 | async-start | bytes 4456448 | tf_op jit(solution)/shard_map/all_gather | solution.py:110
  12.3 46.0 %copy-start.4 = (bf16[256,4,256]{2,1,0:T(4,128)(2,1)S(1)}, bf16[256,4,256]{2,1,0:T(4,128)(2,1)}, u32[]{:S(2)}) copy-start(bf16[256,4,256]{2,1,0:T(4,128)(2,1)} %param.18) | copy-start | bytes 1572868
  47.4 11.2 %copy-start.10 = (s32[512]{0:T(512)S(1)}, s32[512]{0:T(512)}, u32[]{:S(2)}) copy-start(s32[512]{0:T(512)} %param.16) | copy-start | bytes 6148
  47.4 35.2 %all-to-all-start = ((bf16[80,32,256]{2,1,0:T(8,128)(2,1)}), bf16[80,32,256]{2,1,0:T(8,128)(2,1)S(1)}, u32[]{:S(2)}, u32[]{:S(2)}) async-start(bf16[80,32,256]{2,1,0:T(8,128)(2,1)} %param.14), calls=%async_computation | async-start | bytes 2621440 | tf_op jit(solution)/shard_map/all_to_all | solution.py:109
  184.6 4.6 copy-start.9
  184.6 31.3 %all-to-all-start.1 = ((bf16[5,512,256]{2,0,1:T(8,128)(2,1)}), bf16[5,512,256]{2,0,1:T(8,128)(2,1)S(1)}, u32[]{:S(2)}, u32[]{:S(2)}) async-start(bf16[5,512,256]{2,0,1:T(8,128)(2,1)} %copy.92), calls=%async_computation.1 | async-start | bytes 4194304 | tf_op jit(solution)/shard_map/all_to_all | solution.py:128
  188.9 27.3 %copy-start.5 = (bf16[256,256]{1,0:T(8,128)(2,1)S(1)}, bf16[256,256]{1,0:T(8,128)(2,1)}, u32[]{:S(2)}) copy-start(bf16[256,256]{1,0:T(8,128)(2,1)} %param.19) | copy-start | bytes 393220
  189.0 113.5 %all-gather.10.cloned.1.call-start = ((), (), s32[]{:S(2)}) async-start(), calls=%async_computation.5 | async-start | bytes 5898240 | tf_op jit(solution)/shard_map/all_gather | solution.py:153
  216.3 2.8 copy-start.7
  218.2 1.7 copy-start.1
  221.5 161.4 %all-gather.8.cloned.1.call-start = ((), (), s32[]{:S(2)}) async-start(), calls=%async_computation.4 | async-start | bytes 5898240 | tf_op jit(solution)/shard_map/all_gather | solution.py:152
  222.2 397.9 %all-reduce.3.cloned.1.call-start = ((), (), s32[]{:S(2)}) async-start(), calls=%async_computation.8 | async-start | bytes 20971520 | tf_op jit(solution)/shard_map/psum | solution.py:12
  309.5 0.9 copy-start.6
  309.6 416.9 %all-gather.12.cloned.1.call-start = ((), (), s32[]{:S(2)}) async-start(), calls=%async_computation.6 | async-start | bytes 8912896 | tf_op jit(solution)/shard_map/all_gather | solution.py:191
  633.5 1.3 copy-start.3
  639.8 19.5 %copy-start.2 = (bf16[32,64,128]{2,1,0:T(8,128)(2,1)S(1)}, bf16[32,64,128]{2,1,0:T(8,128)(2,1)}, u32[]{:S(2)}) copy-start(bf16[32,64,128]{2,1,0:T(8,128)(2,1)} %param.15) | copy-start | bytes 1572868
  672.5 210.5 %all-gather.14.cloned.1.call-start = ((), (), s32[]{:S(2)}) async-start(), calls=%async_computation.7 | async-start | bytes 4718592 | tf_op jit(solution)/shard_map/all_gather | solution.py:195
  673.1 60.1 %copy-start.11 = (bf16[128,128]{1,0:T(8,128)(2,1)S(1)}, bf16[128,128]{1,0:T(8,128)(2,1)}, u32[]{:S(2)}) copy-start(bf16[128,128]{1,0:T(8,128)(2,1)} %param.24) | copy-start | bytes 98308
  726.4 164.6 %all-to-all-start.2 = ((bf16[512,64,128]{2,1,0:T(8,128)(2,1)}), bf16[512,64,128]{2,1,0:T(8,128)(2,1)}, u32[]{:S(2)}, u32[]{:S(2)}) async-start(bf16[512,64,128]{2,1,0:T(8,128)(2,1)} %all-gather.12.cloned.1.call-done), calls=%async_computation.2 | async-start | bytes 16777216 | tf_op jit(solution)/shard_map/all_to_all | solution.py:192
  920.1 0.8 copy-start.8
Sparse Core Ops, SparseCore 0:
  47.5 53.5 all-gather.5
  221.6 80.7 all-gather.9
  304.8 78.0 all-gather.7
  385.3 234.7 all-reduce.2
  672.6 53.7 all-gather.11
  729.2 153.7 all-gather.13
where the time goes:
time: 935 us; the launch traced here: 930 us
  waiting for transfers between devices  646 us (69%)
  local copies, waits for them, and re-layouts  103 us (11%)
  matrix products  83.3 us (9%)
  blocking collectives  33.4 us (4%)
  other arithmetic  26.5 us (3%)
  starting transfers between devices  22.4 us (2%)
  between operations  15 us (2%)
    psum x1, waiting for transfers between devices, from_root(): return lax.psum(kept, axis)  230 us
    all_gather x1, waiting for transfers between devices, body(): lax.all_gather(left_tri, 'col', axis=1, tiled=True)  149 us
    all_gather x1, waiting for transfers between devices, body(): lax.all_gather(right_outer, 'col', axis=0, tiled=True)  80.2 us
    all_gather x1, waiting for transfers between devices, body(): lax.all_gather(left_outer, 'col', axis=0, tiled=True)  72.2 us
    all_gather x1, waiting for transfers between devices, body(): right_tall = lax.all_gather(right_tri, 'row', axis=0, tiled=True)  53.4 us
    all_gather x1, blocking collectives, body(): bias_rows = lax.all_gather(bias_local, 'col', axis=2, tiled=True)  33.4 us
    dot_general x5, matrix products, attend(): jnp.einsum('shij,sjhd->sihd', weights, value_heads, preferred_element_typ...  29.2 us
    all_to_all x1, waiting for transfers between devices, body(): lax.all_to_all(seq_results, 'row', split_axis=1, concat_axis=0, tiled=True)  25.2 us
  transfers between devices with their start and end apart: 9, of which 8 were waited for; matrix products, arithmetic and copies ran while one was open for 4% of the time, Pallas kernels for 0%

commit v1 on v0

v1 whole, which is shorter than its diff:
```python
import jax
import jax.numpy as jnp
from jax import lax
from jax.experimental import pallas as pl
from jax.experimental.pallas import tpu as pltpu
from jax.sharding import Mesh, PartitionSpec as P

EPS = 1e-05
BIG = 1000000000.0
F32 = jnp.float32
BF16 = jnp.bfloat16
ROW = ("x", "zl", "core")
COL = ("zh", "y")
ALL = ROW + COL
CHIP = ("x", "zl", "zh", "y")
NT = (((1,), (1,)), ((), ()))
TN = (((0,), (0,)), ((), ()))
MB = 1 << 20


def layer_norm(v):
    v = v.astype(F32)
    centered = v - jnp.mean(v, axis=-1, keepdims=True)
    variance = jnp.mean(centered * centered, axis=-1, keepdims=True)
    return centered * lax.rsqrt(variance + EPS)


def low_lanes(shape):
    return lax.broadcasted_iota(jnp.int32, shape, len(shape) - 1) < 64


def mix(first, second):
    keep = low_lanes(first.shape)
    turn = len(first.shape) - 1
    return (
        jnp.where(keep, first, pltpu.roll(second, 64, turn)),
        jnp.where(keep, pltpu.roll(first, 64, turn), second),
    )


def params(mib):
    return pltpu.CompilerParams(vmem_limit_bytes=mib * MB)


def bias_kernel(pair_ref, weight_ref, out_ref):
    heads = weight_ref.shape[0]
    for u in range(16):
        block = jnp.concatenate([pair_ref[u], pair_ref[16 + u]], axis=0)
        normed = layer_norm(block).astype(BF16)
        out_ref[:, u, :] = lax.dot_general(
            weight_ref[...], normed, NT, preferred_element_type=F32
        ).astype(out_ref.dtype)


def pair_bias(pairwise, weight):
    heads = weight.shape[0]
    return pl.pallas_call(
        bias_kernel,
        out_shape=jax.ShapeDtypeStruct((heads, 16, 128), F32),
        compiler_params=params(16),
        name="pair_bias",
    )(pairwise, weight)


def attention_kernel(
    core_ref,
    seq_ref,
    own_ref,
    other_ref,
    x_ref,
    win_ref,
    wo_ref,
    wl_ref,
    wr_ref,
    live_ref,
    live_col_ref,
    out_ref,
    left_ref,
    right_ref,
    bias_ref,
    q_ref,
    k_ref,
    v_ref,
    acc_ref,
):
    heads = bias_ref.shape[0]
    step = pl.program_id(0)

    @pl.when(step == 0)
    def _():
        penalty = (live_ref[...] - 1.0) * BIG

        def assemble(xz, carry):
            for ref, core in ((own_ref, core_ref[0]), (other_ref, 1 - core_ref[0])):
                base = pl.multiple_of((xz * 2 + core) * 32, 32)
                for h in range(heads):
                    for m in range(4):
                        even = ref[xz * 8 + 2 * m, 16 * h : 16 * h + 16, :].astype(F32)
                        odd = ref[xz * 8 + 2 * m + 1, 16 * h : 16 * h + 16, :].astype(F32)
                        low, high = mix(even, odd)
                        pen = penalty[:, 128 * m : 128 * m + 128]
                        bias_ref[h, pl.ds(base, 16), 128 * m : 128 * m + 128] = low + pen
                        bias_ref[h, pl.ds(base + 16, 16), 128 * m : 128 * m + 128] = high + pen
            return carry

        lax.fori_loop(0, 8, assemble, 0)

    x = x_ref[:, 0].reshape(512, 256)
    normed = layer_norm(x).astype(BF16)

    def project(t):
        return jnp.dot(normed, win_ref[:, 256 * t : 256 * t + 256], preferred_element_type=F32)

    q_ref[...] = (project(0) * 32 ** (-0.5)).astype(BF16)
    k_ref[...] = project(1).astype(BF16)
    v_ref[...] = project(2).astype(BF16)
    acc_ref[...] = jnp.zeros_like(acc_ref)
    lane_head = lax.broadcasted_iota(jnp.int32, (512, 256), 1) // 32

    def head(h, carry):
        mine = lane_head == h
        k_h = jnp.where(mine, k_ref[...], jnp.zeros((), BF16))
        v_h = jnp.where(mine, v_ref[...], jnp.zeros((), BF16))
        for t in range(2):
            rows = slice(256 * t, 256 * t + 256)
            s = lax.dot_general(q_ref[rows], k_h, NT, preferred_element_type=F32)
            s = s + bias_ref[h, rows, :]
            p = jnp.exp(s - jnp.max(s, axis=-1, keepdims=True))
            total = jnp.sum(p, axis=-1, keepdims=True)
            o = jnp.dot(p.astype(BF16), v_h, preferred_element_type=F32)
            acc_ref[rows] += o * (1.0 / total)
        return carry

    lax.fori_loop(0, heads, head, 0)
    gate = jax.nn.sigmoid(project(3))
    attended = (acc_ref[...] * gate).astype(BF16)
    out = (
        x.astype(F32) + jnp.dot(attended, wo_ref[...], preferred_element_type=F32)
    ).astype(BF16)
    out_ref[:, 0] = out.reshape(16, 32, 256)
    second = layer_norm(out).astype(BF16)
    seq_live = seq_ref[step]
    left = jnp.dot(second, wl_ref[...], preferred_element_type=F32)
    left = (left * (live_col_ref[...] * seq_live)).reshape(16, 4, 8, 128)
    group = lax.broadcasted_iota(jnp.int32, (16, 8, 128), 2) // 32
    packed = left[:, 0]
    for q in range(1, 4):
        packed = jnp.where(group == q, left[:, q], packed)
    left_ref[:, 0] = packed.astype(BF16)
    right = lax.dot_general(wr_ref[...], second, NT, preferred_element_type=F32)
    right = right * (live_ref[...] * seq_live)
    for m in range(4):
        tile = right[:, 128 * m : 128 * m + 128]
        even, odd = mix(tile[:16], tile[16:])
        right_ref[2 * m, 0] = even.astype(BF16)
        right_ref[2 * m + 1, 0] = odd.astype(BF16)


def attention(core, seq_live, own, other, x, win, wo, wl, wr, live, live_col):
    count = x.shape[1]
    smem = pl.BlockSpec(memory_space=pltpu.SMEM)

    def whole(a):
        return pl.BlockSpec(a.shape, lambda s: (0,) * a.ndim)

    def per_seq(*dims):
        return pl.BlockSpec(dims, lambda s: (0, s) + (0,) * (len(dims) - 2))

    return pl.pallas_call(
        attention_kernel,
        grid=(count,),
        in_specs=[
            smem,
            smem,
            whole(own),
            whole(other),
            per_seq(16, 1, 32, 256),
            whole(win),
            whole(wo),
            whole(wl),
            whole(wr),
            whole(live),
            whole(live_col),
        ],
        out_specs=[
            per_seq(16, 1, 32, 256),
            per_seq(16, 1, 8, 128),
            per_seq(8, 1, 16, 128),
        ],
        out_shape=[
            jax.ShapeDtypeStruct(x.shape, BF16),
            jax.ShapeDtypeStruct((16, count, 8, 128), BF16),
            jax.ShapeDtypeStruct((8, count, 16, 128), BF16),
        ],
        scratch_shapes=[
            pltpu.VMEM((8, 512, 512), F32),
            pltpu.VMEM((512, 256), BF16),
            pltpu.VMEM((512, 256), BF16),
            pltpu.VMEM((512, 256), BF16),
            pltpu.VMEM((512, 256), F32),
        ],
        compiler_params=params(48),
        name="row_attention",
    )(core, seq_live, own, other, x, win, wo, wl, wr, live, live_col)


def outer_kernel(l_ref, r_ref, w_ref, inv_ref, plane_ref, pair_ref, wp_ref, mid_ref, tri_ref, x_ref):
    product = lax.dot_general(l_ref[...], r_ref[...], TN, preferred_element_type=F32)
    for half in range(2):
        for u in range(16):
            first = product[32 * half : 32 * half + 32, 128 * u : 128 * u + 128]
            second = product[32 * half + 64 : 32 * half + 96, 128 * u : 128 * u + 128]
            low, high = mix(first, second)
            columns = slice(128 * half, 128 * half + 128)
            x_ref[64 * u : 64 * u + 32, columns] = low.astype(BF16)
            x_ref[64 * u + 32 : 64 * u + 64, columns] = high.astype(BF16)
    update = jnp.dot(w_ref[...], x_ref[...], preferred_element_type=F32)
    for half in range(2):
        part = update[:, 128 * half : 128 * half + 128] * inv_ref[half, 0]
        before = jnp.concatenate([pair_ref[half, 0], pair_ref[half + 2, 0]], axis=0)
        mid = (before.astype(F32) + part.T).astype(BF16)
        mid_ref[half, 0] = mid[:64]
        mid_ref[half + 2, 0] = mid[64:]
        normed = layer_norm(mid).astype(BF16)
        terms = lax.dot_general(wp_ref[...], normed, NT, preferred_element_type=F32)
        plane = plane_ref[half, 0]
        tri_ref[half, 0, :128] = (jax.nn.sigmoid(terms[:128]) * terms[128:256] * plane).astype(BF16)
        tri_ref[half, 0, 128:] = (jax.nn.sigmoid(terms[256:384]) * terms[384:] * plane).astype(BF16)


def outer_update(left, right, weight, inv, plane, pairwise, wp):
    total = left.shape[0]

    def whole(a):
        return pl.BlockSpec(a.shape, lambda v: (0,) * a.ndim)

    def by_v(*dims):
        return pl.BlockSpec(dims, lambda v: (0, v) + (0,) * (len(dims) - 2))

    return pl.pallas_call(
        outer_kernel,
        grid=(8,),
        in_specs=[
            by_v(total, 128),
            whole(right),
            whole(weight),
            by_v(2, 1, 1, 128),
            by_v(2, 1, 1, 128),
            by_v(4, 1, 64, 128),
            whole(wp),
        ],
        out_specs=[by_v(4, 1, 64, 128), by_v(2, 1, 256, 128)],
        out_shape=[
            jax.ShapeDtypeStruct((4, 8, 64, 128), BF16),
            jax.ShapeDtypeStruct((2, 8, 256, 128), BF16),
        ],
        scratch_shapes=[pltpu.VMEM((1024, 256), BF16)],
        compiler_params=params(32),
        name="outer_update",
    )(left, right, weight, inv, plane, pairwise, wp)


def triangle_kernel(in_ref, out_ref, a_ref, b_ref):
    def assemble(r, carry):
        base = pl.multiple_of(r * 32, 32)
        for t, ref in ((0, a_ref), (1, b_ref)):
            for m in range(4):
                low, high = mix(
                    in_ref[r * 8 + 2 * m, t].astype(F32), in_ref[r * 8 + 2 * m + 1, t].astype(F32)
                )
                ref[pl.ds(base, 16), 128 * m : 128 * m + 128] = low.astype(BF16)
                ref[pl.ds(base + 16, 16), 128 * m : 128 * m + 128] = high.astype(BF16)
        return carry

    lax.fori_loop(0, 16, assemble, 0)

    def multiply(g, carry):
        base = pl.multiple_of(g * 128, 128)
        c = lax.dot_general(a_ref[pl.ds(base, 128), :], b_ref[...], NT, preferred_element_type=F32)
        for part in range(4):
            for m in range(4):
                columns = slice(128 * m, 128 * m + 128)
                even, odd = mix(
                    c[32 * part : 32 * part + 16, columns], c[32 * part + 16 : 32 * part + 32, columns]
                )
                out_ref[(g * 4 + part) * 8 + 2 * m] = even.astype(BF16)
                out_ref[(g * 4 + part) * 8 + 2 * m + 1] = odd.astype(BF16)
        return carry

    lax.fori_loop(0, 4, multiply, 0)


def triangle(blocks):
    return pl.pallas_call(
        triangle_kernel,
        out_shape=jax.ShapeDtypeStruct((128, 16, 128), BF16),
        scratch_shapes=[pltpu.VMEM((512, 512), BF16), pltpu.VMEM((512, 512), BF16)],
        compiler_params=params(16),
        name="triangle",
    )(blocks)


def final_kernel(tri_ref, mid_ref, wt_ref, wg_ref, out_ref):
    for u in range(16):
        combined = tri_ref[u].astype(F32)
        centered = combined - jnp.mean(combined, axis=0, keepdims=True)
        variance = jnp.mean(centered * centered, axis=0, keepdims=True)
        normed = (centered * lax.rsqrt(variance + EPS)).astype(BF16)
        update = jnp.dot(wt_ref[...], normed, preferred_element_type=F32)
        mid = jnp.concatenate([mid_ref[u], mid_ref[16 + u]], axis=0)
        gate = jax.nn.sigmoid(
            jnp.dot(layer_norm(mid).astype(BF16), wg_ref[...], preferred_element_type=F32)
        )
        out = (mid.astype(F32) + gate * update.T).astype(BF16)
        out_ref[u] = out[:64]
        out_ref[16 + u] = out[64:]


def final(tri, mid, wt, wg):
    return pl.pallas_call(
        final_kernel,
        out_shape=jax.ShapeDtypeStruct((32, 64, 128), BF16),
        compiler_params=params(16),
        name="pair_final",
    )(tri, mid, wt, wg)


def body(
    alignment,
    pairwise,
    residue_mask,
    sequence_mask,
    attention_input_weight,
    attention_output_weight,
    bias_project,
    outer_factor_weight,
    outer_output,
    tri_project,
    tri_gate,
    tri_output,
):
    row = lax.axis_index(ROW)
    col = lax.axis_index(COL)
    core = lax.axis_index("core")
    swap = [(0, 1), (1, 0)]
    res_live = residue_mask.astype(F32)
    seq_live = sequence_mask.astype(F32)
    row_live = lax.dynamic_slice_in_dim(res_live, row * 32, 32)
    col_live = lax.dynamic_slice_in_dim(res_live, col * 64, 64)
    my_seqs = lax.dynamic_slice_in_dim(seq_live, col * 80 + row * 5, 5)

    bias = pair_bias(pairwise, bias_project.T).astype(BF16).reshape(128, 128)
    bias_own = lax.all_to_all(
        jnp.broadcast_to(bias, (64, 128, 128)), CHIP, split_axis=0, concat_axis=0, tiled=True
    )
    sequences = lax.all_to_all(
        alignment.reshape(16, 5, 32, 256), ROW, split_axis=0, concat_axis=0, tiled=True
    )
    bias_other = lax.ppermute(bias_own, "core", swap)
    out_seq, left, right = attention(
        core.reshape(1),
        my_seqs,
        bias_own,
        bias_other,
        sequences,
        attention_input_weight.reshape(256, 1024),
        attention_output_weight,
        jnp.tile(outer_factor_weight[:, 0], (1, 4)),
        outer_factor_weight[:, 1].T,
        res_live.reshape(1, 512),
        jnp.broadcast_to(res_live[:, None], (512, 128)),
    )
    right_own = lax.all_to_all(
        jnp.broadcast_to(right[None], (8, 8, 5, 16, 128)).reshape(64, 80, 128),
        CHIP,
        split_axis=0,
        concat_axis=0,
        tiled=True,
    )
    left_all = lax.all_to_all(
        jnp.broadcast_to(left[:, None], (16, 8, 5, 8, 128)).reshape(128, 40, 128),
        ALL,
        split_axis=0,
        concat_axis=0,
        tiled=True,
    )
    right_other = lax.ppermute(right_own, "core", swap)
    left_all = left_all.reshape(8, 2, 320 // 8, 1024)
    left_own = lax.dynamic_index_in_dim(left_all, core, 1, keepdims=False)
    left_other = lax.dynamic_index_in_dim(left_all, 1 - core, 1, keepdims=False)
    left_cat = jnp.concatenate([left_own, left_other], axis=0).reshape(640, 1024)
    right_cat = jnp.concatenate([right_own, right_other], axis=0).reshape(640, 2048)
    alignment_output = lax.all_to_all(
        out_seq, ROW, split_axis=0, concat_axis=0, tiled=True
    ).reshape(80, 32, 256)

    plane = row_live[:, None] * col_live[None, :]
    inv = 1.0 / jnp.maximum(jnp.sum(seq_live) * plane, 1.0)

    def pairs(a):
        return a.reshape(2, 16, 64).transpose(1, 0, 2).reshape(2, 8, 1, 128)

    weight = outer_output.reshape(32, 2, 16, 128).transpose(3, 2, 1, 0).reshape(128, 1024)
    mid, tri = outer_update(
        left_cat,
        right_cat,
        weight,
        pairs(inv),
        pairs(plane),
        pairwise.reshape(4, 8, 64, 128),
        tri_project.reshape(128, 512).T,
    )
    tri = tri.reshape(16, 2, 128, 128).transpose(2, 1, 0, 3)
    blocks = lax.all_to_all(tri, ALL, split_axis=0, concat_axis=0, tiled=True)
    combined = lax.all_to_all(triangle(blocks), ALL, split_axis=0, concat_axis=0, tiled=True)
    pair_output_state = final(
        combined.transpose(1, 0, 2), mid.reshape(32, 64, 128), tri_output.T, tri_gate
    )
    return (alignment_output, pair_output_state)


def solution(mesh):
    fine = Mesh(mesh.devices.reshape(4, 2, 2, 2, 4), ALL)
    placed = (P(COL, ROW, None), P(ROW, COL, None)) + (P(),) * 10
    return jax.shard_map(
        body,
        mesh=fine,
        in_specs=placed,
        out_specs=(P(COL, ROW, None), P(ROW, COL, None)),
        check_vma=False,
    )
```

time: 935 us -> 262 us (0.28)
  waiting for transfers between devices: 646 us -> 61.9 us
  matrix products: 83.3 us -> 0 us
  local copies, waits for them, and re-layouts: 103 us -> 20.3 us
  Pallas kernels: 0 us -> 61.4 us
  blocking collectives: 33.4 us -> 88.8 us
  other arithmetic: 26.5 us -> 5.54 us
  between operations: 15 us -> 0.92 us
    all_gather x5 -> x0, waiting for transfers between devices: 366 us -> none  [the longest x1 149 us: body(): lax.all_gather(left_tri, 'col', axis=1, tiled=True)]
    psum x1 -> x0, waiting for transfers between devices: 230 us -> none  [from_root(): return lax.psum(kept, axis)]
    all_to_all x0 -> x3, blocking collectives: none -> 88.8 us  [the longest x1 39.5 us: body(): lax.all_to_all(jnp.broadcast_to(bias, (64, 128, 128)), CHIP, split_axis=0...]
    pallas_call x0 -> x5, Pallas kernels: none -> 61.4 us  [the longest x1 41.3 us: attention(): pl.pallas_call(attention_kernel, grid=(count,), in_specs=[smem, smem, who...]
    dot_general x15 -> x0, matrix products: 59.2 us -> none  [the longest x5 29.2 us: attend(): jnp.einsum('shij,sjhd->sihd', weights, value_heads, preferred_element_typ...]
    all_gather x1 -> x0, blocking collectives: 33.4 us -> none  [body(): bias_rows = lax.all_gather(bias_local, 'col', axis=2, tiled=True)]
    sub x5 -> x0, matrix products: 24.1 us -> none  [attend(): scores = scores - jnp.max(scores, axis=-1, keepdims=True)]
    all_to_all x3 -> x1, local copies, waits for them, and re-layouts: 22.6 us -> 0.14 us  [body(): lax.all_to_all(triangle(blocks), ALL, split_axis=0, concat_axis=0, tiled=...]
  transfers between devices with their start and end apart: 9 -> 6, of which waited for: 8 -> 4; matrix products, arithmetic and copies ran while one was open for 4% -> 4% of each run, Pallas kernels for 0% -> 1%
where the time goes in v1:
time: 262 us; the launch traced here: 261 us
  blocking collectives  88.8 us (34%)
  waiting for transfers between devices  61.9 us (24%)
  Pallas kernels  61.4 us (23%)
  starting transfers between devices  22.4 us (9%)
  local copies, waits for them, and re-layouts  20.3 us (8%)
  other arithmetic  5.54 us (2%)
    pallas_call x1, Pallas kernels, attention(): pl.pallas_call(attention_kernel, grid=(count,), in_specs=[smem, smem, who...  41.3 us
    all_to_all x1, blocking collectives, body(): lax.all_to_all(jnp.broadcast_to(bias, (64, 128, 128)), CHIP, split_axis=0...  39.5 us
    all_to_all x1, blocking collectives, body(): lax.all_to_all(jnp.broadcast_to(right[None], (8, 8, 5, 16, 128)).reshape(...  25.9 us
    all_to_all x1, blocking collectives, body(): blocks = lax.all_to_all(tri, ALL, split_axis=0, concat_axis=0, tiled=True)  23.4 us
    all_to_all x1, waiting for transfers between devices, body(): lax.all_to_all(jnp.broadcast_to(left[:, None], (16, 8, 5, 8, 128)).reshap...  18.4 us
    all_to_all x1, waiting for transfers between devices, body(): lax.all_to_all(out_seq, ROW, split_axis=0, concat_axis=0, tiled=True)  14.8 us
    all_to_all x1, waiting for transfers between devices, body(): lax.all_to_all(alignment.reshape(16, 5, 32, 256), ROW, split_axis=0, conc...  14.8 us
    all_to_all x1, waiting for transfers between devices, body(): lax.all_to_all(triangle(blocks), ALL, split_axis=0, concat_axis=0, tiled=...  13.8 us
  transfers between devices with their start and end apart: 6, of which 4 were waited for; matrix products, arithmetic and copies ran while one was open for 4% of the time, Pallas kernels for 1%

profile of v1, /device:TPU:1, one launch (start us, length us, event | category | flops | bytes accessed | tf_op | source)
XLA Modules:
  0.0 261.3 jit_solution(11729799070032198720)
XLA Ops:
  0.6 0.0 copy-start.1
  0.6 1.0 copy-done.1
  1.7 0.7 copy-done.8
  2.4 1.0 pair_bias.1
  3.3 0.5 broadcast_in_dim.8
  3.8 39.5 %all_to_all.35.own_ref = bf16[64,128,128]{2,1,0:T(8,128)(2,1)S(1)} all-to-all(bf16[64,128,128]{2,1,0:T(8,128)(2,1)S(1)} %broadcast_in_dim.8), channel_id=1, replica_groups=mesh['x'=4,'zl'=2,'core'=2,'zh'=2,'y'=4] {'x','zl','zh','y'}, dimensions={0} | all-to-all | bytes 4194304 | tf_op jit(solution)/shard_map/all_to_all | solution.py:353
  43.3 2.3 collective-permute-start
  45.6 3.7 %all-to-all-start.1 = ((bf16[16,5,32,256]{3,2,1,0:T(8,128)(2,1)}), bf16[16,5,32,256]{3,2,1,0:T(8,128)(2,1)S(1)}, u32[]{:S(2)}, u32[]{:S(2)}) async-start(bf16[16,5,32,256]{3,2,1,0:T(8,128)(2,1)} %bitcast.55), calls=%async_computation.1 | async-start | bytes 2621440 | tf_op jit(solution)/shard_map/all_to_all | solution.py:356
  49.4 0.0 copy-done.13
  49.4 0.0 copy-done.14
  49.4 0.0 copy-done.11
  49.4 0.6 tile.11
  50.1 0.9 copy.43.wl_ref
  51.0 1.9 copy.53
  53.0 0.1 dynamic_slice.16.seq_ref
  53.1 14.8 %all-to-all-done.1.x_ref = bf16[16,5,32,256]{3,2,1,0:T(8,128)(2,1)S(1)} async-done(((bf16[16,5,32,256]{3,2,1,0:T(8,128)(2,1)}), bf16[16,5,32,256]{3,2,1,0:T(8,128)(2,1)S(1)}, u32[]{:S(2)}, u32[]{:S(2)}) %all-to-all-start.1) | async-done | bytes 1310752 | tf_op jit(solution)/shard_map/all_to_all | solution.py:356
  67.9 0.0 collective-permute-done.other_ref
  67.9 0.1 broadcast_in_dim.9.live_col_ref
  68.0 0.0 copy-start.3
  68.0 1.0 copy-done.3
  69.0 0.9 copy-done.6
  70.0 41.3 %row_attention.1 = (bf16[16,5,32,256]{3,2,1,0:T(8,128)(2,1)}, bf16[16,5,8,128]{3,2,1,0:T(8,128)(2,1)S(1)}, bf16[8,5,16,128]{3,2,1,0:T(8,128)(2,1)S(1)}) custom-call(s32[1]{0:T(128)} %bitcast.core_ref, f32[5]{0:T(128)S(1)} %dynamic_slice.16.seq_ref, bf16[64,128,128]{2,1,0:T(8,128)(2,1)S(1)} %all_to_all.35.own_ref, ...), custom_call_target="tpu_custom_call" | custom-call | tf_op jit(solution)/shard_map/row_attention/pallas_call | solution.py:169
  111.2 0.2 broadcast_in_dim.11
  111.4 25.9 %all_to_all.36 = bf16[64,80,128]{2,1,0:T(8,128)(2,1)S(1)} all-to-all(bf16[64,80,128]{2,1,0:T(8,128)(2,1)S(1)} %bitcast.53), channel_id=1, replica_groups=mesh['x'=4,'zl'=2,'core'=2,'zh'=2,'y'=4] {'x','zl','zh','y'}, dimensions={0} | all-to-all | bytes 2621440 | tf_op jit(solution)/shard_map/all_to_all | solution.py:373
  137.3 1.2 broadcast_in_dim.10
  138.5 6.1 %all-to-all-start.3 = ((bf16[128,40,128]{2,1,0:T(8,128)(2,1)}), bf16[128,40,128]{2,1,0:T(8,128)(2,1)S(1)}, u32[]{:S(2)}, u32[]{:S(2)}) async-start(bf16[128,40,128]{2,1,0:T(8,128)(2,1)} %bitcast.51), calls=%async_computation.3 | async-start | bytes 2621440 | tf_op jit(solution)/shard_map/all_to_all | solution.py:380
  144.7 1.1 collective-permute-start.1
  145.8 0.1 dynamic_slice.19
  145.9 0.1 mul.76
  146.0 0.1 copy.45
  146.1 0.1 mul.78
  146.2 0.1 mul.79
  146.3 0.1 dynamic_slice.20
  146.3 0.1 mul.82
  146.4 0.1 copy.44
  146.5 0.1 copy.49.w_ref
  146.7 0.1 copy.48
  146.8 0.6 convert_reduce_fusion
  147.5 0.7 maximum_divide_fusion
  148.1 18.4 %all-to-all-done.3 = bf16[128,40,128]{2,1,0:T(8,128)(2,1)S(1)} async-done(((bf16[128,40,128]{2,1,0:T(8,128)(2,1)}), bf16[128,40,128]{2,1,0:T(8,128)(2,1)S(1)}, u32[]{:S(2)}, u32[]{:S(2)}) %all-to-all-start.3) | async-done | bytes 1310752 | tf_op jit(solution)/shard_map/all_to_all | solution.py:380
  166.6 1.4 reshape.115
  168.0 1.4 dynamic-slice_bitcast_fusion.1
  169.4 1.2 pad_maximum_fusion.1
  170.6 0.0 collective-permute-done.1
  170.6 3.1 %pad_maximum_fusion = bf16[128,80,128]{2,1,0:T(8,128)(2,1)} fusion(bf16[64,80,128]{2,1,0:T(8,128)(2,1)} %collective-permute-done.1, bf16[64,80,128]{2,1,0:T(8,128)(2,1)S(1)} %all_to_all.36), kind=kLoop, calls=%fused_computation | loop fusion | flops 1310720 | bytes 5242880 | tf_op jit(solution)/shard_map/concatenate | solution.py:392
  173.7 3.9 %reshape.118.r_ref = bf16[640,2048]{1,0:T(8,128)(2,1)S(1)} reshape(bf16[128,80,128]{2,1,0:T(8,128)(2,1)} %pad_maximum_fusion) | data formatting | bytes 5242880 | tf_op jit(solution)/shard_map/reshape | solution.py:392
  177.5 0.0 copy-done.2
  177.6 0.0 copy-start
  177.6 1.3 copy-done
  178.9 12.8 %outer_update.1 = (bf16[4,8,64,128]{3,2,1,0:T(8,128)(2,1)S(1)}, bf16[2,8,256,128]{3,2,1,0:T(8,128)(2,1)S(1)}) custom-call(bf16[640,1024]{1,0:T(8,128)(2,1)S(1)} %bitcast.41, bf16[640,2048]{1,0:T(8,128)(2,1)S(1)} %reshape.118.r_ref, bf16[128,1024]{1,0:T(8,128)(2,1)S(1)} %copy.49.w_ref, f32[2,8,1,128]{3,2,1,0:T(1,128)S(1)} %get-tuple-element.12.inv_ref, ...), custom_call_target="tpu_custom_call" | custom-call | tf_op jit(solution)/shard_map/outer_update/pallas_call | solution.py:240
  191.6 0.7 copy.56
  192.3 23.4 %all_to_all.37.in_ref = bf16[128,2,16,128]{3,2,1,0:T(8,128)(2,1)S(1)} all-to-all(bf16[128,2,16,128]{3,2,1,0:T(8,128)(2,1)S(1)} %bitcast.54), channel_id=1, replica_groups=mesh['x'=4,'zl'=2,'core'=2,'zh'=2,'y'=4] {'x','zl','core','zh','y'}, dimensions={0} | all-to-all | bytes 2097152 | tf_op jit(solution)/shard_map/all_to_all | solution.py:414
  215.8 0.0 copy-done.4
  215.8 4.8 %all-to-all-start.2 = ((bf16[16,5,32,256]{3,2,1,0:T(8,128)(2,1)}), bf16[16,5,32,256]{3,2,1,0:T(8,128)(2,1)S(1)}, u32[]{:S(2)}, u32[]{:S(2)}) async-start(bf16[16,5,32,256]{3,2,1,0:T(8,128)(2,1)} %get-tuple-element.7), calls=%async_computation.2 | async-start | bytes 2621440 | tf_op jit(solution)/shard_map/all_to_all | solution.py:393
  220.6 3.8 %triangle.1 = bf16[128,16,128]{2,1,0:T(8,128)(2,1)} custom-call(bf16[128,2,16,128]{3,2,1,0:T(8,128)(2,1)S(1)} %all_to_all.37.in_ref), custom_call_target="tpu_custom_call" | custom-call | tf_op jit(solution)/shard_map/triangle/pallas_call | solution.py:294
  224.3 14.8 %all-to-all-done.2 = bf16[16,5,32,256]{3,2,1,0:T(8,128)(2,1)S(1)} async-done(((bf16[16,5,32,256]{3,2,1,0:T(8,128)(2,1)}), bf16[16,5,32,256]{3,2,1,0:T(8,128)(2,1)S(1)}, u32[]{:S(2)}, u32[]{:S(2)}) %all-to-all-start.2) | async-done | bytes 1310752 | tf_op jit(solution)/shard_map/all_to_all | solution.py:393
  239.2 4.3 %all-to-all-start.6 = ((bf16[128,16,128]{2,1,0:T(8,128)(2,1)}), bf16[128,16,128]{2,1,0:T(8,128)(2,1)S(1)}, u32[]{:S(2)}, u32[]{:S(2)}) async-start(bf16[128,16,128]{2,1,0:T(8,128)(2,1)} %triangle.1), calls=%async_computation.6 | async-start | bytes 1048576 | tf_op jit(solution)/shard_map/all_to_all | solution.py:415
  243.5 0.1 copy.52
  243.6 13.8 %all-to-all-done.6 = bf16[128,16,128]{2,1,0:T(8,128)(2,1)S(1)} async-done(((bf16[128,16,128]{2,1,0:T(8,128)(2,1)}), bf16[128,16,128]{2,1,0:T(8,128)(2,1)S(1)}, u32[]{:S(2)}, u32[]{:S(2)}) %all-to-all-start.6) | async-done | bytes 524320 | tf_op jit(solution)/shard_map/all_to_all | solution.py:415
  257.4 0.1 copy.57
  257.6 0.0 copy-done.5
  257.6 0.0 copy-done.7
  257.6 2.6 %pair_final.1 = bf16[32,64,128]{2,1,0:T(8,128)(2,1)} custom-call(bf16[16,128,128]{2,1,0:T(8,128)(2,1)S(1)} %bitcast.44, bf16[32,64,128]{2,1,0:T(8,128)(2,1)S(1)} %bitcast.46, bf16[128,128]{1,0:T(8,128)(2,1)S(1)} %bitcast.48, bf16[128,128]{1,0:T(8,128)(2,1)S(1)} %copy-done.7), custom_call_target="tpu_custom_call" | custom-call | tf_op jit(solution)/shard_map/pair_final/pallas_call | solution.py:320
  260.2 1.1 copy.59
  (21 shorter events, 0.1 us)
Async XLA Ops:
  0.6 1.0 copy-start.1
  1.7 0.7 copy-start.8
  43.3 24.5 %collective-permute-start = (bf16[64,128,128]{2,1,0:T(8,128)(2,1)S(1)}, bf16[64,128,128]{2,1,0:T(8,128)(2,1)}, u32[]{:S(2)}, u32[]{:S(2)}) collective-permute-start(bf16[64,128,128]{2,1,0:T(8,128)(2,1)S(1)} %all_to_all.35.own_ref), channel_id=1, source_target_pairs={{0,8},{8,0},{1,9},{9,1},{2,10},{10,2},{3,11},{11,3},{4,12},{12,4},... | collective-permute-start | bytes 6291464 | tf_op jit(solution)/shard_map/ppermute | solution.py:359
  45.6 3.8 %copy-start.13 = (s32[640]{0:T(1024)S(1)}, s32[640]{0:T(1024)}, u32[]{:S(2)}) copy-start(s32[640]{0:T(1024)} %param.15) | copy-start | bytes 7684
  45.6 3.8 %copy-start.14 = (s32[512]{0:T(512)S(1)}, s32[512]{0:T(512)}, u32[]{:S(2)}) copy-start(s32[512]{0:T(512)} %param.14) | copy-start | bytes 6148
  45.6 3.8 %copy-start.11 = (bf16[256,2,32]{0,2,1:T(8,128)(2,1)S(1)}, bf16[256,2,32]{0,2,1:T(8,128)(2,1)}, u32[]{:S(2)}) copy-start(bf16[256,2,32]{0,2,1:T(8,128)(2,1)} %param.19) | copy-start | bytes 98308
  45.6 22.2 %all-to-all-start.1 = ((bf16[16,5,32,256]{3,2,1,0:T(8,128)(2,1)}), bf16[16,5,32,256]{3,2,1,0:T(8,128)(2,1)S(1)}, u32[]{:S(2)}, u32[]{:S(2)}) async-start(bf16[16,5,32,256]{3,2,1,0:T(8,128)(2,1)} %bitcast.55), calls=%async_computation.1 | async-start | bytes 2621440 | tf_op jit(solution)/shard_map/all_to_all | solution.py:356
  68.0 1.0 copy-start.3
  69.0 0.9 copy-start.6
  138.5 7.9 %copy-start.9 = (bf16[1024,128]{1,0:T(8,128)(2,1)S(1)}, bf16[1024,128]{1,0:T(8,128)(2,1)}, u32[]{:S(2)}) copy-start(bf16[1024,128]{1,0:T(8,128)(2,1)} %param.20) | copy-start | bytes 786436
  138.5 8.1 %copy-start.10 = (bf16[128,4,128]{2,1,0:T(4,128)(2,1)S(1)}, bf16[128,4,128]{2,1,0:T(4,128)(2,1)}, u32[]{:S(2)}) copy-start(bf16[128,4,128]{2,1,0:T(4,128)(2,1)} %param.21) | copy-start | bytes 393220
  138.5 28.0 %all-to-all-start.3 = ((bf16[128,40,128]{2,1,0:T(8,128)(2,1)}), bf16[128,40,128]{2,1,0:T(8,128)(2,1)S(1)}, u32[]{:S(2)}, u32[]{:S(2)}) async-start(bf16[128,40,128]{2,1,0:T(8,128)(2,1)} %bitcast.51), calls=%async_computation.3 | async-start | bytes 2621440 | tf_op jit(solution)/shard_map/all_to_all | solution.py:380
  144.7 25.9 %collective-permute-start.1 = (bf16[64,80,128]{2,1,0:T(8,128)(2,1)S(1)}, bf16[64,80,128]{2,1,0:T(8,128)(2,1)}, u32[]{:S(2)}, u32[]{:S(2)}) collective-permute-start(bf16[64,80,128]{2,1,0:T(8,128)(2,1)S(1)} %all_to_all.36), channel_id=1, source_target_pairs={{0,8},{8,0},{1,9},{9,1},{2,10},{10,2},{3,11},{11,3},{4,12},{12,4},... | collective-permute-start | bytes 3932168 | tf_op jit(solution)/shard_map/ppermute | solution.py:387
  173.6 3.9 %copy-start.2 = (bf16[32,64,128]{2,1,0:T(8,128)(2,1)S(1)}, bf16[32,64,128]{2,1,0:T(8,128)(2,1)}, u32[]{:S(2)}) copy-start(bf16[32,64,128]{2,1,0:T(8,128)(2,1)} %pair_ref.1) | copy-start | bytes 1572868
  177.6 1.3 copy-start
  191.6 24.1 %copy-start.4 = (bf16[4,8,64,128]{3,2,1,0:T(8,128)(2,1)}, bf16[4,8,64,128]{3,2,1,0:T(8,128)(2,1)S(1)}, u32[]{:S(2)}) copy-start(bf16[4,8,64,128]{3,2,1,0:T(8,128)(2,1)S(1)} %get-tuple-element.11) | copy-start | bytes 1572868
  215.8 23.4 %all-to-all-start.2 = ((bf16[16,5,32,256]{3,2,1,0:T(8,128)(2,1)}), bf16[16,5,32,256]{3,2,1,0:T(8,128)(2,1)S(1)}, u32[]{:S(2)}, u32[]{:S(2)}) async-start(bf16[16,5,32,256]{3,2,1,0:T(8,128)(2,1)} %get-tuple-element.7), calls=%async_computation.2 | async-start | bytes 2621440 | tf_op jit(solution)/shard_map/all_to_all | solution.py:393
  220.6 22.9 %copy-start.12 = (bf16[128,128]{1,0:T(8,128)(2,1)S(1)}, bf16[128,128]{1,0:T(8,128)(2,1)}, u32[]{:S(2)}) copy-start(bf16[128,128]{1,0:T(8,128)(2,1)} %param.23) | copy-start | bytes 98308
  224.3 33.2 %copy-start.5 = (bf16[4,8,64,128]{3,2,1,0:T(8,128)(2,1)S(1)}, bf16[4,8,64,128]{3,2,1,0:T(8,128)(2,1)}, u32[]{:S(2)}) copy-start(bf16[4,8,64,128]{3,2,1,0:T(8,128)(2,1)} %copy-done.4) | copy-start | bytes 1572868
  224.3 33.2 %copy-start.7 = (bf16[128,128]{1,0:T(8,128)(2,1)S(1)}, bf16[128,128]{1,0:T(8,128)(2,1)}, u32[]{:S(2)}) copy-start(bf16[128,128]{1,0:T(8,128)(2,1)} %wg_ref.1) | copy-start | bytes 98308
  239.2 18.2 %all-to-all-start.6 = ((bf16[128,16,128]{2,1,0:T(8,128)(2,1)}), bf16[128,16,128]{2,1,0:T(8,128)(2,1)S(1)}, u32[]{:S(2)}, u32[]{:S(2)}) async-start(bf16[128,16,128]{2,1,0:T(8,128)(2,1)} %triangle.1), calls=%async_computation.6 | async-start | bytes 1048576 | tf_op jit(solution)/shard_map/all_to_all | solution.py:415

commit v2 on v1

--- a/solution.py
+++ b/solution.py
@@ -63,10 +63,16 @@
 
 
 def attention_kernel(
-    core_ref,
+    place_ref,
     seq_ref,
-    own_ref,
-    other_ref,
+    own0_ref,
+    own1_ref,
+    own2_ref,
+    own3_ref,
+    other0_ref,
+    other1_ref,
+    other2_ref,
+    other3_ref,
     x_ref,
     win_ref,
     wo_ref,
@@ -75,13 +81,13 @@
     live_ref,
     live_col_ref,
     out_ref,
-    left_ref,
-    right_ref,
+    factor_ref,
     bias_ref,
     q_ref,
     k_ref,
     v_ref,
     acc_ref,
+    penalty_ref,
 ):
     heads = bias_ref.shape[0]
     step = pl.program_id(0)
@@ -89,21 +95,40 @@
     @pl.when(step == 0)
     def _():
         penalty = (live_ref[...] - 1.0) * BIG
-
-        def assemble(xz, carry):
-            for ref, core in ((own_ref, core_ref[0]), (other_ref, 1 - core_ref[0])):
-                base = pl.multiple_of((xz * 2 + core) * 32, 32)
-                for h in range(heads):
-                    for m in range(4):
-                        even = ref[xz * 8 + 2 * m, 16 * h : 16 * h + 16, :].astype(F32)
-                        odd = ref[xz * 8 + 2 * m + 1, 16 * h : 16 * h + 16, :].astype(F32)
-                        low, high = mix(even, odd)
-                        pen = penalty[:, 128 * m : 128 * m + 128]
-                        bias_ref[h, pl.ds(base, 16), 128 * m : 128 * m + 128] = low + pen
-                        bias_ref[h, pl.ds(base + 16, 16), 128 * m : 128 * m + 128] = high + pen
-            return carry
-
-        lax.fori_loop(0, 8, assemble, 0)
+        own = (own0_ref, own1_ref, own2_ref, own3_ref)
+        other = (other0_ref, other1_ref, other2_ref, other3_ref)
+        core, y = place_ref[0], place_ref[1]
+
+        def assemble(pairs):
+            def at_chips(xz, carry):
+                for refs, side in ((own, core), (other, 1 - core)):
+                    base = pl.multiple_of((xz * 2 + side) * 32, 32)
+                    for even_at, odd_at in pairs:
+                        y_even = lax.rem(y + 4 - even_at, 4)
+                        for zh in range(2):
+                            lanes = pl.ds(pl.multiple_of((zh * 2 + y_even // 2) * 128, 128), 128)
+                            pen = penalty_ref[:, lanes]
+                            for h in range(heads):
+                                rows = slice(16 * h, 16 * h + 16)
+                                low, high = mix(
+                                    refs[even_at][xz * 2 + zh, rows, :].astype(F32),
+                                    refs[odd_at][xz * 2 + zh, rows, :].astype(F32),
+                                )
+                                bias_ref[h, pl.ds(base, 16), lanes] = low + pen
+                                bias_ref[h, pl.ds(base + 16, 16), lanes] = high + pen
+                return carry
+
+            lax.fori_loop(0, 8, at_chips, 0)
+
+        penalty_ref[...] = penalty
+
+        @pl.when(lax.rem(y, 2) == 0)
+        def _():
+            assemble(((0, 3), (2, 1)))
+
+        @pl.when(lax.rem(y, 2) == 1)
+        def _():
+            assemble(((1, 0), (3, 2)))
 
     x = x_ref[:, 0].reshape(512, 256)
     normed = layer_norm(x).astype(BF16)
@@ -146,17 +171,20 @@
     packed = left[:, 0]
     for q in range(1, 4):
         packed = jnp.where(group == q, left[:, q], packed)
-    left_ref[:, 0] = packed.astype(BF16)
     right = lax.dot_general(wr_ref[...], second, NT, preferred_element_type=F32)
     right = right * (live_ref[...] * seq_live)
     for m in range(4):
         tile = right[:, 128 * m : 128 * m + 128]
-        even, odd = mix(tile[:16], tile[16:])
-        right_ref[2 * m, 0] = even.astype(BF16)
-        right_ref[2 * m + 1, 0] = odd.astype(BF16)
-
-
-def attention(core, seq_live, own, other, x, win, wo, wl, wr, live, live_col):
+        for c, chunk in enumerate(mix(tile[:16], tile[16:])):
+            for core in range(2):
+                half = chunk[8 * core : 8 * core + 8]
+                for xz in range(8):
+                    factor_ref[xz, core, 2 * m + c, 0] = jnp.concatenate(
+                        [packed[2 * xz + core], half], axis=0
+                    ).astype(BF16)
+
+
+def attention(place, seq_live, biases, x, win, wo, wl, wr, live, live_col):
     count = x.shape[1]
     smem = pl.BlockSpec(memory_space=pltpu.SMEM)
 
@@ -172,8 +200,7 @@
         in_specs=[
             smem,
             smem,
-            whole(own),
-            whole(other),
+            *(whole(b) for b in biases),
             per_seq(16, 1, 32, 256),
             whole(win),
             whole(wo),
@@ -184,13 +211,11 @@
         ],
         out_specs=[
             per_seq(16, 1, 32, 256),
-            per_seq(16, 1, 8, 128),
-            per_seq(8, 1, 16, 128),
+            pl.BlockSpec((8, 2, 8, 1, 16, 128), lambda s: (0, 0, 0, s, 0, 0)),
         ],
         out_shape=[
             jax.ShapeDtypeStruct(x.shape, BF16),
-            jax.ShapeDtypeStruct((16, count, 8, 128), BF16),
-            jax.ShapeDtypeStruct((8, count, 16, 128), BF16),
+            jax.ShapeDtypeStruct((8, 2, 8, count, 16, 128), BF16),
         ],
         scratch_shapes=[
             pltpu.VMEM((8, 512, 512), F32),
@@ -198,22 +223,25 @@
             pltpu.VMEM((512, 256), BF16),
             pltpu.VMEM((512, 256), BF16),
             pltpu.VMEM((512, 256), F32),
+            pltpu.VMEM((1, 512), F32),
         ],
         compiler_params=params(48),
         name="row_attention",
-    )(core, seq_live, own, other, x, win, wo, wl, wr, live, live_col)
-
-
-def outer_kernel(l_ref, r_ref, w_ref, inv_ref, plane_ref, pair_ref, wp_ref, mid_ref, tri_ref, x_ref):
-    product = lax.dot_general(l_ref[...], r_ref[...], TN, preferred_element_type=F32)
-    for half in range(2):
-        for u in range(16):
-            first = product[32 * half : 32 * half + 32, 128 * u : 128 * u + 128]
-            second = product[32 * half + 64 : 32 * half + 96, 128 * u : 128 * u + 128]
-            low, high = mix(first, second)
+    )(place, seq_live, *biases, x, win, wo, wl, wr, live, live_col)
+
+
+def outer_kernel(core_ref, l_ref, own_ref, other_ref, w_ref, inv_ref, plane_ref, pair_ref, wp_ref, mid_ref, tri_ref, x_ref):
+    for ref, core in ((own_ref, core_ref[0]), (other_ref, 1 - core_ref[0])):
+        product = lax.dot_general(l_ref[...], ref[...], TN, preferred_element_type=F32)
+        for half in range(2):
             columns = slice(128 * half, 128 * half + 128)
-            x_ref[64 * u : 64 * u + 32, columns] = low.astype(BF16)
-            x_ref[64 * u + 32 : 64 * u + 64, columns] = high.astype(BF16)
+            for u in range(8):
+                first = product[32 * half : 32 * half + 32, 128 * u : 128 * u + 128]
+                second = product[32 * half + 64 : 32 * half + 96, 128 * u : 128 * u + 128]
+                low, high = mix(first, second)
+                base = pl.multiple_of(core * 512 + 64 * u, 64)
+                x_ref[pl.ds(base, 32), columns] = low.astype(BF16)
+                x_ref[pl.ds(base + 32, 32), columns] = high.astype(BF16)
     update = jnp.dot(w_ref[...], x_ref[...], preferred_element_type=F32)
     for half in range(2):
         part = update[:, 128 * half : 128 * half + 128] * inv_ref[half, 0]
@@ -228,7 +256,7 @@
         tri_ref[half, 0, 128:] = (jax.nn.sigmoid(terms[256:384]) * terms[384:] * plane).astype(BF16)
 
 
-def outer_update(left, right, weight, inv, plane, pairwise, wp):
+def outer_update(core, left, own, other, weight, inv, plane, pairwise, wp):
     total = left.shape[0]
 
     def whole(a):
@@ -241,8 +269,10 @@
         outer_kernel,
         grid=(8,),
         in_specs=[
+            pl.BlockSpec(memory_space=pltpu.SMEM),
             by_v(total, 128),
-            whole(right),
+            whole(own),
+            whole(other),
             whole(weight),
             by_v(2, 1, 1, 128),
             by_v(2, 1, 1, 128),
@@ -257,7 +287,7 @@
         scratch_shapes=[pltpu.VMEM((1024, 256), BF16)],
         compiler_params=params(32),
         name="outer_update",
-    )(left, right, weight, inv, plane, pairwise, wp)
+    )(core, left, own, other, weight, inv, plane, pairwise, wp)
 
 
 def triangle_kernel(in_ref, out_ref, a_ref, b_ref):
@@ -350,18 +380,25 @@
     my_seqs = lax.dynamic_slice_in_dim(seq_live, col * 80 + row * 5, 5)
 
     bias = pair_bias(pairwise, bias_project.T).astype(BF16).reshape(128, 128)
-    bias_own = lax.all_to_all(
-        jnp.broadcast_to(bias, (64, 128, 128)), CHIP, split_axis=0, concat_axis=0, tiled=True
-    )
-    sequences = lax.all_to_all(
-        alignment.reshape(16, 5, 32, 256), ROW, split_axis=0, concat_axis=0, tiled=True
-    )
-    bias_other = lax.ppermute(bias_own, "core", swap)
-    out_seq, left, right = attention(
-        core.reshape(1),
+    bias_plane = lax.all_to_all(
+        jnp.broadcast_to(bias, (16, 128, 128)),
+        ("x", "zl", "zh"),
+        split_axis=0,
+        concat_axis=0,
+        tiled=True,
+    )
+    own = [bias_plane] + [
+        lax.ppermute(bias_plane, "y", [(i, (i + d) % 4) for i in range(4)]) for d in (1, 2, 3)
+    ]
+    other = [lax.ppermute(b, "core", swap) for b in own]
+    outgoing, bias_plane = lax.optimization_barrier(
+        (alignment.reshape(16, 5, 32, 256), bias_plane)
+    )
+    sequences = lax.all_to_all(outgoing, ROW, split_axis=0, concat_axis=0, tiled=True)
+    out_seq, factors = attention(
+        jnp.stack([core, lax.axis_index("y")]),
         my_seqs,
-        bias_own,
-        bias_other,
+        own + other,
         sequences,
         attention_input_weight.reshape(256, 1024),
         attention_output_weight,
@@ -370,26 +407,14 @@
         res_live.reshape(1, 512),
         jnp.broadcast_to(res_live[:, None], (512, 128)),
     )
-    right_own = lax.all_to_all(
-        jnp.broadcast_to(right[None], (8, 8, 5, 16, 128)).reshape(64, 80, 128),
-        CHIP,
-        split_axis=0,
-        concat_axis=0,
-        tiled=True,
-    )
-    left_all = lax.all_to_all(
-        jnp.broadcast_to(left[:, None], (16, 8, 5, 8, 128)).reshape(128, 40, 128),
-        ALL,
-        split_axis=0,
-        concat_axis=0,
-        tiled=True,
-    )
+    factors = lax.all_to_all(
+        factors.reshape(128, 80, 128), ALL, split_axis=0, concat_axis=0, tiled=True
+    )
+    out_seq, factors = lax.optimization_barrier((out_seq, factors))
+    factors = factors.reshape(640, 16, 128)
+    right_own = factors[:, 8:].reshape(640, 1024)
     right_other = lax.ppermute(right_own, "core", swap)
-    left_all = left_all.reshape(8, 2, 320 // 8, 1024)
-    left_own = lax.dynamic_index_in_dim(left_all, core, 1, keepdims=False)
-    left_other = lax.dynamic_index_in_dim(left_all, 1 - core, 1, keepdims=False)
-    left_cat = jnp.concatenate([left_own, left_other], axis=0).reshape(640, 1024)
-    right_cat = jnp.concatenate([right_own, right_other], axis=0).reshape(640, 2048)
+    left = factors[:, :8].reshape(640, 1024)
     alignment_output = lax.all_to_all(
         out_seq, ROW, split_axis=0, concat_axis=0, tiled=True
     ).reshape(80, 32, 256)
@@ -402,14 +427,17 @@
 
     weight = outer_output.reshape(32, 2, 16, 128).transpose(3, 2, 1, 0).reshape(128, 1024)
     mid, tri = outer_update(
-        left_cat,
-        right_cat,
+        core.reshape(1),
+        left,
+        right_own,
+        right_other,
         weight,
         pairs(inv),
         pairs(plane),
         pairwise.reshape(4, 8, 64, 128),
         tri_project.reshape(128, 512).T,
     )
+    tri, alignment_output = lax.optimization_barrier((tri, alignment_output))
     tri = tri.reshape(16, 2, 128, 128).transpose(2, 1, 0, 3)
     blocks = lax.all_to_all(tri, ALL, split_axis=0, concat_axis=0, tiled=True)
     combined = lax.all_to_all(triangle(blocks), ALL, split_axis=0, concat_axis=0, tiled=True)

time: 262 us -> 225 us (0.86)
  waiting for transfers between devices: 61.9 us -> 34.6 us
  local copies, waits for them, and re-layouts: 20.3 us -> 14.1 us
  other arithmetic: 5.54 us -> 1.36 us
  blocking collectives: 88.8 us -> 85.3 us
  starting transfers between devices: 22.4 us -> 25.1 us
    all_to_all x2 -> x1, waiting for transfers between devices: 33.3 us -> 0.01 us  [body(): lax.all_to_all(outgoing, ROW, split_axis=0, concat_axis=0, tiled=True)]
    ppermute x1 -> x7, waiting for transfers between devices: 0.01 us -> 20.8 us  [the longest x3 19.9 us: body(): lax.ppermute(bias_plane, 'y', [(i, (i + d) % 4) for i in range(4)])]
    all_to_all x1, waiting for transfers between devices: 14.8 us -> 0.01 us  [body(): lax.all_to_all(out_seq, ROW, split_axis=0, concat_axis=0, tiled=True)]
    ppermute x1 -> x7, starting transfers between devices: 2.29 us -> 8.19 us  [the longest x3 5.05 us: body(): lax.ppermute(bias_plane, 'y', [(i, (i + d) % 4) for i in range(4)])]
    reshape x2 -> x0, local copies, waits for them, and re-layouts: 5.32 us -> none  [the longest x1 3.88 us: body(): jnp.concatenate([right_own, right_other], axis=0).reshape(640, 2048)]
    all_to_all x2, blocking collectives: 65.4 us -> 61.1 us  [the longest x1 42.4 us: body(): lax.all_to_all(factors.reshape(128, 80, 128), ALL, split_axis=0, concat_a...]
    concatenate x2 -> x0, other arithmetic: 4.25 us -> none  [the longest x1 3.05 us: body(): jnp.concatenate([right_own, right_other], axis=0).reshape(640, 2048)]
    all_to_all x2 -> x1, starting transfers between devices: 9.87 us -> 6.15 us  [body(): lax.all_to_all(outgoing, ROW, split_axis=0, concat_axis=0, tiled=True)]
  transfers between devices with their start and end apart: 6 -> 11, of which waited for: 4 -> 5; matrix products, arithmetic and copies ran while one was open for 4% -> 3% of each run, Pallas kernels for 1% -> 6%
where the time goes in v2:
time: 225 us; the launch traced here: 224 us
  blocking collectives  85.3 us (38%)
  Pallas kernels  62.8 us (28%)
  waiting for transfers between devices  34.6 us (15%)
  starting transfers between devices  25.1 us (11%)
  local copies, waits for them, and re-layouts  14.1 us (6%)
    all_to_all x1, blocking collectives, body(): lax.all_to_all(factors.reshape(128, 80, 128), ALL, split_axis=0, concat_a...  42.4 us
    pallas_call x1, Pallas kernels, attention(): pl.pallas_call(attention_kernel, grid=(count,), in_specs=[smem, smem, *(w...  41.7 us
    all_to_all x1, blocking collectives, body(): blocks = lax.all_to_all(tri, ALL, split_axis=0, concat_axis=0, tiled=True)  24.2 us
    ppermute x3, waiting for transfers between devices, body(): lax.ppermute(bias_plane, 'y', [(i, (i + d) % 4) for i in range(4)])  19.9 us
    all_to_all x1, blocking collectives, body(): lax.all_to_all(jnp.broadcast_to(bias, (16, 128, 128)), ('x', 'zl', 'zh'),...  18.8 us
    all_to_all x1, waiting for transfers between devices, body(): lax.all_to_all(triangle(blocks), ALL, split_axis=0, concat_axis=0, tiled=...  13.8 us
    pallas_call x1, Pallas kernels, outer_update(): pl.pallas_call(outer_kernel, grid=(8,), in_specs=[pl.BlockSpec(memory_spa...  13.8 us
    unnamed x28, local copies, waits for them, and re-layouts  9.56 us
  transfers between devices with their start and end apart: 11, of which 5 were waited for; matrix products, arithmetic and copies ran while one was open for 3% of the time, Pallas kernels for 6%

profile of v2, /device:TPU:1, one launch (start us, length us, event | category | flops | bytes accessed | tf_op | source)
XLA Modules:
  0.0 224.2 jit_solution(6607888471550829623)
XLA Ops:
  0.6 0.0 copy-start
  0.6 1.0 copy-done
  1.7 0.7 copy-done.5
  2.4 1.0 pair_bias.1
  3.3 0.1 broadcast_in_dim.4
  3.4 18.8 %all_to_all.30.own0_ref = bf16[16,128,128]{2,1,0:T(8,128)(2,1)S(1)} all-to-all(bf16[16,128,128]{2,1,0:T(8,128)(2,1)S(1)} %broadcast_in_dim.4), channel_id=1, replica_groups=mesh['x'=4,'zl'=2,'core'=2,'zh'=2,'y'=4] {'x','zl','zh'}, dimensions={0} | all-to-all | bytes 1048576 | tf_op jit(solution)/shard_map/all_to_all | solution.py:383
  22.2 6.1 %all-to-all-start.1 = ((bf16[16,5,32,256]{3,2,1,0:T(8,128)(2,1)}), bf16[16,5,32,256]{3,2,1,0:T(8,128)(2,1)}, u32[]{:S(2)}, u32[]{:S(2)}) async-start(bf16[16,5,32,256]{3,2,1,0:T(8,128)(2,1)} %bitcast.4), calls=%async_computation.1 | async-start | bytes 2621440 | tf_op jit(solution)/shard_map/all_to_all | solution.py:397
  28.4 1.4 collective-permute-start
  29.7 2.6 %collective-permute-start.1 = (bf16[16,128,128]{2,1,0:T(8,128)(2,1)S(1)}, bf16[16,128,128]{2,1,0:T(8,128)(2,1)S(1)}, u32[]{:S(2)}, u32[]{:S(2)}) collective-permute-start(bf16[16,128,128]{2,1,0:T(8,128)(2,1)S(1)} %all_to_all.30.own0_ref), channel_id=1, source_target_pairs={{0,2},{1,3},{2,0},{3,1},{4,6},{5,7},{6,4},{7,5},{8,10},{9,11},{10,... | collective-permute-start | bytes 1572872 | tf_op jit(solution)/shard_map/ppermute | solution.py:391
  32.4 1.1 collective-permute-start.2
  33.4 1.1 collective-permute-start.3
  34.6 8.6 %collective-permute-done.own1_ref = bf16[16,128,128]{2,1,0:T(8,128)(2,1)S(1)} collective-permute-done((bf16[16,128,128]{2,1,0:T(8,128)(2,1)S(1)}, bf16[16,128,128]{2,1,0:T(8,128)(2,1)S(1)}, u32[]{:S(2)}, u32[]{:S(2)}) %collective-permute-start) | collective-permute-done | bytes 524320 | tf_op jit(solution)/shard_map/ppermute | solution.py:391
  43.1 0.9 collective-permute-start.4
  44.1 11.3 %collective-permute-done.1.own2_ref = bf16[16,128,128]{2,1,0:T(8,128)(2,1)S(1)} collective-permute-done((bf16[16,128,128]{2,1,0:T(8,128)(2,1)S(1)}, bf16[16,128,128]{2,1,0:T(8,128)(2,1)S(1)}, u32[]{:S(2)}, u32[]{:S(2)}) %collective-permute-start.1) | collective-permute-done | bytes 524320 | tf_op jit(solution)/shard_map/ppermute | solution.py:391
  55.4 1.1 collective-permute-start.5
  56.5 0.0 collective-permute-done.2.own3_ref
  56.5 0.0 collective-permute-start.6
  56.5 0.0 copy-done.9
  56.5 0.0 copy-done.10
  56.6 0.1 copy.43.wl_ref
  56.7 1.1 copy.53
  57.8 0.1 dynamic_slice.9.seq_ref
  57.9 0.1 pad_add_fusion.place_ref
  58.0 0.0 collective-permute-done.3.other0_ref
  58.0 0.0 collective-permute-done.4.other1_ref
  58.0 0.2 collective-permute-done.5.other2_ref
  58.1 0.7 collective-permute-done.6.other3_ref
  58.9 0.0 all-to-all-done.1.x_ref
  58.9 0.1 broadcast_in_dim.5.live_col_ref
  59.0 41.7 %row_attention.1 = (bf16[16,5,32,256]{3,2,1,0:T(8,128)(2,1)}, bf16[8,2,8,5,16,128]{5,4,3,2,1,0:T(8,128)(2,1)}) custom-call(s32[2]{0:T(128)S(1)} %pad_add_fusion.place_ref, f32[5]{0:T(128)S(1)} %dynamic_slice.9.seq_ref, bf16[16,128,128]{2,1,0:T(8,128)(2,1)S(1)} %all_to_all.30.own0_ref, bf16[16,128,128]{2,1,0:T(8,128)(2,1)S(1)} %collective-permute-done.own1_ref, ...), custom_call_target="tpu_custom_call" | custom-call | tf_op jit(solution)/shard_map/row_attention/pallas_call | solution.py:197
  100.7 42.4 %all_to_all.31 = bf16[128,80,128]{2,1,0:T(8,128)(2,1)S(1)} all-to-all(bf16[128,80,128]{2,1,0:T(8,128)(2,1)} %bitcast.61), channel_id=1, replica_groups=mesh['x'=4,'zl'=2,'core'=2,'zh'=2,'y'=4] {'x','zl','core','zh','y'}, dimensions={0} | all-to-all | bytes 5242880 | tf_op jit(solution)/shard_map/all_to_all | solution.py:410
  143.0 1.2 fusion
  144.3 0.4 copy.60
  144.6 0.0 copy-start.6
  144.7 1.6 collective-permute-start.7
  146.3 4.3 %all-to-all-start.3 = ((bf16[16,5,32,256]{3,2,1,0:T(8,128)(2,1)}), bf16[16,5,32,256]{3,2,1,0:T(8,128)(2,1)}, u32[]{:S(2)}, u32[]{:S(2)}) async-start(bf16[16,5,32,256]{3,2,1,0:T(8,128)(2,1)} %get-tuple-element.16), calls=%async_computation.3 | async-start | bytes 2621440 | tf_op jit(solution)/shard_map/all_to_all | solution.py:418
  150.6 0.1 dynamic_slice.10
  150.7 0.1 mul.76
  150.8 0.1 copy.45
  150.9 0.1 mul.78
  150.9 0.1 mul.79
  151.0 0.1 dynamic_slice.11
  151.1 0.1 mul.82
  151.2 0.0 copy-done.6
  151.2 0.1 copy.44
  151.3 0.1 copy.49.w_ref
  151.5 1.0 copy.48
  152.5 0.6 convert_reduce_fusion
  153.1 0.7 maximum_divide_fusion
  153.8 0.0 copy-start.1
  153.8 1.7 copy.61
  155.5 0.0 collective-permute-done.7.other_ref
  155.5 13.8 %outer_update.1 = (bf16[4,8,64,128]{3,2,1,0:T(8,128)(2,1)S(1)}, bf16[2,8,256,128]{3,2,1,0:T(8,128)(2,1)S(1)}) custom-call(s32[1]{0:T(128)} %bitcast.core_ref, bf16[640,1024]{1,0:T(8,128)(2,1)S(1)} %bitcast.47, bf16[640,1024]{1,0:T(8,128)(2,1)S(1)} %bitcast.46, bf16[640,1024]{1,0:T(8,128)(2,1)S(1)} %collective-permute-done.7.other_ref, ...), custom_call_target="tpu_custom_call" | custom-call | tf_op jit(solution)/shard_map/outer_update/pallas_call | solution.py:268
  169.4 1.0 copy-done.2
  170.3 0.0 all-to-all-done.3
  170.3 1.9 copy.62
  172.2 24.2 %all_to_all.32.in_ref = bf16[128,2,16,128]{3,2,1,0:T(8,128)(2,1)S(1)} all-to-all(bf16[128,2,16,128]{3,2,1,0:T(8,128)(2,1)S(1)} %bitcast.60), channel_id=1, replica_groups=mesh['x'=4,'zl'=2,'core'=2,'zh'=2,'y'=4] {'x','zl','core','zh','y'}, dimensions={0} | all-to-all | bytes 2097152 | tf_op jit(solution)/shard_map/all_to_all | solution.py:442
  196.4 3.7 %triangle.1 = bf16[128,16,128]{2,1,0:T(8,128)(2,1)} custom-call(bf16[128,2,16,128]{3,2,1,0:T(8,128)(2,1)S(1)} %all_to_all.32.in_ref), custom_call_target="tpu_custom_call" | custom-call | tf_op jit(solution)/shard_map/triangle/pallas_call | solution.py:324
  200.2 4.8 %all-to-all-start.5 = ((bf16[128,16,128]{2,1,0:T(8,128)(2,1)}), bf16[128,16,128]{2,1,0:T(8,128)(2,1)S(1)}, u32[]{:S(2)}, u32[]{:S(2)}) async-start(bf16[128,16,128]{2,1,0:T(8,128)(2,1)} %triangle.1), calls=%async_computation.5 | async-start | bytes 1048576 | tf_op jit(solution)/shard_map/all_to_all | solution.py:443
  205.0 0.1 copy.52
  205.1 13.8 %all-to-all-done.5 = bf16[128,16,128]{2,1,0:T(8,128)(2,1)S(1)} async-done(((bf16[128,16,128]{2,1,0:T(8,128)(2,1)}), bf16[128,16,128]{2,1,0:T(8,128)(2,1)S(1)}, u32[]{:S(2)}, u32[]{:S(2)}) %all-to-all-start.5) | async-done | bytes 524320 | tf_op jit(solution)/shard_map/all_to_all | solution.py:443
  219.0 0.1 copy.63
  219.1 2.6 %pair_final.1 = bf16[32,64,128]{2,1,0:T(8,128)(2,1)} custom-call(bf16[16,128,128]{2,1,0:T(8,128)(2,1)S(1)} %bitcast.50, bf16[32,64,128]{2,1,0:T(8,128)(2,1)S(1)} %bitcast.52, bf16[128,128]{1,0:T(8,128)(2,1)S(1)} %bitcast.54, bf16[128,128]{1,0:T(8,128)(2,1)S(1)} %copy-done.4), custom_call_target="tpu_custom_call" | custom-call | tf_op jit(solution)/shard_map/pair_final/pallas_call | solution.py:350
  221.7 2.5 %copy.65 = bf16[80,32,256]{2,1,0:T(8,128)(2,1)} copy(bf16[80,32,256]{2,1,0:T(8,128)(2,1)} %bitcast.20) | data formatting | bytes 2621440
  (20 shorter events, 0.1 us)
Async XLA Ops:
  0.6 1.0 copy-start
  1.7 0.7 copy-start.5
  22.2 34.3 %copy-start.9 = (s32[640]{0:T(1024)S(1)}, s32[640]{0:T(1024)}, u32[]{:S(2)}) copy-start(s32[640]{0:T(1024)} %param.15) | copy-start | bytes 7684
  22.2 34.3 %copy-start.10 = (s32[512]{0:T(512)S(1)}, s32[512]{0:T(512)}, u32[]{:S(2)}) copy-start(s32[512]{0:T(512)} %param.14) | copy-start | bytes 6148
  22.2 34.3 %copy-start.7 = (bf16[256,2,32]{0,2,1:T(8,128)(2,1)S(1)}, bf16[256,2,32]{0,2,1:T(8,128)(2,1)}, u32[]{:S(2)}) copy-start(bf16[256,2,32]{0,2,1:T(8,128)(2,1)} %param.19) | copy-start | bytes 98308
  22.2 36.7 %all-to-all-start.1 = ((bf16[16,5,32,256]{3,2,1,0:T(8,128)(2,1)}), bf16[16,5,32,256]{3,2,1,0:T(8,128)(2,1)}, u32[]{:S(2)}, u32[]{:S(2)}) async-start(bf16[16,5,32,256]{3,2,1,0:T(8,128)(2,1)} %bitcast.4), calls=%async_computation.1 | async-start | bytes 2621440 | tf_op jit(solution)/shard_map/all_to_all | solution.py:397
  28.4 30.7 %copy-start.3 = (bf16[256,256]{1,0:T(8,128)(2,1)S(1)}, bf16[256,256]{1,0:T(8,128)(2,1)}, u32[]{:S(2)}) copy-start(bf16[256,256]{1,0:T(8,128)(2,1)} %wo_ref.1) | copy-start | bytes 393220
  28.4 14.8 %collective-permute-start = (bf16[16,128,128]{2,1,0:T(8,128)(2,1)S(1)}, bf16[16,128,128]{2,1,0:T(8,128)(2,1)S(1)}, u32[]{:S(2)}, u32[]{:S(2)}) collective-permute-start(bf16[16,128,128]{2,1,0:T(8,128)(2,1)S(1)} %all_to_all.30.own0_ref), channel_id=1, source_target_pairs={{0,1},{1,2},{2,3},{3,0},{4,5},{5,6},{6,7},{7,4},{8,9},{9,10},{10,1... | collective-permute-start | bytes 1572872 | tf_op jit(solution)/shard_map/ppermute | solution.py:391
  29.7 25.6 %collective-permute-start.1 = (bf16[16,128,128]{2,1,0:T(8,128)(2,1)S(1)}, bf16[16,128,128]{2,1,0:T(8,128)(2,1)S(1)}, u32[]{:S(2)}, u32[]{:S(2)}) collective-permute-start(bf16[16,128,128]{2,1,0:T(8,128)(2,1)S(1)} %all_to_all.30.own0_ref), channel_id=1, source_target_pairs={{0,2},{1,3},{2,0},{3,1},{4,6},{5,7},{6,4},{7,5},{8,10},{9,11},{10,... | collective-permute-start | bytes 1572872 | tf_op jit(solution)/shard_map/ppermute | solution.py:391
  32.4 24.1 %collective-permute-start.2 = (bf16[16,128,128]{2,1,0:T(8,128)(2,1)S(1)}, bf16[16,128,128]{2,1,0:T(8,128)(2,1)S(1)}, u32[]{:S(2)}, u32[]{:S(2)}) collective-permute-start(bf16[16,128,128]{2,1,0:T(8,128)(2,1)S(1)} %all_to_all.30.own0_ref), channel_id=1, source_target_pairs={{0,3},{1,0},{2,1},{3,2},{4,7},{5,4},{6,5},{7,6},{8,11},{9,8},{10,9... | collective-permute-start | bytes 1572872 | tf_op jit(solution)/shard_map/ppermute | solution.py:391
  33.4 24.5 %collective-permute-start.3 = (bf16[16,128,128]{2,1,0:T(8,128)(2,1)S(1)}, bf16[16,128,128]{2,1,0:T(8,128)(2,1)S(1)}, u32[]{:S(2)}, u32[]{:S(2)}) collective-permute-start(bf16[16,128,128]{2,1,0:T(8,128)(2,1)S(1)} %all_to_all.30.own0_ref), channel_id=1, source_target_pairs={{0,8},{8,0},{1,9},{9,1},{2,10},{10,2},{3,11},{11,3},{4,12},{12,4},... | collective-permute-start | bytes 1572872 | tf_op jit(solution)/shard_map/ppermute | solution.py:393
  43.1 14.8 %collective-permute-start.4 = (bf16[16,128,128]{2,1,0:T(8,128)(2,1)S(1)}, bf16[16,128,128]{2,1,0:T(8,128)(2,1)}, u32[]{:S(2)}, u32[]{:S(2)}) collective-permute-start(bf16[16,128,128]{2,1,0:T(8,128)(2,1)S(1)} %collective-permute-done.own1_ref), channel_id=1, source_target_pairs={{0,8},{8,0},{1,9},{9,1},{2,10},{10,2},{3,11},{11,3},{4,12},{12,4},... | collective-permute-start | bytes 1572872 | tf_op jit(solution)/shard_map/ppermute | solution.py:393
  55.4 2.8 %collective-permute-start.5 = (bf16[16,128,128]{2,1,0:T(8,128)(2,1)S(1)}, bf16[16,128,128]{2,1,0:T(8,128)(2,1)}, u32[]{:S(2)}, u32[]{:S(2)}) collective-permute-start(bf16[16,128,128]{2,1,0:T(8,128)(2,1)S(1)} %collective-permute-done.1.own2_ref), channel_id=1, source_target_pairs={{0,8},{8,0},{1,9},{9,1},{2,10},{10,2},{3,11},{11,3},{4,12},{12,4},... | collective-permute-start | bytes 1572872 | tf_op jit(solution)/shard_map/ppermute | solution.py:393
  56.5 2.4 %collective-permute-start.6 = (bf16[16,128,128]{2,1,0:T(8,128)(2,1)S(1)}, bf16[16,128,128]{2,1,0:T(8,128)(2,1)}, u32[]{:S(2)}, u32[]{:S(2)}) collective-permute-start(bf16[16,128,128]{2,1,0:T(8,128)(2,1)S(1)} %collective-permute-done.2.own3_ref), channel_id=1, source_target_pairs={{0,8},{8,0},{1,9},{9,1},{2,10},{10,2},{3,11},{11,3},{4,12},{12,4},... | collective-permute-start | bytes 1572872 | tf_op jit(solution)/shard_map/ppermute | solution.py:393
  144.6 6.6 %copy-start.6 = (bf16[1024,128]{1,0:T(8,128)(2,1)S(1)}, bf16[1024,128]{1,0:T(8,128)(2,1)}, u32[]{:S(2)}) copy-start(bf16[1024,128]{1,0:T(8,128)(2,1)} %param.20) | copy-start | bytes 786436
  144.7 10.9 %collective-permute-start.7 = (bf16[640,1024]{1,0:T(8,128)(2,1)S(1)}, bf16[640,1024]{1,0:T(8,128)(2,1)S(1)}, u32[]{:S(2)}, u32[]{:S(2)}) collective-permute-start(bf16[640,1024]{1,0:T(8,128)(2,1)S(1)} %bitcast.45), channel_id=1, source_target_pairs={{0,8},{8,0},{1,9},{9,1},{2,10},{10,2},{3,11},{11,3},{4,12},{12,4},... | collective-permute-start | bytes 3932168 | tf_op jit(solution)/shard_map/ppermute | solution.py:416
  146.3 24.0 %all-to-all-start.3 = ((bf16[16,5,32,256]{3,2,1,0:T(8,128)(2,1)}), bf16[16,5,32,256]{3,2,1,0:T(8,128)(2,1)}, u32[]{:S(2)}, u32[]{:S(2)}) async-start(bf16[16,5,32,256]{3,2,1,0:T(8,128)(2,1)} %get-tuple-element.16), calls=%async_computation.3 | async-start | bytes 2621440 | tf_op jit(solution)/shard_map/all_to_all | solution.py:418
  153.8 1.8 copy-start.1
  169.3 1.0 copy-start.2
  196.4 8.6 %copy-start.8 = (bf16[128,128]{1,0:T(8,128)(2,1)S(1)}, bf16[128,128]{1,0:T(8,128)(2,1)}, u32[]{:S(2)}) copy-start(bf16[128,128]{1,0:T(8,128)(2,1)} %param.23) | copy-start | bytes 98308
  200.2 18.9 %copy-start.4 = (bf16[128,128]{1,0:T(8,128)(2,1)S(1)}, bf16[128,128]{1,0:T(8,128)(2,1)}, u32[]{:S(2)}) copy-start(bf16[128,128]{1,0:T(8,128)(2,1)} %wg_ref.1) | copy-start | bytes 98308
  200.2 18.8 %all-to-all-start.5 = ((bf16[128,16,128]{2,1,0:T(8,128)(2,1)}), bf16[128,16,128]{2,1,0:T(8,128)(2,1)S(1)}, u32[]{:S(2)}, u32[]{:S(2)}) async-start(bf16[128,16,128]{2,1,0:T(8,128)(2,1)} %triangle.1), calls=%async_computation.5 | async-start | bytes 1048576 | tf_op jit(solution)/shard_map/all_to_all | solution.py:443

commit v3 on v2

--- a/solution.py
+++ b/solution.py
@@ -7,6 +7,7 @@
 
 EPS = 1e-05
 BIG = 1000000000.0
+LOG2E = 1.4426950408889634
 F32 = jnp.float32
 BF16 = jnp.bfloat16
 ROW = ("x", "zl", "core")
@@ -42,24 +43,60 @@
     return pltpu.CompilerParams(vmem_limit_bytes=mib * MB)
 
 
-def bias_kernel(pair_ref, weight_ref, out_ref):
-    heads = weight_ref.shape[0]
-    for u in range(16):
-        block = jnp.concatenate([pair_ref[u], pair_ref[16 + u]], axis=0)
-        normed = layer_norm(block).astype(BF16)
-        out_ref[:, u, :] = lax.dot_general(
-            weight_ref[...], normed, NT, preferred_element_type=F32
-        ).astype(out_ref.dtype)
+def bias_kernel(pair_ref, weight_ref, out_ref, normed_ref, bias_ref):
+    normed_ref[...] = layer_norm(pair_ref[...])
+    for w in range(16):
+        block = jnp.concatenate([normed_ref[:, jq * 16 + w, :] for jq in range(4)], axis=0)
+        bias_ref[:, w, :] = lax.dot_general(
+            weight_ref[...], block.astype(BF16), NT, preferred_element_type=F32
+        )
+    for core in range(2):
+        chunk = bias_ref[4 * core : 4 * core + 4].reshape(64, 128).astype(BF16)
+        for xz in range(8):
+            for zh in range(2):
+                out_ref[xz, core, zh] = chunk
 
 
 def pair_bias(pairwise, weight):
-    heads = weight.shape[0]
     return pl.pallas_call(
         bias_kernel,
-        out_shape=jax.ShapeDtypeStruct((heads, 16, 128), F32),
+        out_shape=jax.ShapeDtypeStruct((8, 2, 2, 64, 128), BF16),
+        scratch_shapes=[pltpu.VMEM((32, 64, 128), F32), pltpu.VMEM((8, 16, 128), F32)],
         compiler_params=params(16),
         name="pair_bias",
     )(pairwise, weight)
+
+
+def plane_kernel(in_ref, out_ref):
+    group = lax.broadcasted_iota(jnp.int32, (16, 128), 1) // 32
+    for zh in range(2):
+        for hh in range(4):
+            for x in range(4):
+                parts = [
+                    in_ref[(x * 4 + g) * 2 + zh, 16 * hh : 16 * hh + 16, :].astype(F32)
+                    for g in range(4)
+                ]
+                for jq in range(4):
+                    turned = [
+                        part if g == jq else pltpu.roll(part, 32 * ((g - jq) % 4), 1)
+                        for g, part in enumerate(parts)
+                    ]
+                    row = jnp.where(
+                        group < 2,
+                        jnp.where(group == 0, turned[0], turned[1]),
+                        jnp.where(group == 2, turned[2], turned[3]),
+                    )
+                    base = 64 * zh + 16 * jq
+                    out_ref[hh, base : base + 16, 128 * x : 128 * x + 128] = row.astype(BF16)
+
+
+def plane(blocks):
+    return pl.pallas_call(
+        plane_kernel,
+        out_shape=jax.ShapeDtypeStruct((4, 128, 512), BF16),
+        compiler_params=params(8),
+        name="bias_plane",
+    )(blocks)
 
 
 def attention_kernel(
@@ -83,82 +120,56 @@
     out_ref,
     factor_ref,
     bias_ref,
-    q_ref,
+    qt_ref,
     k_ref,
-    v_ref,
+    vt_ref,
     acc_ref,
-    penalty_ref,
 ):
     heads = bias_ref.shape[0]
     step = pl.program_id(0)
 
     @pl.when(step == 0)
     def _():
-        penalty = (live_ref[...] - 1.0) * BIG
+        core, y = place_ref[0], place_ref[1]
         own = (own0_ref, own1_ref, own2_ref, own3_ref)
         other = (other0_ref, other1_ref, other2_ref, other3_ref)
-        core, y = place_ref[0], place_ref[1]
-
-        def assemble(pairs):
-            def at_chips(xz, carry):
-                for refs, side in ((own, core), (other, 1 - core)):
-                    base = pl.multiple_of((xz * 2 + side) * 32, 32)
-                    for even_at, odd_at in pairs:
-                        y_even = lax.rem(y + 4 - even_at, 4)
-                        for zh in range(2):
-                            lanes = pl.ds(pl.multiple_of((zh * 2 + y_even // 2) * 128, 128), 128)
-                            pen = penalty_ref[:, lanes]
-                            for h in range(heads):
-                                rows = slice(16 * h, 16 * h + 16)
-                                low, high = mix(
-                                    refs[even_at][xz * 2 + zh, rows, :].astype(F32),
-                                    refs[odd_at][xz * 2 + zh, rows, :].astype(F32),
-                                )
-                                bias_ref[h, pl.ds(base, 16), lanes] = low + pen
-                                bias_ref[h, pl.ds(base + 16, 16), lanes] = high + pen
-                return carry
-
-            lax.fori_loop(0, 8, at_chips, 0)
-
-        penalty_ref[...] = penalty
-
-        @pl.when(lax.rem(y, 2) == 0)
-        def _():
-            assemble(((0, 3), (2, 1)))
-
-        @pl.when(lax.rem(y, 2) == 1)
-        def _():
-            assemble(((1, 0), (3, 2)))
+        for refs, side in ((own, core), (other, 1 - core)):
+            for d in range(4):
+                source = lax.rem(y + 4 - d, 4)
+                for zh in range(2):
+                    rows = pl.ds(pl.multiple_of(256 * zh + 64 * source, 64), 64)
+                    penalty = (live_col_ref[rows, :] - 1.0) * BIG
+                    for m in range(4):
+                        lanes = slice(128 * m, 128 * m + 128)
+                        for hh in range(4):
+                            bias_ref[4 * side + hh, rows, lanes] = (
+                                refs[d][hh, 64 * zh : 64 * zh + 64, lanes].astype(F32) * LOG2E
+                                + penalty
+                            )
 
     x = x_ref[:, 0].reshape(512, 256)
     normed = layer_norm(x).astype(BF16)
 
     def project(t):
-        return jnp.dot(normed, win_ref[:, 256 * t : 256 * t + 256], preferred_element_type=F32)
-
-    q_ref[...] = (project(0) * 32 ** (-0.5)).astype(BF16)
-    k_ref[...] = project(1).astype(BF16)
-    v_ref[...] = project(2).astype(BF16)
-    acc_ref[...] = jnp.zeros_like(acc_ref)
-    lane_head = lax.broadcasted_iota(jnp.int32, (512, 256), 1) // 32
-
-    def head(h, carry):
-        mine = lane_head == h
-        k_h = jnp.where(mine, k_ref[...], jnp.zeros((), BF16))
-        v_h = jnp.where(mine, v_ref[...], jnp.zeros((), BF16))
-        for t in range(2):
-            rows = slice(256 * t, 256 * t + 256)
-            s = lax.dot_general(q_ref[rows], k_h, NT, preferred_element_type=F32)
-            s = s + bias_ref[h, rows, :]
-            p = jnp.exp(s - jnp.max(s, axis=-1, keepdims=True))
-            total = jnp.sum(p, axis=-1, keepdims=True)
-            o = jnp.dot(p.astype(BF16), v_h, preferred_element_type=F32)
-            acc_ref[rows] += o * (1.0 / total)
-        return carry
-
-    lax.fori_loop(0, heads, head, 0)
-    gate = jax.nn.sigmoid(project(3))
-    attended = (acc_ref[...] * gate).astype(BF16)
+        return lax.dot_general(
+            win_ref[256 * t : 256 * t + 256], normed, NT, preferred_element_type=F32
+        )
+
+    qt_ref[...] = (project(0) * (32 ** (-0.5) * LOG2E)).astype(BF16)
+    k_ref[...] = lax.dot_general(
+        normed, win_ref[256:512], NT, preferred_element_type=F32
+    ).astype(BF16)
+    vt_ref[:, :32] = project(2).astype(BF16).reshape(heads, 32, 512)
+    vt_ref[:, 32:] = jnp.ones((heads, 16, 512), BF16)
+    row_head = lax.broadcasted_iota(jnp.int32, (128, 512), 0) // 32
+    for h in range(heads):
+        lanes = slice(128 * (h // 4), 128 * (h // 4) + 128)
+        q_h = jnp.where(row_head == h % 4, qt_ref[lanes, :], jnp.zeros((), BF16))
+        s = jnp.dot(k_ref[:, lanes], q_h, preferred_element_type=F32) + bias_ref[h]
+        p = jnp.exp2(s - jnp.max(s, axis=0, keepdims=True)).astype(BF16)
+        o = jnp.dot(vt_ref[h], p, preferred_element_type=F32)
+        acc_ref[32 * h : 32 * h + 32, :] = o[:32] / o[32:33]
+    attended = (acc_ref[...] * jax.nn.sigmoid(project(3))).T.astype(BF16)
     out = (
         x.astype(F32) + jnp.dot(attended, wo_ref[...], preferred_element_type=F32)
     ).astype(BF16)
@@ -219,30 +230,60 @@
         ],
         scratch_shapes=[
             pltpu.VMEM((8, 512, 512), F32),
+            pltpu.VMEM((256, 512), BF16),
             pltpu.VMEM((512, 256), BF16),
-            pltpu.VMEM((512, 256), BF16),
-            pltpu.VMEM((512, 256), BF16),
-            pltpu.VMEM((512, 256), F32),
-            pltpu.VMEM((1, 512), F32),
+            pltpu.VMEM((8, 48, 512), BF16),
+            pltpu.VMEM((256, 512), F32),
         ],
         compiler_params=params(48),
         name="row_attention",
     )(place, seq_live, *biases, x, win, wo, wl, wr, live, live_col)
 
 
-def outer_kernel(core_ref, l_ref, own_ref, other_ref, w_ref, inv_ref, plane_ref, pair_ref, wp_ref, mid_ref, tri_ref, x_ref):
-    for ref, core in ((own_ref, core_ref[0]), (other_ref, 1 - core_ref[0])):
-        product = lax.dot_general(l_ref[...], ref[...], TN, preferred_element_type=F32)
-        for half in range(2):
-            columns = slice(128 * half, 128 * half + 128)
-            for u in range(8):
-                first = product[32 * half : 32 * half + 32, 128 * u : 128 * u + 128]
-                second = product[32 * half + 64 : 32 * half + 96, 128 * u : 128 * u + 128]
-                low, high = mix(first, second)
-                base = pl.multiple_of(core * 512 + 64 * u, 64)
-                x_ref[pl.ds(base, 32), columns] = low.astype(BF16)
-                x_ref[pl.ds(base + 32, 32), columns] = high.astype(BF16)
-    update = jnp.dot(w_ref[...], x_ref[...], preferred_element_type=F32)
+def outer_kernel(
+    core_ref,
+    l_ref,
+    own_ref,
+    other_ref,
+    w_ref,
+    inv_ref,
+    plane_ref,
+    pair_ref,
+    wp_ref,
+    mid_ref,
+    tri_ref,
+    lt_ref,
+    x_ref,
+):
+    step = pl.program_id(0)
+
+    @pl.when(step == 0)
+    def _():
+        for v in range(8):
+            rows = slice(128 * v, 128 * v + 128)
+            lt_ref[rows, :] = l_ref[:, rows].astype(F32).T.astype(BF16)
+        for ref, core in ((own_ref, core_ref[0]), (other_ref, 1 - core_ref[0])):
+
+            def some(n, carry):
+                lanes = pl.ds(pl.multiple_of(n * 256, 256), 256)
+                product = jnp.dot(lt_ref[...], ref[:, lanes], preferred_element_type=F32)
+                for k in range(2):
+                    base = pl.multiple_of(core * 512 + n * 128 + 64 * k, 64)
+                    for v in range(8):
+                        for half in range(2):
+                            at = 128 * v + 32 * half
+                            low, high = mix(
+                                product[at : at + 32, 128 * k : 128 * k + 128],
+                                product[at + 64 : at + 96, 128 * k : 128 * k + 128],
+                            )
+                            columns = slice(128 * half, 128 * half + 128)
+                            x_ref[v, pl.ds(base, 32), columns] = low.astype(BF16)
+                            x_ref[v, pl.ds(base + 32, 32), columns] = high.astype(BF16)
+                return carry
+
+            lax.fori_loop(0, 4, some, 0)
+
+    update = jnp.dot(w_ref[...], x_ref[step], preferred_element_type=F32)
     for half in range(2):
         part = update[:, 128 * half : 128 * half + 128] * inv_ref[half, 0]
         before = jnp.concatenate([pair_ref[half, 0], pair_ref[half + 2, 0]], axis=0)
@@ -270,7 +311,7 @@
         grid=(8,),
         in_specs=[
             pl.BlockSpec(memory_space=pltpu.SMEM),
-            by_v(total, 128),
+            whole(left),
             whole(own),
             whole(other),
             whole(weight),
@@ -284,7 +325,7 @@
             jax.ShapeDtypeStruct((4, 8, 64, 128), BF16),
             jax.ShapeDtypeStruct((2, 8, 256, 128), BF16),
         ],
-        scratch_shapes=[pltpu.VMEM((1024, 256), BF16)],
+        scratch_shapes=[pltpu.VMEM((1024, total), BF16), pltpu.VMEM((8, 1024, 256), BF16)],
         compiler_params=params(32),
         name="outer_update",
     )(core, left, own, other, weight, inv, plane, pairwise, wp)
@@ -353,6 +394,19 @@
         compiler_params=params(16),
         name="pair_final",
     )(tri, mid, wt, wg)
+
+
+def copy_kernel(in_ref, out_ref):
+    out_ref[...] = in_ref[...]
+
+
+def copied(a):
+    return pl.pallas_call(
+        copy_kernel,
+        out_shape=jax.ShapeDtypeStruct(a.shape, a.dtype),
+        compiler_params=params(8),
+        name="copied",
+    )(a)
 
 
 def body(
@@ -379,28 +433,39 @@
     col_live = lax.dynamic_slice_in_dim(res_live, col * 64, 64)
     my_seqs = lax.dynamic_slice_in_dim(seq_live, col * 80 + row * 5, 5)
 
-    bias = pair_bias(pairwise, bias_project.T).astype(BF16).reshape(128, 128)
-    bias_plane = lax.all_to_all(
-        jnp.broadcast_to(bias, (16, 128, 128)),
-        ("x", "zl", "zh"),
+    blocks = lax.all_to_all(
+        pair_bias(pairwise, bias_project.T).reshape(32, 64, 128),
+        ROW + ("zh",),
         split_axis=0,
         concat_axis=0,
         tiled=True,
     )
+    outgoing, blocks = lax.optimization_barrier((alignment.reshape(16, 5, 32, 256), blocks))
+    bias_plane = plane(blocks)
     own = [bias_plane] + [
         lax.ppermute(bias_plane, "y", [(i, (i + d) % 4) for i in range(4)]) for d in (1, 2, 3)
     ]
     other = [lax.ppermute(b, "core", swap) for b in own]
-    outgoing, bias_plane = lax.optimization_barrier(
-        (alignment.reshape(16, 5, 32, 256), bias_plane)
-    )
     sequences = lax.all_to_all(outgoing, ROW, split_axis=0, concat_axis=0, tiled=True)
+    live_plane = row_live[:, None] * col_live[None, :]
+    inv = 1.0 / jnp.maximum(jnp.sum(seq_live) * live_plane, 1.0)
+
+    def pairs(a):
+        return a.reshape(2, 16, 64).transpose(1, 0, 2).reshape(2, 8, 1, 128)
+
+    weight = outer_output.reshape(32, 2, 16, 128).transpose(3, 2, 1, 0).reshape(128, 1024)
+    win = attention_input_weight.reshape(256, 1024).T
+    wp = tri_project.reshape(128, 512).T
+    wt = tri_output.T
+    sequences, weight, wp, wt, inv, live_plane, win = lax.optimization_barrier(
+        (sequences, weight, wp, wt, pairs(inv), pairs(live_plane), win)
+    )
     out_seq, factors = attention(
         jnp.stack([core, lax.axis_index("y")]),
         my_seqs,
         own + other,
         sequences,
-        attention_input_weight.reshape(256, 1024),
+        win,
         attention_output_weight,
         jnp.tile(outer_factor_weight[:, 0], (1, 4)),
         outer_factor_weight[:, 1].T,
@@ -419,30 +484,24 @@
         out_seq, ROW, split_axis=0, concat_axis=0, tiled=True
     ).reshape(80, 32, 256)
 
-    plane = row_live[:, None] * col_live[None, :]
-    inv = 1.0 / jnp.maximum(jnp.sum(seq_live) * plane, 1.0)
-
-    def pairs(a):
-        return a.reshape(2, 16, 64).transpose(1, 0, 2).reshape(2, 8, 1, 128)
-
-    weight = outer_output.reshape(32, 2, 16, 128).transpose(3, 2, 1, 0).reshape(128, 1024)
     mid, tri = outer_update(
         core.reshape(1),
         left,
         right_own,
         right_other,
         weight,
-        pairs(inv),
-        pairs(plane),
+        inv,
+        live_plane,
         pairwise.reshape(4, 8, 64, 128),
-        tri_project.reshape(128, 512).T,
+        wp,
     )
     tri, alignment_output = lax.optimization_barrier((tri, alignment_output))
+    alignment_output = copied(alignment_output)
     tri = tri.reshape(16, 2, 128, 128).transpose(2, 1, 0, 3)
     blocks = lax.all_to_all(tri, ALL, split_axis=0, concat_axis=0, tiled=True)
     combined = lax.all_to_all(triangle(blocks), ALL, split_axis=0, concat_axis=0, tiled=True)
     pair_output_state = final(
-        combined.transpose(1, 0, 2), mid.reshape(32, 64, 128), tri_output.T, tri_gate
+        combined.transpose(1, 0, 2), mid.reshape(32, 64, 128), wt, tri_gate
     )
     return (alignment_output, pair_output_state)
 

time: 225 us -> 213 us (0.947)
  Pallas kernels: 62.8 us -> 51.6 us
  starting transfers between devices: 25.1 us -> 21.9 us
    pallas_call x1, Pallas kernels: 41.7 us -> 27.3 us  [attention(): pl.pallas_call(attention_kernel, grid=(count,), in_specs=[smem, smem, *(w...]
    ppermute x3, waiting for transfers between devices: 19.9 us -> 23.2 us  [body(): lax.ppermute(bias_plane, 'y', [(i, (i + d) % 4) for i in range(4)])]
    unnamed x28 -> x31, local copies, waits for them, and re-layouts: 9.56 us -> 7.9 us
  transfers between devices with their start and end apart: 11 -> 11, of which waited for: 5 -> 4; matrix products, arithmetic and copies ran while one was open for 3% -> 4% of each run, Pallas kernels for 6% -> 8%
where the time goes in v3:
time: 213 us; the launch traced here: 212 us
  blocking collectives  85.5 us (40%)
  Pallas kernels  51.6 us (24%)
  waiting for transfers between devices  36.6 us (17%)
  starting transfers between devices  21.9 us (10%)
  local copies, waits for them, and re-layouts  14.5 us (7%)
    all_to_all x1, blocking collectives, body(): lax.all_to_all(factors.reshape(128, 80, 128), ALL, split_axis=0, concat_a...  40.9 us
    pallas_call x1, Pallas kernels, attention(): pl.pallas_call(attention_kernel, grid=(count,), in_specs=[smem, smem, *(w...  27.3 us
    all_to_all x1, blocking collectives, body(): blocks = lax.all_to_all(tri, ALL, split_axis=0, concat_axis=0, tiled=True)  23.7 us
    ppermute x3, waiting for transfers between devices, body(): lax.ppermute(bias_plane, 'y', [(i, (i + d) % 4) for i in range(4)])  23.2 us
    all_to_all x1, blocking collectives, body(): lax.all_to_all(pair_bias(pairwise, bias_project.T).reshape(32, 64, 128),...  20.9 us
    pallas_call x1, Pallas kernels, outer_update(): pl.pallas_call(outer_kernel, grid=(8,), in_specs=[pl.BlockSpec(memory_spa...  15 us
    all_to_all x1, waiting for transfers between devices, body(): lax.all_to_all(triangle(blocks), ALL, split_axis=0, concat_axis=0, tiled=...  12.8 us
    unnamed x31, local copies, waits for them, and re-layouts  7.9 us
  transfers between devices with their start and end apart: 11, of which 4 were waited for; matrix products, arithmetic and copies ran while one was open for 4% of the time, Pallas kernels for 8%

profile of v3, /device:TPU:1, one launch (start us, length us, event | category | flops | bytes accessed | tf_op | source)
XLA Modules:
  0.0 212.4 jit_solution(12697999582917771515)
XLA Ops:
  0.6 0.0 copy-start
  0.6 1.0 copy-done
  1.7 0.7 copy-done.6
  2.4 1.3 pair_bias.1
  3.7 20.9 %all_to_all.30.in_ref = bf16[32,64,128]{2,1,0:T(8,128)(2,1)S(1)} all-to-all(bf16[32,64,128]{2,1,0:T(8,128)(2,1)S(1)} %bitcast.52), channel_id=1, replica_groups=mesh['x'=4,'zl'=2,'core'=2,'zh'=2,'y'=4] {'x','zl','core','zh'}, dimensions={0} | all-to-all | bytes 1048576 | tf_op jit(solution)/shard_map/all_to_all | solution.py:436
  24.6 5.1 %all-to-all-start.1 = ((bf16[16,5,32,256]{3,2,1,0:T(8,128)(2,1)}), bf16[16,5,32,256]{3,2,1,0:T(8,128)(2,1)}, u32[]{:S(2)}, u32[]{:S(2)}) async-start(bf16[16,5,32,256]{3,2,1,0:T(8,128)(2,1)} %bitcast.2), calls=%async_computation.1 | async-start | bytes 2621440 | tf_op jit(solution)/shard_map/all_to_all | solution.py:449
  29.7 0.5 bias_plane.1.own0_ref
  30.2 0.0 copy-start.3
  30.2 2.8 %collective-permute-start.2 = (bf16[4,128,512]{2,1,0:T(8,128)(2,1)S(1)}, bf16[4,128,512]{2,1,0:T(8,128)(2,1)S(1)}, u32[]{:S(2)}, u32[]{:S(2)}) collective-permute-start(bf16[4,128,512]{2,1,0:T(8,128)(2,1)S(1)} %bias_plane.1.own0_ref), channel_id=1, source_target_pairs={{0,3},{1,0},{2,1},{3,2},{4,7},{5,4},{6,5},{7,6},{8,11},{9,8},{10,9... | collective-permute-start | bytes 1572872 | tf_op jit(solution)/shard_map/ppermute | solution.py:446
  33.0 0.3 collective-permute-start.1
  33.3 0.7 collective-permute-start
  34.0 1.1 collective-permute-start.3
  35.2 20.0 %collective-permute-done.2.own3_ref = bf16[4,128,512]{2,1,0:T(8,128)(2,1)S(1)} collective-permute-done((bf16[4,128,512]{2,1,0:T(8,128)(2,1)S(1)}, bf16[4,128,512]{2,1,0:T(8,128)(2,1)S(1)}, u32[]{:S(2)}, u32[]{:S(2)}) %collective-permute-start.2) | collective-permute-done | bytes 524320 | tf_op jit(solution)/shard_map/ppermute | solution.py:446
  55.1 1.2 collective-permute-start.6
  56.4 0.0 collective-permute-done.1.own2_ref
  56.4 0.0 collective-permute-start.5
  56.4 3.2 %collective-permute-done.own1_ref = bf16[4,128,512]{2,1,0:T(8,128)(2,1)S(1)} collective-permute-done((bf16[4,128,512]{2,1,0:T(8,128)(2,1)S(1)}, bf16[4,128,512]{2,1,0:T(8,128)(2,1)S(1)}, u32[]{:S(2)}, u32[]{:S(2)}) %collective-permute-start) | collective-permute-done | bytes 524320 | tf_op jit(solution)/shard_map/ppermute | solution.py:446
  59.6 0.5 collective-permute-start.4
  60.1 0.1 dynamic_slice.11
  60.2 0.1 dynamic_slice.10
  60.3 0.1 mul.76
  60.3 0.6 mul.82
  61.0 0.1 copy.41
  61.0 0.1 mul.78
  61.1 0.1 mul.79
  61.2 0.0 copy-done.9
  61.2 0.7 copy.40
  61.9 0.1 copy.43.wl_ref
  62.1 1.0 copy.39
  63.1 1.8 copy.38
  64.9 1.3 copy.42
  66.2 0.1 dynamic_slice.9.seq_ref
  66.3 0.1 pad_add_fusion.place_ref
  66.3 0.6 convert_reduce_fusion
  66.9 0.7 maximum_divide_fusion
  67.6 0.0 all-to-all-done.1.x_ref
  67.6 0.0 collective-permute-done.3.other0_ref
  67.6 0.0 collective-permute-done.6.other3_ref
  67.6 0.0 collective-permute-done.5.other2_ref
  67.7 0.0 collective-permute-done.4.other1_ref
  67.7 0.1 broadcast_in_dim.2.live_col_ref
  67.8 27.3 %row_attention.1 = (bf16[16,5,32,256]{3,2,1,0:T(8,128)(2,1)}, bf16[8,2,8,5,16,128]{5,4,3,2,1,0:T(8,128)(2,1)}) custom-call(s32[2]{0:T(128)S(1)} %pad_add_fusion.place_ref, f32[5]{0:T(128)S(1)} %dynamic_slice.9.seq_ref, bf16[4,128,512]{2,1,0:T(8,128)(2,1)S(1)} %bias_plane.1.own0_ref, bf16[4,128,512]{2,1,0:T(8,128)(2,1)S(1)} %collective-permute-done.own1_ref, ...), custom_call_target="tpu_custom_call" | custom-call | tf_op jit(solution)/shard_map/row_attention/pallas_call | solution.py:208
  95.1 40.9 %all_to_all.31 = bf16[128,80,128]{2,1,0:T(8,128)(2,1)S(1)} all-to-all(bf16[128,80,128]{2,1,0:T(8,128)(2,1)} %bitcast.63), channel_id=1, replica_groups=mesh['x'=4,'zl'=2,'core'=2,'zh'=2,'y'=4] {'x','zl','core','zh','y'}, dimensions={0} | all-to-all | bytes 5242880 | tf_op jit(solution)/shard_map/all_to_all | solution.py:475
  136.0 1.2 fusion
  137.3 0.4 copy.53
  137.6 0.0 copy-start.7
  137.7 1.6 collective-permute-start.7
  139.3 3.8 %all-to-all-start.3 = ((bf16[16,5,32,256]{3,2,1,0:T(8,128)(2,1)}), bf16[16,5,32,256]{3,2,1,0:T(8,128)(2,1)S(1)}, u32[]{:S(2)}, u32[]{:S(2)}) async-start(bf16[16,5,32,256]{3,2,1,0:T(8,128)(2,1)} %get-tuple-element.31), calls=%async_computation.3 | async-start | bytes 2621440 | tf_op jit(solution)/shard_map/all_to_all | solution.py:483
  143.1 0.1 copy.44.w_ref
  143.3 0.0 copy-start.1
  143.3 1.7 copy.54
  145.0 0.0 collective-permute-done.7.other_ref
  145.0 15.0 %outer_update.1 = (bf16[4,8,64,128]{3,2,1,0:T(8,128)(2,1)S(1)}, bf16[2,8,256,128]{3,2,1,0:T(8,128)(2,1)S(1)}) custom-call(s32[1]{0:T(128)} %bitcast.core_ref, bf16[640,1024]{1,0:T(8,128)(2,1)S(1)} %bitcast.47, bf16[640,1024]{1,0:T(8,128)(2,1)S(1)} %bitcast.46, bf16[640,1024]{1,0:T(8,128)(2,1)} %collective-permute-done.7.other_ref, ...), custom_call_target="tpu_custom_call" | custom-call | tf_op jit(solution)/shard_map/outer_update/pallas_call | solution.py:309
  160.0 1.0 copy-done.2
  161.0 0.6 all-to-all-done.3
  161.6 1.9 copy.55
  163.5 23.7 %all_to_all.32.in_ref = bf16[128,2,16,128]{3,2,1,0:T(8,128)(2,1)S(1)} all-to-all(bf16[128,2,16,128]{3,2,1,0:T(8,128)(2,1)S(1)} %bitcast.62), channel_id=1, replica_groups=mesh['x'=4,'zl'=2,'core'=2,'zh'=2,'y'=4] {'x','zl','core','zh','y'}, dimensions={0} | all-to-all | bytes 2097152 | tf_op jit(solution)/shard_map/all_to_all | solution.py:501
  187.2 3.7 %triangle.1 = bf16[128,16,128]{2,1,0:T(8,128)(2,1)} custom-call(bf16[128,2,16,128]{3,2,1,0:T(8,128)(2,1)S(1)} %all_to_all.32.in_ref), custom_call_target="tpu_custom_call" | custom-call | tf_op jit(solution)/shard_map/triangle/pallas_call | solution.py:365
  190.9 4.7 %all-to-all-start.5 = ((bf16[128,16,128]{2,1,0:T(8,128)(2,1)}), bf16[128,16,128]{2,1,0:T(8,128)(2,1)S(1)}, u32[]{:S(2)}, u32[]{:S(2)}) async-start(bf16[128,16,128]{2,1,0:T(8,128)(2,1)} %triangle.1), calls=%async_computation.5 | async-start | bytes 1048576 | tf_op jit(solution)/shard_map/all_to_all | solution.py:502
  195.7 0.0 copy-start.5
  195.7 1.1 copied.1
  196.8 12.8 %all-to-all-done.5 = bf16[128,16,128]{2,1,0:T(8,128)(2,1)S(1)} async-done(((bf16[128,16,128]{2,1,0:T(8,128)(2,1)}), bf16[128,16,128]{2,1,0:T(8,128)(2,1)S(1)}, u32[]{:S(2)}, u32[]{:S(2)}) %all-to-all-start.5) | async-done | bytes 524320 | tf_op jit(solution)/shard_map/all_to_all | solution.py:502
  209.6 0.1 copy.56
  209.8 2.6 %pair_final.1 = bf16[32,64,128]{2,1,0:T(8,128)(2,1)} custom-call(bf16[16,128,128]{2,1,0:T(8,128)(2,1)S(1)} %bitcast.51, bf16[32,64,128]{2,1,0:T(8,128)(2,1)S(1)} %bitcast.54, bf16[128,128]{1,0:T(8,128)(2,1)S(1)} %bitcast.56, bf16[128,128]{1,0:T(8,128)(2,1)S(1)} %copy-done.5), custom_call_target="tpu_custom_call" | custom-call | tf_op jit(solution)/shard_map/pair_final/pallas_call | solution.py:391
  (22 shorter events, 0.0 us)
Async XLA Ops:
  0.6 1.0 copy-start
  1.7 0.7 copy-start.6
  24.6 35.5 %copy-start.8 = (bf16[256,2,32]{0,2,1:T(8,128)(2,1)S(1)}, bf16[256,2,32]{0,2,1:T(8,128)(2,1)}, u32[]{:S(2)}) copy-start(bf16[256,2,32]{0,2,1:T(8,128)(2,1)} %param.19) | copy-start | bytes 98308
  24.6 35.5 %copy-start.11 = (s32[512]{0:T(512)S(1)}, s32[512]{0:T(512)}, u32[]{:S(2)}) copy-start(s32[512]{0:T(512)} %param.14) | copy-start | bytes 6148
  24.6 36.4 %copy-start.10 = (s32[640]{0:T(1024)S(1)}, s32[640]{0:T(1024)}, u32[]{:S(2)}) copy-start(s32[640]{0:T(1024)} %param.15) | copy-start | bytes 7684
  24.6 36.6 %copy-start.9 = (bf16[128,128]{1,0:T(8,128)(2,1)S(1)}, bf16[128,128]{1,0:T(8,128)(2,1)}, u32[]{:S(2)}) copy-start(bf16[128,128]{1,0:T(8,128)(2,1)} %param.23) | copy-start | bytes 98308
  24.6 43.0 %all-to-all-start.1 = ((bf16[16,5,32,256]{3,2,1,0:T(8,128)(2,1)}), bf16[16,5,32,256]{3,2,1,0:T(8,128)(2,1)}, u32[]{:S(2)}, u32[]{:S(2)}) async-start(bf16[16,5,32,256]{3,2,1,0:T(8,128)(2,1)} %bitcast.2), calls=%async_computation.1 | async-start | bytes 2621440 | tf_op jit(solution)/shard_map/all_to_all | solution.py:449
  30.2 37.6 %copy-start.3 = (bf16[256,256]{1,0:T(8,128)(2,1)S(1)}, bf16[256,256]{1,0:T(8,128)(2,1)}, u32[]{:S(2)}) copy-start(bf16[256,256]{1,0:T(8,128)(2,1)} %wo_ref.1) | copy-start | bytes 393220
  30.2 24.9 %collective-permute-start.2 = (bf16[4,128,512]{2,1,0:T(8,128)(2,1)S(1)}, bf16[4,128,512]{2,1,0:T(8,128)(2,1)S(1)}, u32[]{:S(2)}, u32[]{:S(2)}) collective-permute-start(bf16[4,128,512]{2,1,0:T(8,128)(2,1)S(1)} %bias_plane.1.own0_ref), channel_id=1, source_target_pairs={{0,3},{1,0},{2,1},{3,2},{4,7},{5,4},{6,5},{7,6},{8,11},{9,8},{10,9... | collective-permute-start | bytes 1572872 | tf_op jit(solution)/shard_map/ppermute | solution.py:446
  33.0 23.4 %collective-permute-start.1 = (bf16[4,128,512]{2,1,0:T(8,128)(2,1)S(1)}, bf16[4,128,512]{2,1,0:T(8,128)(2,1)S(1)}, u32[]{:S(2)}, u32[]{:S(2)}) collective-permute-start(bf16[4,128,512]{2,1,0:T(8,128)(2,1)S(1)} %bias_plane.1.own0_ref), channel_id=1, source_target_pairs={{0,2},{1,3},{2,0},{3,1},{4,6},{5,7},{6,4},{7,5},{8,10},{9,11},{10,... | collective-permute-start | bytes 1572872 | tf_op jit(solution)/shard_map/ppermute | solution.py:446
  33.3 26.2 %collective-permute-start = (bf16[4,128,512]{2,1,0:T(8,128)(2,1)S(1)}, bf16[4,128,512]{2,1,0:T(8,128)(2,1)S(1)}, u32[]{:S(2)}, u32[]{:S(2)}) collective-permute-start(bf16[4,128,512]{2,1,0:T(8,128)(2,1)S(1)} %bias_plane.1.own0_ref), channel_id=1, source_target_pairs={{0,1},{1,2},{2,3},{3,0},{4,5},{5,6},{6,7},{7,4},{8,9},{9,10},{10,1... | collective-permute-start | bytes 1572872 | tf_op jit(solution)/shard_map/ppermute | solution.py:446
  34.0 33.6 %collective-permute-start.3 = (bf16[4,128,512]{2,1,0:T(8,128)(2,1)S(1)}, bf16[4,128,512]{2,1,0:T(8,128)(2,1)S(1)}, u32[]{:S(2)}, u32[]{:S(2)}) collective-permute-start(bf16[4,128,512]{2,1,0:T(8,128)(2,1)S(1)} %bias_plane.1.own0_ref), channel_id=1, source_target_pairs={{0,8},{8,0},{1,9},{9,1},{2,10},{10,2},{3,11},{11,3},{4,12},{12,4},... | collective-permute-start | bytes 1572872 | tf_op jit(solution)/shard_map/ppermute | solution.py:448
  55.1 12.5 %collective-permute-start.6 = (bf16[4,128,512]{2,1,0:T(8,128)(2,1)S(1)}, bf16[4,128,512]{2,1,0:T(8,128)(2,1)}, u32[]{:S(2)}, u32[]{:S(2)}) collective-permute-start(bf16[4,128,512]{2,1,0:T(8,128)(2,1)S(1)} %collective-permute-done.2.own3_ref), channel_id=1, source_target_pairs={{0,8},{8,0},{1,9},{9,1},{2,10},{10,2},{3,11},{11,3},{4,12},{12,4},... | collective-permute-start | bytes 1572872 | tf_op jit(solution)/shard_map/ppermute | solution.py:448
  56.4 11.3 %collective-permute-start.5 = (bf16[4,128,512]{2,1,0:T(8,128)(2,1)S(1)}, bf16[4,128,512]{2,1,0:T(8,128)(2,1)}, u32[]{:S(2)}, u32[]{:S(2)}) collective-permute-start(bf16[4,128,512]{2,1,0:T(8,128)(2,1)S(1)} %collective-permute-done.1.own2_ref), channel_id=1, source_target_pairs={{0,8},{8,0},{1,9},{9,1},{2,10},{10,2},{3,11},{11,3},{4,12},{12,4},... | collective-permute-start | bytes 1572872 | tf_op jit(solution)/shard_map/ppermute | solution.py:448
  59.6 8.1 %collective-permute-start.4 = (bf16[4,128,512]{2,1,0:T(8,128)(2,1)S(1)}, bf16[4,128,512]{2,1,0:T(8,128)(2,1)}, u32[]{:S(2)}, u32[]{:S(2)}) collective-permute-start(bf16[4,128,512]{2,1,0:T(8,128)(2,1)S(1)} %collective-permute-done.own1_ref), channel_id=1, source_target_pairs={{0,8},{8,0},{1,9},{9,1},{2,10},{10,2},{3,11},{11,3},{4,12},{12,4},... | collective-permute-start | bytes 1572872 | tf_op jit(solution)/shard_map/ppermute | solution.py:448
  61.9 5.0 %copy-start.12 = (f32[128]{0:T(128)S(1)}, f32[128]{0:T(128)}, u32[]{:S(2)}) copy-start(f32[128]{0:T(128)} %mul.82) | copy-start | bytes 1540
  137.6 5.4 %copy-start.7 = (bf16[128,16,2,32]{0,3,2,1:T(8,128)(2,1)S(1)}, bf16[128,16,2,32]{0,3,2,1:T(8,128)(2,1)}, u32[]{:S(2)}) copy-start(bf16[128,16,2,32]{0,3,2,1:T(8,128)(2,1)} %copy.38) | copy-start | bytes 786436
  137.7 7.4 %collective-permute-start.7 = (bf16[640,1024]{1,0:T(8,128)(2,1)S(1)}, bf16[640,1024]{1,0:T(8,128)(2,1)}, u32[]{:S(2)}, u32[]{:S(2)}) collective-permute-start(bf16[640,1024]{1,0:T(8,128)(2,1)S(1)} %bitcast.45), channel_id=1, source_target_pairs={{0,8},{8,0},{1,9},{9,1},{2,10},{10,2},{3,11},{11,3},{4,12},{12,4},... | collective-permute-start | bytes 3932168 | tf_op jit(solution)/shard_map/ppermute | solution.py:481
  139.3 22.3 %all-to-all-start.3 = ((bf16[16,5,32,256]{3,2,1,0:T(8,128)(2,1)}), bf16[16,5,32,256]{3,2,1,0:T(8,128)(2,1)S(1)}, u32[]{:S(2)}, u32[]{:S(2)}) async-start(bf16[16,5,32,256]{3,2,1,0:T(8,128)(2,1)} %get-tuple-element.31), calls=%async_computation.3 | async-start | bytes 2621440 | tf_op jit(solution)/shard_map/all_to_all | solution.py:483
  143.3 1.8 copy-start.1
  160.0 1.0 copy-start.2
  190.9 18.7 %all-to-all-start.5 = ((bf16[128,16,128]{2,1,0:T(8,128)(2,1)}), bf16[128,16,128]{2,1,0:T(8,128)(2,1)S(1)}, u32[]{:S(2)}, u32[]{:S(2)}) async-start(bf16[128,16,128]{2,1,0:T(8,128)(2,1)} %triangle.1), calls=%async_computation.5 | async-start | bytes 1048576 | tf_op jit(solution)/shard_map/all_to_all | solution.py:502
  195.7 14.1 %copy-start.4 = (bf16[128,128]{0,1:T(8,128)(2,1)S(1)}, bf16[128,128]{0,1:T(8,128)(2,1)}, u32[]{:S(2)}) copy-start(bf16[128,128]{0,1:T(8,128)(2,1)} %copy.40) | copy-start | bytes 98308
  195.7 14.1 %copy-start.5 = (bf16[128,128]{1,0:T(8,128)(2,1)S(1)}, bf16[128,128]{1,0:T(8,128)(2,1)}, u32[]{:S(2)}) copy-start(bf16[128,128]{1,0:T(8,128)(2,1)} %wg_ref.1) | copy-start | bytes 98308

commit v4 on v3

--- a/solution.py
+++ b/solution.py
@@ -43,39 +43,47 @@
     return pltpu.CompilerParams(vmem_limit_bytes=mib * MB)
 
 
-def bias_kernel(pair_ref, weight_ref, out_ref, normed_ref, bias_ref):
+def bias_kernel(core_ref, pair_ref, weight_ref, own_ref, other_ref, normed_ref, bias_ref):
     normed_ref[...] = layer_norm(pair_ref[...])
     for w in range(16):
         block = jnp.concatenate([normed_ref[:, jq * 16 + w, :] for jq in range(4)], axis=0)
         bias_ref[:, w, :] = lax.dot_general(
             weight_ref[...], block.astype(BF16), NT, preferred_element_type=F32
         )
-    for core in range(2):
-        chunk = bias_ref[4 * core : 4 * core + 4].reshape(64, 128).astype(BF16)
-        for xz in range(8):
-            for zh in range(2):
-                out_ref[xz, core, zh] = chunk
-
-
-def pair_bias(pairwise, weight):
+    core = core_ref[0]
+    own_ref[...] = bias_ref[pl.ds(4 * core, 4)].reshape(64, 128).astype(BF16)
+    other_ref[...] = bias_ref[pl.ds(4 - 4 * core, 4)].reshape(64, 128).astype(BF16)
+
+
+def pair_bias(core, pairwise, weight):
     return pl.pallas_call(
         bias_kernel,
-        out_shape=jax.ShapeDtypeStruct((8, 2, 2, 64, 128), BF16),
+        in_specs=[
+            pl.BlockSpec(memory_space=pltpu.SMEM),
+            pl.BlockSpec(memory_space=pltpu.VMEM),
+            pl.BlockSpec(memory_space=pltpu.VMEM),
+        ],
+        out_shape=[jax.ShapeDtypeStruct((64, 128), BF16)] * 2,
         scratch_shapes=[pltpu.VMEM((32, 64, 128), F32), pltpu.VMEM((8, 16, 128), F32)],
         compiler_params=params(16),
         name="pair_bias",
-    )(pairwise, weight)
-
-
-def plane_kernel(in_ref, out_ref):
+    )(core, pairwise, weight)
+
+
+def plane_kernel(place_ref, d0_ref, d1_ref, d2_ref, d3_ref, out_ref):
     group = lax.broadcasted_iota(jnp.int32, (16, 128), 1) // 32
-    for zh in range(2):
-        for hh in range(4):
-            for x in range(4):
-                parts = [
-                    in_ref[(x * 4 + g) * 2 + zh, 16 * hh : 16 * hh + 16, :].astype(F32)
-                    for g in range(4)
-                ]
+    x, zl, core, zh = (place_ref[k] for k in range(4))
+    for d, ref in enumerate((d0_ref, d1_ref, d2_ref, d3_ref)):
+        lanes = pl.ds(pl.multiple_of(lax.rem(x + 4 - d, 4) * 128, 128), 128)
+        for at in range(2):
+            for hh in range(4):
+                parts = []
+                for g in range(4):
+                    far_zl = jnp.where(zl == g // 2, 0, 1)
+                    far_core = jnp.where(core == g % 2, 0, 1)
+                    far_zh = jnp.where(zh == at, 0, 1)
+                    block = (far_zl * 2 + far_zh) * 2 + far_core
+                    parts.append(ref[block, 16 * hh : 16 * hh + 16, :].astype(F32))
                 for jq in range(4):
                     turned = [
                         part if g == jq else pltpu.roll(part, 32 * ((g - jq) % 4), 1)
@@ -86,17 +94,59 @@
                         jnp.where(group == 0, turned[0], turned[1]),
                         jnp.where(group == 2, turned[2], turned[3]),
                     )
-                    base = 64 * zh + 16 * jq
-                    out_ref[hh, base : base + 16, 128 * x : 128 * x + 128] = row.astype(BF16)
-
-
-def plane(blocks):
+                    base = 64 * at + 16 * jq
+                    out_ref[hh, base : base + 16, lanes] = row.astype(BF16)
+
+
+def plane(place, blocks):
+    vmem = pl.BlockSpec(memory_space=pltpu.VMEM)
     return pl.pallas_call(
         plane_kernel,
+        in_specs=[pl.BlockSpec(memory_space=pltpu.SMEM)] + [vmem] * 4,
         out_shape=jax.ShapeDtypeStruct((4, 128, 512), BF16),
         compiler_params=params(8),
         name="bias_plane",
-    )(blocks)
+    )(place, *blocks)
+
+
+def project_kernel(x_ref, win_ref, qt_ref, k_ref, vt_ref, gate_ref):
+    normed = layer_norm(x_ref[:, 0].reshape(512, 256)).astype(BF16)
+
+    def project(t):
+        return lax.dot_general(
+            win_ref[256 * t : 256 * t + 256], normed, NT, preferred_element_type=F32
+        )
+
+    heads = vt_ref.shape[1]
+    qt_ref[0] = (project(0) * (32 ** (-0.5) * LOG2E)).astype(BF16)
+    k_ref[0] = lax.dot_general(normed, win_ref[256:512], NT, preferred_element_type=F32).astype(
+        BF16
+    )
+    vt_ref[0, :, :32] = project(2).astype(BF16).reshape(heads, 32, 512)
+    vt_ref[0, :, 32:] = jnp.ones((heads, 16, 512), BF16)
+    gate_ref[0] = jax.nn.sigmoid(project(3))
+
+
+def projections(x, win):
+    count = x.shape[1]
+    shapes = ((256, 512), (512, 256), (8, 48, 512), (256, 512))
+    types = (BF16, BF16, BF16, F32)
+    return pl.pallas_call(
+        project_kernel,
+        grid=(count,),
+        in_specs=[
+            pl.BlockSpec((16, 1, 32, 256), lambda s: (0, s, 0, 0)),
+            pl.BlockSpec(win.shape, lambda s: (0, 0)),
+        ],
+        out_specs=[
+            pl.BlockSpec((1,) + dims, lambda s, n=len(dims): (s,) + (0,) * n) for dims in shapes
+        ],
+        out_shape=[
+            jax.ShapeDtypeStruct((count,) + dims, t) for dims, t in zip(shapes, types)
+        ],
+        compiler_params=params(24),
+        name="projections",
+    )(x, win)
 
 
 def attention_kernel(
@@ -111,7 +161,10 @@
     other2_ref,
     other3_ref,
     x_ref,
-    win_ref,
+    qt_ref,
+    k_ref,
+    vt_ref,
+    gate_ref,
     wo_ref,
     wl_ref,
     wr_ref,
@@ -120,9 +173,6 @@
     out_ref,
     factor_ref,
     bias_ref,
-    qt_ref,
-    k_ref,
-    vt_ref,
     acc_ref,
 ):
     heads = bias_ref.shape[0]
@@ -148,28 +198,15 @@
                             )
 
     x = x_ref[:, 0].reshape(512, 256)
-    normed = layer_norm(x).astype(BF16)
-
-    def project(t):
-        return lax.dot_general(
-            win_ref[256 * t : 256 * t + 256], normed, NT, preferred_element_type=F32
-        )
-
-    qt_ref[...] = (project(0) * (32 ** (-0.5) * LOG2E)).astype(BF16)
-    k_ref[...] = lax.dot_general(
-        normed, win_ref[256:512], NT, preferred_element_type=F32
-    ).astype(BF16)
-    vt_ref[:, :32] = project(2).astype(BF16).reshape(heads, 32, 512)
-    vt_ref[:, 32:] = jnp.ones((heads, 16, 512), BF16)
     row_head = lax.broadcasted_iota(jnp.int32, (128, 512), 0) // 32
     for h in range(heads):
         lanes = slice(128 * (h // 4), 128 * (h // 4) + 128)
-        q_h = jnp.where(row_head == h % 4, qt_ref[lanes, :], jnp.zeros((), BF16))
-        s = jnp.dot(k_ref[:, lanes], q_h, preferred_element_type=F32) + bias_ref[h]
+        q_h = jnp.where(row_head == h % 4, qt_ref[0, lanes, :], jnp.zeros((), BF16))
+        s = jnp.dot(k_ref[0, :, lanes], q_h, preferred_element_type=F32) + bias_ref[h]
         p = jnp.exp2(s - jnp.max(s, axis=0, keepdims=True)).astype(BF16)
-        o = jnp.dot(vt_ref[h], p, preferred_element_type=F32)
+        o = jnp.dot(vt_ref[0, h], p, preferred_element_type=F32)
         acc_ref[32 * h : 32 * h + 32, :] = o[:32] / o[32:33]
-    attended = (acc_ref[...] * jax.nn.sigmoid(project(3))).T.astype(BF16)
+    attended = (acc_ref[...] * gate_ref[0]).T.astype(BF16)
     out = (
         x.astype(F32) + jnp.dot(attended, wo_ref[...], preferred_element_type=F32)
     ).astype(BF16)
@@ -195,7 +232,7 @@
                     ).astype(BF16)
 
 
-def attention(place, seq_live, biases, x, win, wo, wl, wr, live, live_col):
+def attention(place, seq_live, biases, x, projected, wo, wl, wr, live, live_col):
     count = x.shape[1]
     smem = pl.BlockSpec(memory_space=pltpu.SMEM)
 
@@ -213,7 +250,10 @@
             smem,
             *(whole(b) for b in biases),
             per_seq(16, 1, 32, 256),
-            whole(win),
+            *(
+                pl.BlockSpec((1,) + a.shape[1:], lambda s, n=a.ndim: (s,) + (0,) * (n - 1))
+                for a in projected
+            ),
             whole(wo),
             whole(wl),
             whole(wr),
@@ -230,14 +270,11 @@
         ],
         scratch_shapes=[
             pltpu.VMEM((8, 512, 512), F32),
-            pltpu.VMEM((256, 512), BF16),
-            pltpu.VMEM((512, 256), BF16),
-            pltpu.VMEM((8, 48, 512), BF16),
             pltpu.VMEM((256, 512), F32),
         ],
         compiler_params=params(48),
         name="row_attention",
-    )(place, seq_live, *biases, x, win, wo, wl, wr, live, live_col)
+    )(place, seq_live, *biases, x, *projected, wo, wl, wr, live, live_col)
 
 
 def outer_kernel(
@@ -433,19 +470,23 @@
     col_live = lax.dynamic_slice_in_dim(res_live, col * 64, 64)
     my_seqs = lax.dynamic_slice_in_dim(seq_live, col * 80 + row * 5, 5)
 
-    blocks = lax.all_to_all(
-        pair_bias(pairwise, bias_project.T).reshape(32, 64, 128),
-        ROW + ("zh",),
-        split_axis=0,
-        concat_axis=0,
-        tiled=True,
-    )
-    outgoing, blocks = lax.optimization_barrier((alignment.reshape(16, 5, 32, 256), blocks))
-    bias_plane = plane(blocks)
-    own = [bias_plane] + [
-        lax.ppermute(bias_plane, "y", [(i, (i + d) % 4) for i in range(4)]) for d in (1, 2, 3)
-    ]
-    other = [lax.ppermute(b, "core", swap) for b in own]
+    def gather(a, perms):
+        return [a] + [lax.ppermute(a, axes, perm) for axes, perm in perms]
+
+    def ring(axis):
+        return [(axis, [(i, (i + d) % 4) for i in range(4)]) for d in (1, 2, 3)]
+
+    z = ("zl", "zh")
+    near = [(z, [(i, i ^ d) for i in range(4)]) for d in (1, 2, 3)]
+    half, rest = pair_bias(core.reshape(1), pairwise, bias_project.T)
+    outgoing, half, rest = lax.optimization_barrier(
+        (alignment.reshape(16, 5, 32, 256), half, rest)
+    )
+    both = jnp.stack([half, lax.ppermute(rest, "core", swap)])
+    blocks = jnp.concatenate(gather(both, near), axis=0)
+    place = jnp.stack([lax.axis_index(name) for name in ("x", "zl", "core", "zh", "y")])
+    bias_plane = plane(place, gather(blocks, ring("x")))
+    own = gather(bias_plane, ring("y"))
     sequences = lax.all_to_all(outgoing, ROW, split_axis=0, concat_axis=0, tiled=True)
     live_plane = row_live[:, None] * col_live[None, :]
     inv = 1.0 / jnp.maximum(jnp.sum(seq_live) * live_plane, 1.0)
@@ -457,20 +498,41 @@
     win = attention_input_weight.reshape(256, 1024).T
     wp = tri_project.reshape(128, 512).T
     wt = tri_output.T
-    sequences, weight, wp, wt, inv, live_plane, win = lax.optimization_barrier(
-        (sequences, weight, wp, wt, pairs(inv), pairs(live_plane), win)
-    )
+    wl = jnp.tile(outer_factor_weight[:, 0], (1, 4))
+    wr = outer_factor_weight[:, 1].T
+    live_cols = jnp.broadcast_to(res_live[:, None], (512, 128))
+    sequences, _, weight, wp, wt, inv, live_plane, win, wl, wr, live_cols, my_seqs = (
+        lax.optimization_barrier(
+            (
+                sequences,
+                bias_plane,
+                weight,
+                wp,
+                wt,
+                pairs(inv),
+                pairs(live_plane),
+                win,
+                wl,
+                wr,
+                live_cols,
+                my_seqs,
+            )
+        )
+    )
+    projected = projections(sequences, win)
+    own, projected = lax.optimization_barrier((own, projected))
+    other = [lax.ppermute(b, "core", swap) for b in own]
     out_seq, factors = attention(
         jnp.stack([core, lax.axis_index("y")]),
         my_seqs,
         own + other,
         sequences,
-        win,
+        projected,
         attention_output_weight,
-        jnp.tile(outer_factor_weight[:, 0], (1, 4)),
-        outer_factor_weight[:, 1].T,
+        wl,
+        wr,
         res_live.reshape(1, 512),
-        jnp.broadcast_to(res_live[:, None], (512, 128)),
+        live_cols,
     )
     factors = lax.all_to_all(
         factors.reshape(128, 80, 128), ALL, split_axis=0, concat_axis=0, tiled=True

time: 213 us -> 221 us (1.038)
  blocking collectives: 85.5 us -> 63.7 us
  starting transfers between devices: 21.9 us -> 37.7 us
  waiting for transfers between devices: 36.6 us -> 41.2 us
  local copies, waits for them, and re-layouts: 14.5 us -> 18.9 us
  Pallas kernels: 51.6 us -> 55.2 us
    all_to_all x1 -> x0, blocking collectives: 20.9 us -> none  [body(): lax.all_to_all(pair_bias(pairwise, bias_project.T).reshape(32, 64, 128),...]
    ppermute x3 -> x10, starting transfers between devices: 3.84 us -> 19.4 us  [the longest x9 19.2 us: gather(): return [a] + [lax.ppermute(a, axes, perm) for axes, perm in perms]]
    pallas_call x2 -> x3, Pallas kernels: 1.77 us -> 5.91 us  [the longest x1 3.62 us: projections(): pl.pallas_call(project_kernel, grid=(count,), in_specs=[pl.BlockSpec((16,...]
    unnamed x31 -> x49, local copies, waits for them, and re-layouts: 7.9 us -> 11 us
    ppermute x4, waiting for transfers between devices: 0.01 us -> 2.57 us  [body(): other = [lax.ppermute(b, 'core', swap) for b in own]]
    all_to_all x1, starting transfers between devices: 5.1 us -> 7.31 us  [body(): lax.all_to_all(outgoing, ROW, split_axis=0, concat_axis=0, tiled=True)]
    ppermute x3 -> x10, waiting for transfers between devices: 23.2 us -> 25.2 us  [the longest x9 24.2 us: gather(): return [a] + [lax.ppermute(a, axes, perm) for axes, perm in perms]]
  transfers between devices with their start and end apart: 11 -> 18, of which waited for: 4 -> 12; matrix products, arithmetic and copies ran while one was open for 4% -> 5% of each run, Pallas kernels for 8% -> 9%
where the time goes in v4:
time: 221 us; the launch traced here: 220 us
  blocking collectives  63.7 us (29%)
  Pallas kernels  55.2 us (25%)
  waiting for transfers between devices  41.2 us (19%)
  starting transfers between devices  37.7 us (17%)
  local copies, waits for them, and re-layouts  18.9 us (9%)
  other arithmetic  2.62 us (1%)
    all_to_all x1, blocking collectives, body(): lax.all_to_all(factors.reshape(128, 80, 128), ALL, split_axis=0, concat_a...  40 us
    pallas_call x1, Pallas kernels, attention(): pl.pallas_call(attention_kernel, grid=(count,), in_specs=[smem, smem, *(w...  26.8 us
    ppermute x9, waiting for transfers between devices, gather(): return [a] + [lax.ppermute(a, axes, perm) for axes, perm in perms]  24.2 us
    all_to_all x1, blocking collectives, body(): blocks = lax.all_to_all(tri, ALL, split_axis=0, concat_axis=0, tiled=True)  23.7 us
    ppermute x9, starting transfers between devices, gather(): return [a] + [lax.ppermute(a, axes, perm) for axes, perm in perms]  19.2 us
    pallas_call x1, Pallas kernels, outer_update(): pl.pallas_call(outer_kernel, grid=(8,), in_specs=[pl.BlockSpec(memory_spa...  15 us
    all_to_all x1, waiting for transfers between devices, body(): lax.all_to_all(triangle(blocks), ALL, split_axis=0, concat_axis=0, tiled=...  12.8 us
    unnamed x49, local copies, waits for them, and re-layouts  11 us
  transfers between devices with their start and end apart: 18, of which 12 were waited for; matrix products, arithmetic and copies ran while one was open for 5% of the time, Pallas kernels for 9%

profile of v4, /device:TPU:1, one launch (start us, length us, event | category | flops | bytes accessed | tf_op | source)
XLA Modules:
  0.0 220.2 jit_solution(10204245628259494425)
XLA Ops:
  0.6 1.0 copy-done.2
  1.7 0.7 copy-done.12
  2.4 1.3 pair_bias.1
  3.7 7.3 %all-to-all-start = ((bf16[16,5,32,256]{3,2,1,0:T(8,128)(2,1)}), bf16[16,5,32,256]{3,2,1,0:T(8,128)(2,1)S(1)}, u32[]{:S(2)}, u32[]{:S(2)}) async-start(bf16[16,5,32,256]{3,2,1,0:T(8,128)(2,1)} %bitcast.70), calls=%async_computation | async-start | bytes 2621440 | tf_op jit(solution)/shard_map/all_to_all | solution.py:490
  11.0 0.2 collective-permute-start
  11.2 1.1 collective-permute-done
  12.3 3.5 %collective-permute-start.3 = (bf16[2,64,128]{2,1,0:T(8,128)(2,1)S(1)}, bf16[2,64,128]{2,1,0:T(8,128)(2,1)S(1)}, u32[]{:S(2)}, u32[]{:S(2)}) collective-permute-start(bf16[2,64,128]{2,1,0:T(8,128)(2,1)S(1)} %pad_maximum_fusion), channel_id=1, source_target_pairs={{0,20},{4,16},{16,4},{20,0},{1,21},{5,17},{17,5},{21,1},{2,22},{6,... | collective-permute-start | bytes 98312 | tf_op jit(solution)/shard_map/ppermute | solution.py:474
  15.8 1.3 collective-permute-start.1
  17.1 5.6 %collective-permute-done.1 = bf16[2,64,128]{2,1,0:T(8,128)(2,1)S(1)} collective-permute-done((bf16[2,64,128]{2,1,0:T(8,128)(2,1)S(1)}, bf16[2,64,128]{2,1,0:T(8,128)(2,1)S(1)}, u32[]{:S(2)}, u32[]{:S(2)}) %collective-permute-start.1) | collective-permute-done | bytes 32800 | tf_op jit(solution)/shard_map/ppermute | solution.py:474
  22.6 0.6 collective-permute-done.2
  23.2 9.9 %collective-permute-start.6 = (bf16[8,64,128]{2,1,0:T(8,128)(2,1)S(1)}, bf16[8,64,128]{2,1,0:T(8,128)(2,1)S(1)}, u32[]{:S(2)}, u32[]{:S(2)}) collective-permute-start(bf16[8,64,128]{2,1,0:T(8,128)(2,1)S(1)} %constant_dynamic-update-slice_fusion.d0_ref), channel_id=1, source_target_pairs={{0,96},{32,0},{64,32},{96,64},{1,97},{33,1},{65,33},{97,65},{2,98}... | collective-permute-start | bytes 393224 | tf_op jit(solution)/shard_map/ppermute | solution.py:474
  33.2 0.6 collective-permute-start.5
  33.7 0.1 collective-permute-start.4
  34.0 0.1 mul.73
  34.1 0.6 mul.80
  34.8 0.1 mul.76
  34.9 0.7 copy.40
  35.6 0.1 copy.39
  35.8 0.8 copy.38
  36.6 0.3 copy.42
  37.0 0.1 stack.35.place_ref
  37.1 1.0 collective-permute-done.6.d3_ref
  38.1 0.5 collective-permute-done.5.d2_ref
  38.6 3.5 %collective-permute-done.4.d1_ref = bf16[8,64,128]{2,1,0:T(8,128)(2,1)S(1)} collective-permute-done((bf16[8,64,128]{2,1,0:T(8,128)(2,1)S(1)}, bf16[8,64,128]{2,1,0:T(8,128)(2,1)S(1)}, u32[]{:S(2)}, u32[]{:S(2)}) %collective-permute-start.4) | collective-permute-done | bytes 131104 | tf_op jit(solution)/shard_map/ppermute | solution.py:474
  42.1 1.0 bias_plane.1.own0_ref
  43.2 2.8 %collective-permute-start.9 = (bf16[4,128,512]{2,1,0:T(8,128)(2,1)S(1)}, bf16[4,128,512]{2,1,0:T(8,128)(2,1)S(1)}, u32[]{:S(2)}, u32[]{:S(2)}) collective-permute-start(bf16[4,128,512]{2,1,0:T(8,128)(2,1)S(1)} %bias_plane.1.own0_ref), channel_id=1, source_target_pairs={{0,3},{1,0},{2,1},{3,2},{4,7},{5,4},{6,5},{7,6},{8,11},{9,8},{10,9... | collective-permute-start | bytes 1572872 | tf_op jit(solution)/shard_map/ppermute | solution.py:474
  46.0 0.3 collective-permute-start.8
  46.3 0.7 collective-permute-start.7
  47.0 1.3 convert_reduce_fusion
  48.3 1.2 maximum_divide_fusion
  49.5 0.7 slice_bitcast_fusion
  50.3 0.7 tile.11
  50.9 0.1 broadcast_in_dim.2.live_col_ref
  51.1 3.6 %projections.1 = (bf16[5,256,512]{2,1,0:T(8,128)(2,1)S(1)}, bf16[5,512,256]{2,1,0:T(8,128)(2,1)S(1)}, bf16[5,8,48,512]{3,2,1,0:T(8,128)(2,1)S(1)}, f32[5,256,512]{2,1,0:T(8,128)S(1)}) custom-call(bf16[16,5,32,256]{3,2,1,0:T(8,128)(2,1)S(1)} %all-to-all-done.x_ref, bf16[1024,256]{1,0:T(8,128)(2,1)S(1)} %bitcast.56), custom_call_target="tpu_custom_call" | custom-call | tf_op jit(solution)/shard_map/projections/pallas_call | solution.py:134
  54.7 1.5 copy-done.1
  56.2 1.3 copy-done.4
  57.4 1.1 copy-done.6
  58.6 1.0 copy-done.7
  59.6 13.0 %collective-permute-done.7.own1_ref = bf16[4,128,512]{2,1,0:T(8,128)(2,1)} collective-permute-done((bf16[4,128,512]{2,1,0:T(8,128)(2,1)S(1)}, bf16[4,128,512]{2,1,0:T(8,128)(2,1)}, u32[]{:S(2)}, u32[]{:S(2)}) %collective-permute-start.7) | collective-permute-done | bytes 524320 | tf_op jit(solution)/shard_map/ppermute | solution.py:474
  72.6 0.5 collective-permute-start.10
  73.2 0.5 collective-permute-start.12
  73.7 0.9 copy.43.wl_ref
  74.7 0.6 collective-permute-done.10.other0_ref
  75.3 0.7 collective-permute-done.11.other1_ref
  75.9 1.3 collective-permute-done.12.other2_ref
  77.3 26.8 %row_attention.1 = (bf16[16,5,32,256]{3,2,1,0:T(8,128)(2,1)S(1)}, bf16[8,2,8,5,16,128]{5,4,3,2,1,0:T(8,128)(2,1)}) custom-call(s32[2]{0:T(128)S(1)} %pad_add_fusion.place_ref, f32[5]{0:T(128)S(1)} %dynamic_slice.11.seq_ref, bf16[4,128,512]{2,1,0:T(8,128)(2,1)S(1)} %bias_plane.1.own0_ref, bf16[4,128,512]{2,1,0:T(8,128)(2,1)} %collective-permute-done.7.own1_ref, ...), custom_call_target="tpu_custom_call" | custom-call | tf_op jit(solution)/shard_map/row_attention/pallas_call | solution.py:245
  104.0 40.0 %all_to_all.25 = bf16[128,80,128]{2,1,0:T(8,128)(2,1)S(1)} all-to-all(bf16[128,80,128]{2,1,0:T(8,128)(2,1)} %bitcast.69), channel_id=1, replica_groups=mesh['x'=4,'zl'=2,'core'=2,'zh'=2,'y'=4] {'x','zl','core','zh','y'}, dimensions={0} | all-to-all | bytes 5242880 | tf_op jit(solution)/shard_map/all_to_all | solution.py:537
  144.0 1.2 fusion
  145.2 0.4 copy.53
  145.6 1.6 collective-permute-start.14
  147.3 3.6 %all-to-all-start.2 = ((bf16[16,5,32,256]{3,2,1,0:T(8,128)(2,1)}), bf16[16,5,32,256]{3,2,1,0:T(8,128)(2,1)S(1)}, u32[]{:S(2)}, u32[]{:S(2)}) async-start(bf16[16,5,32,256]{3,2,1,0:T(8,128)(2,1)} %copy-done.5), calls=%async_computation.2 | async-start | bytes 2621440 | tf_op jit(solution)/shard_map/all_to_all | solution.py:545
  150.9 0.1 copy.44.w_ref
  151.0 1.7 copy.54
  152.8 15.0 %outer_update.1 = (bf16[4,8,64,128]{3,2,1,0:T(8,128)(2,1)S(1)}, bf16[2,8,256,128]{3,2,1,0:T(8,128)(2,1)S(1)}) custom-call(s32[1]{0:T(128)} %bitcast.core_ref, bf16[640,1024]{1,0:T(8,128)(2,1)S(1)} %bitcast.53, bf16[640,1024]{1,0:T(8,128)(2,1)S(1)} %bitcast.52, bf16[640,1024]{1,0:T(8,128)(2,1)} %collective-permute-done.14.other_ref, ...), custom_call_target="tpu_custom_call" | custom-call | tf_op jit(solution)/shard_map/outer_update/pallas_call | solution.py:346
  167.8 1.0 copy-done.8
  168.8 0.6 all-to-all-done.2
  169.4 1.9 copy.55
  171.3 23.7 %all_to_all.26.in_ref = bf16[128,2,16,128]{3,2,1,0:T(8,128)(2,1)S(1)} all-to-all(bf16[128,2,16,128]{3,2,1,0:T(8,128)(2,1)S(1)} %bitcast.68), channel_id=1, replica_groups=mesh['x'=4,'zl'=2,'core'=2,'zh'=2,'y'=4] {'x','zl','core','zh','y'}, dimensions={0} | all-to-all | bytes 2097152 | tf_op jit(solution)/shard_map/all_to_all | solution.py:563
  195.0 3.7 %triangle.1 = bf16[128,16,128]{2,1,0:T(8,128)(2,1)} custom-call(bf16[128,2,16,128]{3,2,1,0:T(8,128)(2,1)S(1)} %all_to_all.26.in_ref), custom_call_target="tpu_custom_call" | custom-call | tf_op jit(solution)/shard_map/triangle/pallas_call | solution.py:402
  198.7 4.7 %all-to-all-start.4 = ((bf16[128,16,128]{2,1,0:T(8,128)(2,1)}), bf16[128,16,128]{2,1,0:T(8,128)(2,1)S(1)}, u32[]{:S(2)}, u32[]{:S(2)}) async-start(bf16[128,16,128]{2,1,0:T(8,128)(2,1)} %triangle.1), calls=%async_computation.4 | async-start | bytes 1048576 | tf_op jit(solution)/shard_map/all_to_all | solution.py:564
  203.5 1.1 copied.1
  204.6 12.8 %all-to-all-done.4 = bf16[128,16,128]{2,1,0:T(8,128)(2,1)S(1)} async-done(((bf16[128,16,128]{2,1,0:T(8,128)(2,1)}), bf16[128,16,128]{2,1,0:T(8,128)(2,1)S(1)}, u32[]{:S(2)}, u32[]{:S(2)}) %all-to-all-start.4) | async-done | bytes 524320 | tf_op jit(solution)/shard_map/all_to_all | solution.py:564
  217.4 0.1 copy.56
  217.6 2.6 %pair_final.1 = bf16[32,64,128]{2,1,0:T(8,128)(2,1)} custom-call(bf16[16,128,128]{2,1,0:T(8,128)(2,1)S(1)} %bitcast.57, bf16[32,64,128]{2,1,0:T(8,128)(2,1)S(1)} %bitcast.59, bf16[128,128]{1,0:T(8,128)(2,1)S(1)} %bitcast.61, bf16[128,128]{1,0:T(8,128)(2,1)S(1)} %copy-done.11), custom_call_target="tpu_custom_call" | custom-call | tf_op jit(solution)/shard_map/pair_final/pallas_call | solution.py:428
  (57 shorter events, 0.7 us)
Async XLA Ops:
  0.6 1.0 copy-start.2
  1.7 0.7 copy-start.12
  3.6 30.2 %copy-start.19 = (s32[512]{0:T(512)S(1)}, s32[512]{0:T(512)}, u32[]{:S(2)}) copy-start(s32[512]{0:T(512)} %param.14) | copy-start | bytes 6148
  3.6 31.0 %copy-start.18 = (s32[640]{0:T(1024)S(1)}, s32[640]{0:T(1024)}, u32[]{:S(2)}) copy-start(s32[640]{0:T(1024)} %param.15) | copy-start | bytes 7684
  3.7 31.2 %copy-start.17 = (bf16[128,128]{1,0:T(8,128)(2,1)S(1)}, bf16[128,128]{1,0:T(8,128)(2,1)}, u32[]{:S(2)}) copy-start(bf16[128,128]{1,0:T(8,128)(2,1)} %param.23) | copy-start | bytes 98308
  3.7 32.0 %copy-start.16 = (bf16[128,4,128]{2,1,0:T(4,128)(2,1)S(1)}, bf16[128,4,128]{2,1,0:T(4,128)(2,1)}, u32[]{:S(2)}) copy-start(bf16[128,4,128]{2,1,0:T(4,128)(2,1)} %param.21) | copy-start | bytes 393220
  3.7 32.1 %copy-start.15 = (bf16[1024,128]{1,0:T(8,128)(2,1)S(1)}, bf16[1024,128]{1,0:T(8,128)(2,1)}, u32[]{:S(2)}) copy-start(bf16[1024,128]{1,0:T(8,128)(2,1)} %param.20) | copy-start | bytes 786436
  3.7 46.6 %all-to-all-start = ((bf16[16,5,32,256]{3,2,1,0:T(8,128)(2,1)}), bf16[16,5,32,256]{3,2,1,0:T(8,128)(2,1)S(1)}, u32[]{:S(2)}, u32[]{:S(2)}) async-start(bf16[16,5,32,256]{3,2,1,0:T(8,128)(2,1)} %bitcast.70), calls=%async_computation | async-start | bytes 2621440 | tf_op jit(solution)/shard_map/all_to_all | solution.py:490
  11.0 25.6 %copy-start.14 = (bf16[256,4,256]{2,1,0:T(4,128)(2,1)S(1)}, bf16[256,4,256]{2,1,0:T(4,128)(2,1)}, u32[]{:S(2)}) copy-start(bf16[256,4,256]{2,1,0:T(4,128)(2,1)} %param.16) | copy-start | bytes 1572868
  11.0 1.3 collective-permute-start
  12.3 10.9 %collective-permute-start.3 = (bf16[2,64,128]{2,1,0:T(8,128)(2,1)S(1)}, bf16[2,64,128]{2,1,0:T(8,128)(2,1)S(1)}, u32[]{:S(2)}, u32[]{:S(2)}) collective-permute-start(bf16[2,64,128]{2,1,0:T(8,128)(2,1)S(1)} %pad_maximum_fusion), channel_id=1, source_target_pairs={{0,20},{4,16},{16,4},{20,0},{1,21},{5,17},{17,5},{21,1},{2,22},{6,... | collective-permute-start | bytes 98312 | tf_op jit(solution)/shard_map/ppermute | solution.py:474
  15.8 7.4 %collective-permute-start.2 = (bf16[2,64,128]{2,1,0:T(8,128)(2,1)S(1)}, bf16[2,64,128]{2,1,0:T(8,128)(2,1)S(1)}, u32[]{:S(2)}, u32[]{:S(2)}) collective-permute-start(bf16[2,64,128]{2,1,0:T(8,128)(2,1)S(1)} %pad_maximum_fusion), channel_id=1, source_target_pairs={{0,16},{4,20},{16,0},{20,4},{1,17},{5,21},{17,1},{21,5},{2,18},{6,... | collective-permute-start | bytes 98312 | tf_op jit(solution)/shard_map/ppermute | solution.py:474
  15.8 6.8 %collective-permute-start.1 = (bf16[2,64,128]{2,1,0:T(8,128)(2,1)S(1)}, bf16[2,64,128]{2,1,0:T(8,128)(2,1)S(1)}, u32[]{:S(2)}, u32[]{:S(2)}) collective-permute-start(bf16[2,64,128]{2,1,0:T(8,128)(2,1)S(1)} %pad_maximum_fusion), channel_id=1, source_target_pairs={{0,4},{4,0},{16,20},{20,16},{1,5},{5,1},{17,21},{21,17},{2,6},{6,2... | collective-permute-start | bytes 98312 | tf_op jit(solution)/shard_map/ppermute | solution.py:474
  23.2 14.9 %collective-permute-start.6 = (bf16[8,64,128]{2,1,0:T(8,128)(2,1)S(1)}, bf16[8,64,128]{2,1,0:T(8,128)(2,1)S(1)}, u32[]{:S(2)}, u32[]{:S(2)}) collective-permute-start(bf16[8,64,128]{2,1,0:T(8,128)(2,1)S(1)} %constant_dynamic-update-slice_fusion.d0_ref), channel_id=1, source_target_pairs={{0,96},{32,0},{64,32},{96,64},{1,97},{33,1},{65,33},{97,65},{2,98}... | collective-permute-start | bytes 393224 | tf_op jit(solution)/shard_map/ppermute | solution.py:474
  33.2 5.4 %collective-permute-start.5 = (bf16[8,64,128]{2,1,0:T(8,128)(2,1)S(1)}, bf16[8,64,128]{2,1,0:T(8,128)(2,1)S(1)}, u32[]{:S(2)}, u32[]{:S(2)}) collective-permute-start(bf16[8,64,128]{2,1,0:T(8,128)(2,1)S(1)} %constant_dynamic-update-slice_fusion.d0_ref), channel_id=1, source_target_pairs={{0,64},{32,96},{64,0},{96,32},{1,65},{33,97},{65,1},{97,33},{2,66}... | collective-permute-start | bytes 393224 | tf_op jit(solution)/shard_map/ppermute | solution.py:474
  33.7 8.4 %collective-permute-start.4 = (bf16[8,64,128]{2,1,0:T(8,128)(2,1)S(1)}, bf16[8,64,128]{2,1,0:T(8,128)(2,1)S(1)}, u32[]{:S(2)}, u32[]{:S(2)}) collective-permute-start(bf16[8,64,128]{2,1,0:T(8,128)(2,1)S(1)} %constant_dynamic-update-slice_fusion.d0_ref), channel_id=1, source_target_pairs={{0,32},{32,64},{64,96},{96,0},{1,33},{33,65},{65,97},{97,1},{2,34}... | collective-permute-start | bytes 393224 | tf_op jit(solution)/shard_map/ppermute | solution.py:474
  43.1 34.1 %copy-start.9 = (bf16[256,256]{1,0:T(8,128)(2,1)S(1)}, bf16[256,256]{1,0:T(8,128)(2,1)}, u32[]{:S(2)}) copy-start(bf16[256,256]{1,0:T(8,128)(2,1)} %wo_ref.1) | copy-start | bytes 393220
  43.2 16.5 %collective-permute-start.9 = (bf16[4,128,512]{2,1,0:T(8,128)(2,1)S(1)}, bf16[4,128,512]{2,1,0:T(8,128)(2,1)S(1)}, u32[]{:S(2)}, u32[]{:S(2)}) collective-permute-start(bf16[4,128,512]{2,1,0:T(8,128)(2,1)S(1)} %bias_plane.1.own0_ref), channel_id=1, source_target_pairs={{0,3},{1,0},{2,1},{3,2},{4,7},{5,4},{6,5},{7,6},{8,11},{9,8},{10,9... | collective-permute-start | bytes 1572872 | tf_op jit(solution)/shard_map/ppermute | solution.py:474
  46.0 13.7 %collective-permute-start.8 = (bf16[4,128,512]{2,1,0:T(8,128)(2,1)S(1)}, bf16[4,128,512]{2,1,0:T(8,128)(2,1)}, u32[]{:S(2)}, u32[]{:S(2)}) collective-permute-start(bf16[4,128,512]{2,1,0:T(8,128)(2,1)S(1)} %bias_plane.1.own0_ref), channel_id=1, source_target_pairs={{0,2},{1,3},{2,0},{3,1},{4,6},{5,7},{6,4},{7,5},{8,10},{9,11},{10,... | collective-permute-start | bytes 1572872 | tf_op jit(solution)/shard_map/ppermute | solution.py:474
  46.3 26.3 %collective-permute-start.7 = (bf16[4,128,512]{2,1,0:T(8,128)(2,1)S(1)}, bf16[4,128,512]{2,1,0:T(8,128)(2,1)}, u32[]{:S(2)}, u32[]{:S(2)}) collective-permute-start(bf16[4,128,512]{2,1,0:T(8,128)(2,1)S(1)} %bias_plane.1.own0_ref), channel_id=1, source_target_pairs={{0,1},{1,2},{2,3},{3,0},{4,5},{5,6},{6,7},{7,4},{8,9},{9,10},{10,1... | collective-permute-start | bytes 1572872 | tf_op jit(solution)/shard_map/ppermute | solution.py:474
  50.3 27.0 %copy-start = (bf16[16,5,32,256]{3,2,1,0:T(8,128)(2,1)}, bf16[16,5,32,256]{3,2,1,0:T(8,128)(2,1)S(1)}, u32[]{:S(2)}) copy-start(bf16[16,5,32,256]{3,2,1,0:T(8,128)(2,1)S(1)} %all-to-all-done.x_ref) | copy-start | bytes 3932164
  54.7 1.5 copy-start.1
  56.2 1.3 copy-start.4
  57.4 1.2 copy-start.6
  58.6 1.0 copy-start.7
  72.6 2.6 %collective-permute-start.10 = (bf16[4,128,512]{2,1,0:T(8,128)(2,1)S(1)}, bf16[4,128,512]{2,1,0:T(8,128)(2,1)S(1)}, u32[]{:S(2)}, u32[]{:S(2)}) collective-permute-start(bf16[4,128,512]{2,1,0:T(8,128)(2,1)S(1)} %bias_plane.1.own0_ref), channel_id=1, source_target_pairs={{0,8},{8,0},{1,9},{9,1},{2,10},{10,2},{3,11},{11,3},{4,12},{12,4},... | collective-permute-start | bytes 1572872 | tf_op jit(solution)/shard_map/ppermute | solution.py:524
  73.1 2.8 %collective-permute-start.11 = (bf16[4,128,512]{2,1,0:T(8,128)(2,1)}, bf16[4,128,512]{2,1,0:T(8,128)(2,1)}, u32[]{:S(2)}, u32[]{:S(2)}) collective-permute-start(bf16[4,128,512]{2,1,0:T(8,128)(2,1)} %collective-permute-done.7.own1_ref), channel_id=1, source_target_pairs={{0,8},{8,0},{1,9},{9,1},{2,10},{10,2},{3,11},{11,3},{4,12},{12,4},... | collective-permute-start | bytes 1572872 | tf_op jit(solution)/shard_map/ppermute | solution.py:524
  73.2 4.1 %collective-permute-start.12 = (bf16[4,128,512]{2,1,0:T(8,128)(2,1)}, bf16[4,128,512]{2,1,0:T(8,128)(2,1)}, u32[]{:S(2)}, u32[]{:S(2)}) collective-permute-start(bf16[4,128,512]{2,1,0:T(8,128)(2,1)} %collective-permute-done.8.own2_ref), channel_id=1, source_target_pairs={{0,8},{8,0},{1,9},{9,1},{2,10},{10,2},{3,11},{11,3},{4,12},{12,4},... | collective-permute-start | bytes 1572872 | tf_op jit(solution)/shard_map/ppermute | solution.py:524
  73.7 3.6 %collective-permute-start.13 = (bf16[4,128,512]{2,1,0:T(8,128)(2,1)S(1)}, bf16[4,128,512]{2,1,0:T(8,128)(2,1)}, u32[]{:S(2)}, u32[]{:S(2)}) collective-permute-start(bf16[4,128,512]{2,1,0:T(8,128)(2,1)S(1)} %collective-permute-done.9.own3_ref), channel_id=1, source_target_pairs={{0,8},{8,0},{1,9},{9,1},{2,10},{10,2},{3,11},{11,3},{4,12},{12,4},... | collective-permute-start | bytes 1572872 | tf_op jit(solution)/shard_map/ppermute | solution.py:524
  104.0 40.0 %copy-start.5 = (bf16[16,5,32,256]{3,2,1,0:T(8,128)(2,1)}, bf16[16,5,32,256]{3,2,1,0:T(8,128)(2,1)S(1)}, u32[]{:S(2)}) copy-start(bf16[16,5,32,256]{3,2,1,0:T(8,128)(2,1)S(1)} %get-tuple-element.69) | copy-start | bytes 3932164
  145.6 5.3 %copy-start.13 = (bf16[128,16,2,32]{0,3,2,1:T(8,128)(2,1)S(1)}, bf16[128,16,2,32]{0,3,2,1:T(8,128)(2,1)}, u32[]{:S(2)}) copy-start(bf16[128,16,2,32]{0,3,2,1:T(8,128)(2,1)} %copy.38) | copy-start | bytes 786436
  145.6 7.2 %collective-permute-start.14 = (bf16[640,1024]{1,0:T(8,128)(2,1)S(1)}, bf16[640,1024]{1,0:T(8,128)(2,1)}, u32[]{:S(2)}, u32[]{:S(2)}) collective-permute-start(bf16[640,1024]{1,0:T(8,128)(2,1)S(1)} %bitcast.51), channel_id=1, source_target_pairs={{0,8},{8,0},{1,9},{9,1},{2,10},{10,2},{3,11},{11,3},{4,12},{12,4},... | collective-permute-start | bytes 3932168 | tf_op jit(solution)/shard_map/ppermute | solution.py:543
  147.3 22.1 %all-to-all-start.2 = ((bf16[16,5,32,256]{3,2,1,0:T(8,128)(2,1)}), bf16[16,5,32,256]{3,2,1,0:T(8,128)(2,1)S(1)}, u32[]{:S(2)}, u32[]{:S(2)}) async-start(bf16[16,5,32,256]{3,2,1,0:T(8,128)(2,1)} %copy-done.5), calls=%async_computation.2 | async-start | bytes 2621440 | tf_op jit(solution)/shard_map/all_to_all | solution.py:545
  151.0 1.8 copy-start.3
  167.8 1.0 copy-start.8
  198.7 18.7 %all-to-all-start.4 = ((bf16[128,16,128]{2,1,0:T(8,128)(2,1)}), bf16[128,16,128]{2,1,0:T(8,128)(2,1)S(1)}, u32[]{:S(2)}, u32[]{:S(2)}) async-start(bf16[128,16,128]{2,1,0:T(8,128)(2,1)} %triangle.1), calls=%async_computation.4 | async-start | bytes 1048576 | tf_op jit(solution)/shard_map/all_to_all | solution.py:564
  203.4 14.1 %copy-start.10 = (bf16[128,128]{0,1:T(8,128)(2,1)S(1)}, bf16[128,128]{0,1:T(8,128)(2,1)}, u32[]{:S(2)}) copy-start(bf16[128,128]{0,1:T(8,128)(2,1)} %copy.40) | copy-start | bytes 98308
  203.5 14.1 %copy-start.11 = (bf16[128,128]{1,0:T(8,128)(2,1)S(1)}, bf16[128,128]{1,0:T(8,128)(2,1)}, u32[]{:S(2)}) copy-start(bf16[128,128]{1,0:T(8,128)(2,1)} %wg_ref.1) | copy-start | bytes 98308

commit v5 on v3

--- a/solution.py
+++ b/solution.py
@@ -162,13 +162,27 @@
     vt_ref[:, :32] = project(2).astype(BF16).reshape(heads, 32, 512)
     vt_ref[:, 32:] = jnp.ones((heads, 16, 512), BF16)
     row_head = lax.broadcasted_iota(jnp.int32, (128, 512), 0) // 32
-    for h in range(heads):
+
+    def scores(h):
         lanes = slice(128 * (h // 4), 128 * (h // 4) + 128)
         q_h = jnp.where(row_head == h % 4, qt_ref[lanes, :], jnp.zeros((), BF16))
         s = jnp.dot(k_ref[:, lanes], q_h, preferred_element_type=F32) + bias_ref[h]
-        p = jnp.exp2(s - jnp.max(s, axis=0, keepdims=True)).astype(BF16)
+        return s, jnp.max(s, axis=0, keepdims=True)
+
+    def values(h, p):
         o = jnp.dot(vt_ref[h], p, preferred_element_type=F32)
         acc_ref[32 * h : 32 * h + 32, :] = o[:32] / o[32:33]
+
+    s, top = scores(0)
+    p = None
+    for h in range(heads):
+        ahead = scores(h + 1) if h + 1 < heads else None
+        if p is not None:
+            values(h - 1, p)
+        p = jnp.exp2(s - top).astype(BF16)
+        if ahead is not None:
+            s, top = ahead
+    values(heads - 1, p)
     attended = (acc_ref[...] * jax.nn.sigmoid(project(3))).T.astype(BF16)
     out = (
         x.astype(F32) + jnp.dot(attended, wo_ref[...], preferred_element_type=F32)
@@ -235,7 +249,7 @@
             pltpu.VMEM((8, 48, 512), BF16),
             pltpu.VMEM((256, 512), F32),
         ],
-        compiler_params=params(48),
+        compiler_params=params(32),
         name="row_attention",
     )(place, seq_live, *biases, x, win, wo, wl, wr, live, live_col)
 
@@ -255,80 +269,68 @@
     lt_ref,
     x_ref,
 ):
-    step = pl.program_id(0)
-
-    @pl.when(step == 0)
-    def _():
-        for v in range(8):
-            rows = slice(128 * v, 128 * v + 128)
-            lt_ref[rows, :] = l_ref[:, rows].astype(F32).T.astype(BF16)
-        for ref, core in ((own_ref, core_ref[0]), (other_ref, 1 - core_ref[0])):
-
-            def some(n, carry):
-                lanes = pl.ds(pl.multiple_of(n * 256, 256), 256)
-                product = jnp.dot(lt_ref[...], ref[:, lanes], preferred_element_type=F32)
-                for k in range(2):
-                    base = pl.multiple_of(core * 512 + n * 128 + 64 * k, 64)
-                    for v in range(8):
-                        for half in range(2):
-                            at = 128 * v + 32 * half
-                            low, high = mix(
-                                product[at : at + 32, 128 * k : 128 * k + 128],
-                                product[at + 64 : at + 96, 128 * k : 128 * k + 128],
-                            )
-                            columns = slice(128 * half, 128 * half + 128)
-                            x_ref[v, pl.ds(base, 32), columns] = low.astype(BF16)
-                            x_ref[v, pl.ds(base + 32, 32), columns] = high.astype(BF16)
-                return carry
-
-            lax.fori_loop(0, 4, some, 0)
-
-    update = jnp.dot(w_ref[...], x_ref[step], preferred_element_type=F32)
-    for half in range(2):
-        part = update[:, 128 * half : 128 * half + 128] * inv_ref[half, 0]
-        before = jnp.concatenate([pair_ref[half, 0], pair_ref[half + 2, 0]], axis=0)
-        mid = (before.astype(F32) + part.T).astype(BF16)
-        mid_ref[half, 0] = mid[:64]
-        mid_ref[half + 2, 0] = mid[64:]
+    for v in range(8):
+        rows = slice(128 * v, 128 * v + 128)
+        lt_ref[rows, :] = l_ref[:, rows].astype(F32).T.astype(BF16)
+    for ref, core in ((own_ref, core_ref[0]), (other_ref, 1 - core_ref[0])):
+
+        def some(n, carry):
+            lanes = pl.ds(pl.multiple_of(n * 256, 256), 256)
+            product = jnp.dot(lt_ref[...], ref[:, lanes], preferred_element_type=F32)
+            for k in range(2):
+                base = pl.multiple_of(core * 512 + n * 128 + 64 * k, 64)
+                for v in range(8):
+                    for half in range(2):
+                        at = 128 * v + 32 * half
+                        low, high = mix(
+                            product[at : at + 32, 128 * k : 128 * k + 128],
+                            product[at + 64 : at + 96, 128 * k : 128 * k + 128],
+                        )
+                        place = (v % 2) * 256 + 128 * half
+                        columns = slice(place, place + 128)
+                        x_ref[v // 2, pl.ds(base, 32), columns] = low.astype(BF16)
+                        x_ref[v // 2, pl.ds(base + 32, 32), columns] = high.astype(BF16)
+            return carry
+
+        lax.fori_loop(0, 4, some, 0, unroll=2)
+
+    def finish(g, carry):
+        update = jnp.dot(w_ref[...], x_ref[g], preferred_element_type=F32)
+        places = [(half, 2 * g + e) for e in range(2) for half in range(2)]
+        inv = jnp.concatenate([inv_ref[half, v] for half, v in places], axis=1)
+        live = jnp.concatenate([plane_ref[half, v] for half, v in places], axis=1)
+        before = jnp.concatenate(
+            [pair_ref[half + 2 * k, v] for half, v in places for k in range(2)], axis=0
+        )
+        mid = (before.astype(F32) + (update * inv).T).astype(BF16)
         normed = layer_norm(mid).astype(BF16)
         terms = lax.dot_general(wp_ref[...], normed, NT, preferred_element_type=F32)
-        plane = plane_ref[half, 0]
-        tri_ref[half, 0, :128] = (jax.nn.sigmoid(terms[:128]) * terms[128:256] * plane).astype(BF16)
-        tri_ref[half, 0, 128:] = (jax.nn.sigmoid(terms[256:384]) * terms[384:] * plane).astype(BF16)
-
-
-def outer_update(core, left, own, other, weight, inv, plane, pairwise, wp):
+        ta = (jax.nn.sigmoid(terms[:128]) * terms[128:256] * live).astype(BF16)
+        tb = (jax.nn.sigmoid(terms[256:384]) * terms[384:] * live).astype(BF16)
+        for n, (half, v) in enumerate(places):
+            for k in range(2):
+                mid_ref[half + 2 * k, v] = mid[128 * n + 64 * k : 128 * n + 64 * k + 64]
+            tri_ref[half, v, :128] = ta[:, 128 * n : 128 * n + 128]
+            tri_ref[half, v, 128:] = tb[:, 128 * n : 128 * n + 128]
+        return carry
+
+    lax.fori_loop(0, 4, finish, 0, unroll=True)
+
+
+def outer_update(core, left, own, other, weight, inv, live_plane, pairwise, wp):
     total = left.shape[0]
-
-    def whole(a):
-        return pl.BlockSpec(a.shape, lambda v: (0,) * a.ndim)
-
-    def by_v(*dims):
-        return pl.BlockSpec(dims, lambda v: (0, v) + (0,) * (len(dims) - 2))
-
+    vmem = pl.BlockSpec(memory_space=pltpu.VMEM)
     return pl.pallas_call(
         outer_kernel,
-        grid=(8,),
-        in_specs=[
-            pl.BlockSpec(memory_space=pltpu.SMEM),
-            whole(left),
-            whole(own),
-            whole(other),
-            whole(weight),
-            by_v(2, 1, 1, 128),
-            by_v(2, 1, 1, 128),
-            by_v(4, 1, 64, 128),
-            whole(wp),
-        ],
-        out_specs=[by_v(4, 1, 64, 128), by_v(2, 1, 256, 128)],
+        in_specs=[pl.BlockSpec(memory_space=pltpu.SMEM)] + [vmem] * 8,
         out_shape=[
             jax.ShapeDtypeStruct((4, 8, 64, 128), BF16),
             jax.ShapeDtypeStruct((2, 8, 256, 128), BF16),
         ],
-        scratch_shapes=[pltpu.VMEM((1024, total), BF16), pltpu.VMEM((8, 1024, 256), BF16)],
+        scratch_shapes=[pltpu.VMEM((1024, total), BF16), pltpu.VMEM((4, 1024, 512), BF16)],
         compiler_params=params(32),
         name="outer_update",
-    )(core, left, own, other, weight, inv, plane, pairwise, wp)
+    )(core, left, own, other, weight, inv, live_plane, pairwise, wp)
 
 
 def triangle_kernel(in_ref, out_ref, a_ref, b_ref):
@@ -371,7 +373,24 @@
     )(blocks)
 
 
-def final_kernel(tri_ref, mid_ref, wt_ref, wg_ref, out_ref):
+def gate_kernel(mid_ref, wg_ref, out_ref):
+    for u in range(16):
+        mid = jnp.concatenate([mid_ref[u], mid_ref[16 + u]], axis=0)
+        out_ref[u] = jax.nn.sigmoid(
+            jnp.dot(layer_norm(mid).astype(BF16), wg_ref[...], preferred_element_type=F32)
+        )
+
+
+def gates(mid, wg):
+    return pl.pallas_call(
+        gate_kernel,
+        out_shape=jax.ShapeDtypeStruct((16, 128, 128), F32),
+        compiler_params=params(16),
+        name="pair_gate",
+    )(mid, wg)
+
+
+def final_kernel(tri_ref, mid_ref, wt_ref, gate_ref, out_ref):
     for u in range(16):
         combined = tri_ref[u].astype(F32)
         centered = combined - jnp.mean(combined, axis=0, keepdims=True)
@@ -379,21 +398,18 @@
         normed = (centered * lax.rsqrt(variance + EPS)).astype(BF16)
         update = jnp.dot(wt_ref[...], normed, preferred_element_type=F32)
         mid = jnp.concatenate([mid_ref[u], mid_ref[16 + u]], axis=0)
-        gate = jax.nn.sigmoid(
-            jnp.dot(layer_norm(mid).astype(BF16), wg_ref[...], preferred_element_type=F32)
-        )
-        out = (mid.astype(F32) + gate * update.T).astype(BF16)
+        out = (mid.astype(F32) + gate_ref[u] * update.T).astype(BF16)
         out_ref[u] = out[:64]
         out_ref[16 + u] = out[64:]
 
 
-def final(tri, mid, wt, wg):
+def final(tri, mid, wt, gate):
     return pl.pallas_call(
         final_kernel,
         out_shape=jax.ShapeDtypeStruct((32, 64, 128), BF16),
         compiler_params=params(16),
         name="pair_final",
-    )(tri, mid, wt, wg)
+    )(tri, mid, wt, gate)
 
 
 def copy_kernel(in_ref, out_ref):
@@ -440,6 +456,36 @@
         concat_axis=0,
         tiled=True,
     )
+    live_plane = row_live[:, None] * col_live[None, :]
+    inv = 1.0 / jnp.maximum(jnp.sum(seq_live) * live_plane, 1.0)
+
+    def pairs(a):
+        return a.reshape(2, 16, 64).transpose(1, 0, 2).reshape(2, 8, 1, 128)
+
+    weight = outer_output.reshape(32, 2, 16, 128).transpose(3, 2, 1, 0).reshape(128, 1024)
+    win = attention_input_weight.reshape(256, 1024).T
+    wp = tri_project.reshape(128, 512).T
+    wt = tri_output.T
+    wl = jnp.tile(outer_factor_weight[:, 0], (1, 4))
+    wr = outer_factor_weight[:, 1].T
+    live_cols = jnp.broadcast_to(res_live[:, None], (512, 128))
+    blocks, weight, wp, wt, inv, live_plane, win, wl, wr, live_cols, my_seqs = (
+        lax.optimization_barrier(
+            (
+                blocks,
+                weight,
+                wp,
+                wt,
+                pairs(inv),
+                pairs(live_plane),
+                win,
+                wl,
+                wr,
+                live_cols,
+                my_seqs,
+            )
+        )
+    )
     outgoing, blocks = lax.optimization_barrier((alignment.reshape(16, 5, 32, 256), blocks))
     bias_plane = plane(blocks)
     own = [bias_plane] + [
@@ -447,19 +493,6 @@
     ]
     other = [lax.ppermute(b, "core", swap) for b in own]
     sequences = lax.all_to_all(outgoing, ROW, split_axis=0, concat_axis=0, tiled=True)
-    live_plane = row_live[:, None] * col_live[None, :]
-    inv = 1.0 / jnp.maximum(jnp.sum(seq_live) * live_plane, 1.0)
-
-    def pairs(a):
-        return a.reshape(2, 16, 64).transpose(1, 0, 2).reshape(2, 8, 1, 128)
-
-    weight = outer_output.reshape(32, 2, 16, 128).transpose(3, 2, 1, 0).reshape(128, 1024)
-    win = attention_input_weight.reshape(256, 1024).T
-    wp = tri_project.reshape(128, 512).T
-    wt = tri_output.T
-    sequences, weight, wp, wt, inv, live_plane, win = lax.optimization_barrier(
-        (sequences, weight, wp, wt, pairs(inv), pairs(live_plane), win)
-    )
     out_seq, factors = attention(
         jnp.stack([core, lax.axis_index("y")]),
         my_seqs,
@@ -467,10 +500,10 @@
         sequences,
         win,
         attention_output_weight,
-        jnp.tile(outer_factor_weight[:, 0], (1, 4)),
-        outer_factor_weight[:, 1].T,
+        wl,
+        wr,
         res_live.reshape(1, 512),
-        jnp.broadcast_to(res_live[:, None], (512, 128)),
+        live_cols,
     )
     factors = lax.all_to_all(
         factors.reshape(128, 80, 128), ALL, split_axis=0, concat_axis=0, tiled=True
@@ -499,10 +532,9 @@
     alignment_output = copied(alignment_output)
     tri = tri.reshape(16, 2, 128, 128).transpose(2, 1, 0, 3)
     blocks = lax.all_to_all(tri, ALL, split_axis=0, concat_axis=0, tiled=True)
-    combined = lax.all_to_all(triangle(blocks), ALL, split_axis=0, concat_axis=0, tiled=True)
-    pair_output_state = final(
-        combined.transpose(1, 0, 2), mid.reshape(32, 64, 128), wt, tri_gate
-    )
+    product, mid = lax.optimization_barrier((triangle(blocks), mid.reshape(32, 64, 128)))
+    combined = lax.all_to_all(product, ALL, split_axis=0, concat_axis=0, tiled=True)
+    pair_output_state = final(combined.transpose(1, 0, 2), mid, wt, gates(mid, tri_gate))
     return (alignment_output, pair_output_state)
 
 

time: 213 us -> 200 us (0.939)
  blocking collectives: 85.5 us -> 64.7 us
  waiting for transfers between devices: 36.6 us -> 49.4 us
  Pallas kernels: 51.6 us -> 39.9 us
  starting transfers between devices: 21.9 us -> 30.7 us
    all_to_all x1 -> x0, blocking collectives: 20.9 us -> none  [body(): lax.all_to_all(pair_bias(pairwise, bias_project.T).reshape(32, 64, 128),...]
    all_to_all x1 -> x2, starting transfers between devices: 4.72 us -> 14.3 us  [the longest x1 9.56 us: body(): lax.all_to_all(pair_bias(pairwise, bias_project.T).reshape(32, 64, 128),...]
    pallas_call x1, Pallas kernels: 27.3 us -> 20.3 us  [attention(): pl.pallas_call(attention_kernel, grid=(count,), in_specs=[smem, smem, *(w...]
    all_to_all x1 -> x2, waiting for transfers between devices: 12.8 us -> 19.3 us  [the longest x1 11.6 us: body(): lax.all_to_all(product, ALL, split_axis=0, concat_axis=0, tiled=True)]
    all_to_all x1, waiting for transfers between devices: 0.58 us -> 5.84 us  [body(): lax.all_to_all(out_seq, ROW, split_axis=0, concat_axis=0, tiled=True)]
    pallas_call x1 -> x2, Pallas kernels: 15 us -> 10.7 us  [the longest x1 9.55 us: outer_update(): pl.pallas_call(outer_kernel, in_specs=[pl.BlockSpec(memory_space=pltpu.SM...]
    unnamed x31 -> x37, local copies, waits for them, and re-layouts: 7.9 us -> 6.03 us
  transfers between devices with their start and end apart: 11 -> 12, of which waited for: 4 -> 6; matrix products, arithmetic and copies ran while one was open for 4% -> 3% of each run, Pallas kernels for 8% -> 6%
where the time goes in v5:
time: 200 us
  blocking collectives  64.7 us (32%)
  waiting for transfers between devices  49.4 us (25%)
  Pallas kernels  39.9 us (20%)
  starting transfers between devices  30.7 us (15%)
  local copies, waits for them, and re-layouts  12.6 us (6%)
    all_to_all x1, blocking collectives, body(): lax.all_to_all(factors.reshape(128, 80, 128), ALL, split_axis=0, concat_a...  41.7 us
    ppermute x3, waiting for transfers between devices, body(): lax.ppermute(bias_plane, 'y', [(i, (i + d) % 4) for i in range(4)])  23.4 us
    all_to_all x1, blocking collectives, body(): blocks = lax.all_to_all(tri, ALL, split_axis=0, concat_axis=0, tiled=True)  23 us
    pallas_call x1, Pallas kernels, attention(): pl.pallas_call(attention_kernel, grid=(count,), in_specs=[smem, smem, *(w...  20.3 us
    all_to_all x1, waiting for transfers between devices, body(): lax.all_to_all(product, ALL, split_axis=0, concat_axis=0, tiled=True)  11.6 us
    all_to_all x1, starting transfers between devices, body(): lax.all_to_all(pair_bias(pairwise, bias_project.T).reshape(32, 64, 128),...  9.56 us
    pallas_call x1, Pallas kernels, outer_update(): pl.pallas_call(outer_kernel, in_specs=[pl.BlockSpec(memory_space=pltpu.SM...  9.55 us
    all_to_all x1, waiting for transfers between devices, body(): lax.all_to_all(pair_bias(pairwise, bias_project.T).reshape(32, 64, 128),...  7.67 us
  transfers between devices with their start and end apart: 12, of which 6 were waited for; matrix products, arithmetic and copies ran while one was open for 3% of the time, Pallas kernels for 6%

profile of v5, /device:TPU:1, one launch (start us, length us, event | category | flops | bytes accessed | tf_op | source)
XLA Modules:
  0.0 199.6 jit_solution(16120180112515033513)
XLA Ops:
  0.6 0.0 copy-start
  0.6 1.0 copy-done
  1.7 0.7 copy-done.7
  2.4 2.1 %pair_bias.1 = bf16[8,2,2,64,128]{4,3,2,1,0:T(8,128)(2,1)} custom-call(bf16[32,64,128]{2,1,0:T(8,128)(2,1)S(1)} %copy-done, bf16[8,128]{1,0:T(8,128)(2,1)S(1)} %bitcast.59), custom_call_target="tpu_custom_call" | custom-call | tf_op jit(solution)/shard_map/pair_bias/pallas_call | solution.py:61
  4.5 9.6 %all-to-all-start = ((bf16[32,64,128]{2,1,0:T(8,128)(2,1)}), bf16[32,64,128]{2,1,0:T(8,128)(2,1)S(1)}, u32[]{:S(2)}, u32[]{:S(2)}) async-start(bf16[32,64,128]{2,1,0:T(8,128)(2,1)} %bitcast.3), calls=%async_computation | async-start | bytes 1048576 | tf_op jit(solution)/shard_map/all_to_all | solution.py:452
  14.1 0.1 dynamic_slice.10
  14.2 0.1 dynamic_slice.9
  14.3 0.1 mul.73
  14.4 0.1 mul.80
  14.5 0.1 copy.41
  14.5 0.1 mul.75
  14.6 0.1 mul.76
  14.7 0.7 copy.40
  15.4 0.1 copy.39
  15.6 0.8 copy.38
  16.4 0.3 copy.42
  16.7 0.1 dynamic_slice.11.seq_ref
  16.8 0.6 convert_reduce_fusion
  17.4 0.6 maximum_divide_fusion
  18.1 7.7 %all-to-all-done.in_ref = bf16[32,64,128]{2,1,0:T(8,128)(2,1)S(1)} async-done(((bf16[32,64,128]{2,1,0:T(8,128)(2,1)}), bf16[32,64,128]{2,1,0:T(8,128)(2,1)S(1)}, u32[]{:S(2)}, u32[]{:S(2)}) %all-to-all-start) | async-done | bytes 524320 | tf_op jit(solution)/shard_map/all_to_all | solution.py:452
  25.8 0.6 tile.11
  26.4 0.1 broadcast_in_dim.2.live_col_ref
  26.5 0.0 copy-start.4
  26.5 4.5 %all-to-all-start.1 = ((bf16[16,5,32,256]{3,2,1,0:T(8,128)(2,1)}), bf16[16,5,32,256]{3,2,1,0:T(8,128)(2,1)S(1)}, u32[]{:S(2)}, u32[]{:S(2)}) async-start(bf16[16,5,32,256]{3,2,1,0:T(8,128)(2,1)} %bitcast.64), calls=%async_computation.1 | async-start | bytes 2621440 | tf_op jit(solution)/shard_map/all_to_all | solution.py:495
  31.0 0.5 bias_plane.1.own0_ref
  31.5 2.8 %collective-permute-start.2 = (bf16[4,128,512]{2,1,0:T(8,128)(2,1)S(1)}, bf16[4,128,512]{2,1,0:T(8,128)(2,1)S(1)}, u32[]{:S(2)}, u32[]{:S(2)}) collective-permute-start(bf16[4,128,512]{2,1,0:T(8,128)(2,1)S(1)} %bias_plane.1.own0_ref), channel_id=1, source_target_pairs={{0,3},{1,0},{2,1},{3,2},{4,7},{5,4},{6,5},{7,6},{8,11},{9,8},{10,9... | collective-permute-start | bytes 1572872 | tf_op jit(solution)/shard_map/ppermute | solution.py:492
  34.3 0.3 collective-permute-start.1
  34.6 0.7 collective-permute-start
  35.3 1.1 collective-permute-start.3
  36.4 20.1 %collective-permute-done.2.own3_ref = bf16[4,128,512]{2,1,0:T(8,128)(2,1)S(1)} collective-permute-done((bf16[4,128,512]{2,1,0:T(8,128)(2,1)S(1)}, bf16[4,128,512]{2,1,0:T(8,128)(2,1)S(1)}, u32[]{:S(2)}, u32[]{:S(2)}) %collective-permute-start.2) | collective-permute-done | bytes 524320 | tf_op jit(solution)/shard_map/ppermute | solution.py:492
  56.5 1.2 collective-permute-start.6
  57.7 0.0 collective-permute-done.1.own2_ref
  57.7 0.0 collective-permute-start.5
  57.7 3.3 %collective-permute-done.own1_ref = bf16[4,128,512]{2,1,0:T(8,128)(2,1)} collective-permute-done((bf16[4,128,512]{2,1,0:T(8,128)(2,1)S(1)}, bf16[4,128,512]{2,1,0:T(8,128)(2,1)}, u32[]{:S(2)}, u32[]{:S(2)}) %collective-permute-start) | collective-permute-done | bytes 524320 | tf_op jit(solution)/shard_map/ppermute | solution.py:492
  61.0 0.5 collective-permute-start.4
  61.5 0.1 pad_add_fusion.place_ref
  61.5 0.9 copy.43.wl_ref
  62.5 0.0 collective-permute-done.3.other0_ref
  62.5 0.0 collective-permute-done.6.other3_ref
  62.5 0.8 collective-permute-done.4.other1_ref
  63.4 20.3 %row_attention.1 = (bf16[16,5,32,256]{3,2,1,0:T(8,128)(2,1)S(1)}, bf16[8,2,8,5,16,128]{5,4,3,2,1,0:T(8,128)(2,1)S(1)}) custom-call(s32[2]{0:T(128)S(1)} %pad_add_fusion.place_ref, f32[5]{0:T(128)S(1)} %dynamic_slice.11.seq_ref, bf16[4,128,512]{2,1,0:T(8,128)(2,1)S(1)} %bias_plane.1.own0_ref, bf16[4,128,512]{2,1,0:T(8,128)(2,1)} %collective-permute-done.own1_ref, ...), custom_call_target="tpu_custom_call" | custom-call | tf_op jit(solution)/shard_map/row_attention/pallas_call | solution.py:222
  83.6 0.0 copy-start.2
  83.6 41.7 %all_to_all.30 = bf16[128,80,128]{2,1,0:T(8,128)(2,1)S(1)} all-to-all(bf16[128,80,128]{2,1,0:T(8,128)(2,1)S(1)} %bitcast.49), channel_id=1, replica_groups=mesh['x'=4,'zl'=2,'core'=2,'zh'=2,'y'=4] {'x','zl','core','zh','y'}, dimensions={0} | all-to-all | bytes 5242880 | tf_op jit(solution)/shard_map/all_to_all | solution.py:508
  125.3 1.3 fusion
  126.6 0.4 copy.53
  127.0 1.6 collective-permute-start.7
  128.6 3.8 %all-to-all-start.3 = ((bf16[16,5,32,256]{3,2,1,0:T(8,128)(2,1)}), bf16[16,5,32,256]{3,2,1,0:T(8,128)(2,1)S(1)}, u32[]{:S(2)}, u32[]{:S(2)}) async-start(bf16[16,5,32,256]{3,2,1,0:T(8,128)(2,1)} %copy-done.2), calls=%async_computation.3 | async-start | bytes 2621440 | tf_op jit(solution)/shard_map/all_to_all | solution.py:516
  132.4 0.1 copy.44.w_ref
  132.6 0.0 copy-start.1
  132.6 1.7 copy.54
  134.3 0.0 collective-permute-done.7.other_ref
  134.4 9.6 %outer_update.1 = (bf16[4,8,64,128]{3,2,1,0:T(8,128)(2,1)S(1)}, bf16[2,8,256,128]{3,2,1,0:T(8,128)(2,1)S(1)}) custom-call(s32[1]{0:T(128)} %bitcast.core_ref, bf16[640,1024]{1,0:T(8,128)(2,1)S(1)} %bitcast.47, bf16[640,1024]{1,0:T(8,128)(2,1)S(1)} %bitcast.46, bf16[640,1024]{1,0:T(8,128)(2,1)} %collective-permute-done.7.other_ref, ...), custom_call_target="tpu_custom_call" | custom-call | tf_op jit(solution)/shard_map/outer_update/pallas_call | solution.py:323
  143.9 1.0 copy-done.3
  144.9 5.8 %all-to-all-done.3 = bf16[16,5,32,256]{3,2,1,0:T(8,128)(2,1)S(1)} async-done(((bf16[16,5,32,256]{3,2,1,0:T(8,128)(2,1)}), bf16[16,5,32,256]{3,2,1,0:T(8,128)(2,1)S(1)}, u32[]{:S(2)}, u32[]{:S(2)}) %all-to-all-start.3) | async-done | bytes 1310752 | tf_op jit(solution)/shard_map/all_to_all | solution.py:516
  150.7 1.9 copy.55
  152.6 23.0 %all_to_all.31.in_ref = bf16[128,2,16,128]{3,2,1,0:T(8,128)(2,1)S(1)} all-to-all(bf16[128,2,16,128]{3,2,1,0:T(8,128)(2,1)S(1)} %bitcast.63), channel_id=1, replica_groups=mesh['x'=4,'zl'=2,'core'=2,'zh'=2,'y'=4] {'x','zl','core','zh','y'}, dimensions={0} | all-to-all | bytes 2097152 | tf_op jit(solution)/shard_map/all_to_all | solution.py:534
  175.6 3.7 %triangle.1 = bf16[128,16,128]{2,1,0:T(8,128)(2,1)} custom-call(bf16[128,2,16,128]{3,2,1,0:T(8,128)(2,1)S(1)} %all_to_all.31.in_ref), custom_call_target="tpu_custom_call" | custom-call | tf_op jit(solution)/shard_map/triangle/pallas_call | solution.py:367
  179.4 4.7 %all-to-all-start.5 = ((bf16[128,16,128]{2,1,0:T(8,128)(2,1)}), bf16[128,16,128]{2,1,0:T(8,128)(2,1)S(1)}, u32[]{:S(2)}, u32[]{:S(2)}) async-start(bf16[128,16,128]{2,1,0:T(8,128)(2,1)} %triangle.1), calls=%async_computation.5 | async-start | bytes 1048576 | tf_op jit(solution)/shard_map/all_to_all | solution.py:536
  184.1 0.0 copy-start.6
  184.1 1.1 copied.1
  185.2 1.2 pair_gate.1.gate_ref
  186.4 11.6 %all-to-all-done.5 = bf16[128,16,128]{2,1,0:T(8,128)(2,1)S(1)} async-done(((bf16[128,16,128]{2,1,0:T(8,128)(2,1)}), bf16[128,16,128]{2,1,0:T(8,128)(2,1)S(1)}, u32[]{:S(2)}, u32[]{:S(2)}) %all-to-all-start.5) | async-done | bytes 524320 | tf_op jit(solution)/shard_map/all_to_all | solution.py:536
  198.0 0.1 copy.56
  198.2 1.4 pair_final.1
  (30 shorter events, 0.1 us)
Async XLA Ops:
  0.6 1.0 copy-start
  1.7 0.7 copy-start.7
  2.4 11.7 %copy-start.15 = (s32[512]{0:T(512)S(1)}, s32[512]{0:T(512)}, u32[]{:S(2)}) copy-start(s32[512]{0:T(512)} %param.14) | copy-start | bytes 6148
  2.4 12.1 %copy-start.14 = (s32[640]{0:T(1024)S(1)}, s32[640]{0:T(1024)}, u32[]{:S(2)}) copy-start(s32[640]{0:T(1024)} %param.15) | copy-start | bytes 7684
  2.4 12.3 %copy-start.12 = (bf16[128,128]{1,0:T(8,128)(2,1)S(1)}, bf16[128,128]{1,0:T(8,128)(2,1)}, u32[]{:S(2)}) copy-start(bf16[128,128]{1,0:T(8,128)(2,1)} %param.23) | copy-start | bytes 98308
  2.4 13.1 %copy-start.11 = (bf16[128,4,128]{2,1,0:T(4,128)(2,1)S(1)}, bf16[128,4,128]{2,1,0:T(4,128)(2,1)}, u32[]{:S(2)}) copy-start(bf16[128,4,128]{2,1,0:T(4,128)(2,1)} %param.21) | copy-start | bytes 393220
  2.4 13.2 %copy-start.10 = (bf16[1024,128]{1,0:T(8,128)(2,1)S(1)}, bf16[1024,128]{1,0:T(8,128)(2,1)}, u32[]{:S(2)}) copy-start(bf16[1024,128]{1,0:T(8,128)(2,1)} %param.20) | copy-start | bytes 786436
  2.4 14.0 %copy-start.9 = (bf16[256,4,256]{2,1,0:T(4,128)(2,1)S(1)}, bf16[256,4,256]{2,1,0:T(4,128)(2,1)}, u32[]{:S(2)}) copy-start(bf16[256,4,256]{2,1,0:T(4,128)(2,1)} %param.16) | copy-start | bytes 1572868
  4.5 13.6 %copy-start.13 = (bf16[256,2,32]{0,2,1:T(8,128)(2,1)S(1)}, bf16[256,2,32]{0,2,1:T(8,128)(2,1)}, u32[]{:S(2)}) copy-start(bf16[256,2,32]{0,2,1:T(8,128)(2,1)} %param.19) | copy-start | bytes 98308
  4.5 21.3 %all-to-all-start = ((bf16[32,64,128]{2,1,0:T(8,128)(2,1)}), bf16[32,64,128]{2,1,0:T(8,128)(2,1)S(1)}, u32[]{:S(2)}, u32[]{:S(2)}) async-start(bf16[32,64,128]{2,1,0:T(8,128)(2,1)} %bitcast.3), calls=%async_computation | async-start | bytes 1048576 | tf_op jit(solution)/shard_map/all_to_all | solution.py:452
  26.5 36.8 %copy-start.4 = (bf16[256,256]{1,0:T(8,128)(2,1)S(1)}, bf16[256,256]{1,0:T(8,128)(2,1)}, u32[]{:S(2)}) copy-start(bf16[256,256]{1,0:T(8,128)(2,1)} %wo_ref.1) | copy-start | bytes 393220
  26.5 36.8 %all-to-all-start.1 = ((bf16[16,5,32,256]{3,2,1,0:T(8,128)(2,1)}), bf16[16,5,32,256]{3,2,1,0:T(8,128)(2,1)S(1)}, u32[]{:S(2)}, u32[]{:S(2)}) async-start(bf16[16,5,32,256]{3,2,1,0:T(8,128)(2,1)} %bitcast.64), calls=%async_computation.1 | async-start | bytes 2621440 | tf_op jit(solution)/shard_map/all_to_all | solution.py:495
  31.5 25.0 %collective-permute-start.2 = (bf16[4,128,512]{2,1,0:T(8,128)(2,1)S(1)}, bf16[4,128,512]{2,1,0:T(8,128)(2,1)S(1)}, u32[]{:S(2)}, u32[]{:S(2)}) collective-permute-start(bf16[4,128,512]{2,1,0:T(8,128)(2,1)S(1)} %bias_plane.1.own0_ref), channel_id=1, source_target_pairs={{0,3},{1,0},{2,1},{3,2},{4,7},{5,4},{6,5},{7,6},{8,11},{9,8},{10,9... | collective-permute-start | bytes 1572872 | tf_op jit(solution)/shard_map/ppermute | solution.py:492
  34.3 23.4 %collective-permute-start.1 = (bf16[4,128,512]{2,1,0:T(8,128)(2,1)S(1)}, bf16[4,128,512]{2,1,0:T(8,128)(2,1)}, u32[]{:S(2)}, u32[]{:S(2)}) collective-permute-start(bf16[4,128,512]{2,1,0:T(8,128)(2,1)S(1)} %bias_plane.1.own0_ref), channel_id=1, source_target_pairs={{0,2},{1,3},{2,0},{3,1},{4,6},{5,7},{6,4},{7,5},{8,10},{9,11},{10,... | collective-permute-start | bytes 1572872 | tf_op jit(solution)/shard_map/ppermute | solution.py:492
  34.6 26.3 %collective-permute-start = (bf16[4,128,512]{2,1,0:T(8,128)(2,1)S(1)}, bf16[4,128,512]{2,1,0:T(8,128)(2,1)}, u32[]{:S(2)}, u32[]{:S(2)}) collective-permute-start(bf16[4,128,512]{2,1,0:T(8,128)(2,1)S(1)} %bias_plane.1.own0_ref), channel_id=1, source_target_pairs={{0,1},{1,2},{2,3},{3,0},{4,5},{5,6},{6,7},{7,4},{8,9},{9,10},{10,1... | collective-permute-start | bytes 1572872 | tf_op jit(solution)/shard_map/ppermute | solution.py:492
  35.3 27.2 %collective-permute-start.3 = (bf16[4,128,512]{2,1,0:T(8,128)(2,1)S(1)}, bf16[4,128,512]{2,1,0:T(8,128)(2,1)}, u32[]{:S(2)}, u32[]{:S(2)}) collective-permute-start(bf16[4,128,512]{2,1,0:T(8,128)(2,1)S(1)} %bias_plane.1.own0_ref), channel_id=1, source_target_pairs={{0,8},{8,0},{1,9},{9,1},{2,10},{10,2},{3,11},{11,3},{4,12},{12,4},... | collective-permute-start | bytes 1572872 | tf_op jit(solution)/shard_map/ppermute | solution.py:494
  56.5 6.0 %collective-permute-start.6 = (bf16[4,128,512]{2,1,0:T(8,128)(2,1)S(1)}, bf16[4,128,512]{2,1,0:T(8,128)(2,1)}, u32[]{:S(2)}, u32[]{:S(2)}) collective-permute-start(bf16[4,128,512]{2,1,0:T(8,128)(2,1)S(1)} %collective-permute-done.2.own3_ref), channel_id=1, source_target_pairs={{0,8},{8,0},{1,9},{9,1},{2,10},{10,2},{3,11},{11,3},{4,12},{12,4},... | collective-permute-start | bytes 1572872 | tf_op jit(solution)/shard_map/ppermute | solution.py:494
  57.7 4.9 %collective-permute-start.5 = (bf16[4,128,512]{2,1,0:T(8,128)(2,1)}, bf16[4,128,512]{2,1,0:T(8,128)(2,1)}, u32[]{:S(2)}, u32[]{:S(2)}) collective-permute-start(bf16[4,128,512]{2,1,0:T(8,128)(2,1)} %collective-permute-done.1.own2_ref), channel_id=1, source_target_pairs={{0,8},{8,0},{1,9},{9,1},{2,10},{10,2},{3,11},{11,3},{4,12},{12,4},... | collective-permute-start | bytes 1572872 | tf_op jit(solution)/shard_map/ppermute | solution.py:494
  61.0 2.4 %collective-permute-start.4 = (bf16[4,128,512]{2,1,0:T(8,128)(2,1)}, bf16[4,128,512]{2,1,0:T(8,128)(2,1)}, u32[]{:S(2)}, u32[]{:S(2)}) collective-permute-start(bf16[4,128,512]{2,1,0:T(8,128)(2,1)} %collective-permute-done.own1_ref), channel_id=1, source_target_pairs={{0,8},{8,0},{1,9},{9,1},{2,10},{10,2},{3,11},{11,3},{4,12},{12,4},... | collective-permute-start | bytes 1572872 | tf_op jit(solution)/shard_map/ppermute | solution.py:494
  83.6 41.7 %copy-start.2 = (bf16[16,5,32,256]{3,2,1,0:T(8,128)(2,1)}, bf16[16,5,32,256]{3,2,1,0:T(8,128)(2,1)S(1)}, u32[]{:S(2)}) copy-start(bf16[16,5,32,256]{3,2,1,0:T(8,128)(2,1)S(1)} %get-tuple-element.41) | copy-start | bytes 3932164
  127.0 5.4 %copy-start.8 = (bf16[128,16,2,32]{0,3,2,1:T(8,128)(2,1)S(1)}, bf16[128,16,2,32]{0,3,2,1:T(8,128)(2,1)}, u32[]{:S(2)}) copy-start(bf16[128,16,2,32]{0,3,2,1:T(8,128)(2,1)} %copy.38) | copy-start | bytes 786436
  127.0 7.4 %collective-permute-start.7 = (bf16[640,1024]{1,0:T(8,128)(2,1)S(1)}, bf16[640,1024]{1,0:T(8,128)(2,1)}, u32[]{:S(2)}, u32[]{:S(2)}) collective-permute-start(bf16[640,1024]{1,0:T(8,128)(2,1)S(1)} %bitcast.45), channel_id=1, source_target_pairs={{0,8},{8,0},{1,9},{9,1},{2,10},{10,2},{3,11},{11,3},{4,12},{12,4},... | collective-permute-start | bytes 3932168 | tf_op jit(solution)/shard_map/ppermute | solution.py:514
  128.6 22.1 %all-to-all-start.3 = ((bf16[16,5,32,256]{3,2,1,0:T(8,128)(2,1)}), bf16[16,5,32,256]{3,2,1,0:T(8,128)(2,1)S(1)}, u32[]{:S(2)}, u32[]{:S(2)}) async-start(bf16[16,5,32,256]{3,2,1,0:T(8,128)(2,1)} %copy-done.2), calls=%async_computation.3 | async-start | bytes 2621440 | tf_op jit(solution)/shard_map/all_to_all | solution.py:516
  132.6 1.8 copy-start.1
  143.9 1.0 copy-start.3
  179.4 18.7 %all-to-all-start.5 = ((bf16[128,16,128]{2,1,0:T(8,128)(2,1)}), bf16[128,16,128]{2,1,0:T(8,128)(2,1)S(1)}, u32[]{:S(2)}, u32[]{:S(2)}) async-start(bf16[128,16,128]{2,1,0:T(8,128)(2,1)} %triangle.1), calls=%async_computation.5 | async-start | bytes 1048576 | tf_op jit(solution)/shard_map/all_to_all | solution.py:536
  184.1 1.2 copy-start.6
  185.2 12.9 %copy-start.5 = (bf16[128,128]{0,1:T(8,128)(2,1)S(1)}, bf16[128,128]{0,1:T(8,128)(2,1)}, u32[]{:S(2)}) copy-start(bf16[128,128]{0,1:T(8,128)(2,1)} %copy.40) | copy-start | bytes 98308

commit v6 on v5

--- a/solution.py
+++ b/solution.py
@@ -328,7 +328,7 @@
             jax.ShapeDtypeStruct((2, 8, 256, 128), BF16),
         ],
         scratch_shapes=[pltpu.VMEM((1024, total), BF16), pltpu.VMEM((4, 1024, 512), BF16)],
-        compiler_params=params(32),
+        compiler_params=params(20),
         name="outer_update",
     )(core, left, own, other, weight, inv, live_plane, pairwise, wp)
 
@@ -486,11 +486,16 @@
             )
         )
     )
-    outgoing, blocks = lax.optimization_barrier((alignment.reshape(16, 5, 32, 256), blocks))
-    bias_plane = plane(blocks)
-    own = [bias_plane] + [
-        lax.ppermute(bias_plane, "y", [(i, (i + d) % 4) for i in range(4)]) for d in (1, 2, 3)
-    ]
+    outgoing, bias_plane = lax.optimization_barrier(
+        (alignment.reshape(16, 5, 32, 256), plane(blocks))
+    )
+    up, down = ([(i, (i + d) % 4) for i in range(4)] for d in (1, 3))
+    left_plane = lax.ppermute(bias_plane, "y", up)
+    right_plane = lax.ppermute(bias_plane, "y", down)
+    far_plane = jnp.concatenate(
+        [lax.ppermute(left_plane[:2], "y", up), lax.ppermute(right_plane[2:], "y", down)], axis=0
+    )
+    own = [bias_plane, left_plane, far_plane, right_plane]
     other = [lax.ppermute(b, "core", swap) for b in own]
     sequences = lax.all_to_all(outgoing, ROW, split_axis=0, concat_axis=0, tiled=True)
     out_seq, factors = attention(
@@ -528,9 +533,9 @@
         pairwise.reshape(4, 8, 64, 128),
         wp,
     )
+    tri = tri.reshape(16, 2, 128, 128).transpose(2, 1, 0, 3)
     tri, alignment_output = lax.optimization_barrier((tri, alignment_output))
     alignment_output = copied(alignment_output)
-    tri = tri.reshape(16, 2, 128, 128).transpose(2, 1, 0, 3)
     blocks = lax.all_to_all(tri, ALL, split_axis=0, concat_axis=0, tiled=True)
     product, mid = lax.optimization_barrier((triangle(blocks), mid.reshape(32, 64, 128)))
     combined = lax.all_to_all(product, ALL, split_axis=0, concat_axis=0, tiled=True)

time: 200 us -> 194 us (0.970)
  waiting for transfers between devices: 49.4 us -> 32.6 us
  local copies, waits for them, and re-layouts: 12.6 us -> 18.3 us
  starting transfers between devices: 30.7 us -> 35.4 us
    ppermute x3 -> x4, waiting for transfers between devices: 23.4 us -> 8.32 us  [the longest x1 6.42 us: body(): left_plane = lax.ppermute(bias_plane, 'y', up)]
    unnamed x37 -> x52, local copies, waits for them, and re-layouts: 6.03 us -> 10.3 us
    ppermute x4, starting transfers between devices: 2.73 us -> 5.27 us  [body(): other = [lax.ppermute(b, 'core', swap) for b in own]]
    ppermute x3 -> x4, starting transfers between devices: 3.84 us -> 5.68 us  [the longest x1 2.72 us: body(): lax.ppermute(right_plane[2:], 'y', down)]
  transfers between devices with their start and end apart: 12 -> 13, of which waited for: 6 -> 5; matrix products, arithmetic and copies ran while one was open for 3% -> 6% of each run, Pallas kernels for 6% -> 6%
where the time goes in v6:
time: 194 us; the launch traced here: 193 us
  blocking collectives  63.5 us (33%)
  Pallas kernels  39.7 us (20%)
  starting transfers between devices  35.4 us (18%)
  waiting for transfers between devices  32.6 us (17%)
  local copies, waits for them, and re-layouts  18.3 us (9%)
  other arithmetic  2.48 us (1%)
    all_to_all x1, blocking collectives, body(): lax.all_to_all(factors.reshape(128, 80, 128), ALL, split_axis=0, concat_a...  40.5 us
    all_to_all x1, blocking collectives, body(): blocks = lax.all_to_all(tri, ALL, split_axis=0, concat_axis=0, tiled=True)  23 us
    pallas_call x1, Pallas kernels, attention(): pl.pallas_call(attention_kernel, grid=(count,), in_specs=[smem, smem, *(w...  20.1 us
    all_to_all x1, waiting for transfers between devices, body(): lax.all_to_all(product, ALL, split_axis=0, concat_axis=0, tiled=True)  11.6 us
    unnamed x52, local copies, waits for them, and re-layouts  10.3 us
    all_to_all x1, starting transfers between devices, body(): lax.all_to_all(pair_bias(pairwise, bias_project.T).reshape(32, 64, 128),...  9.56 us
    pallas_call x1, Pallas kernels, outer_update(): pl.pallas_call(outer_kernel, in_specs=[pl.BlockSpec(memory_space=pltpu.SM...  9.56 us
    all_to_all x1, waiting for transfers between devices, body(): lax.all_to_all(pair_bias(pairwise, bias_project.T).reshape(32, 64, 128),...  6.58 us
  transfers between devices with their start and end apart: 13, of which 5 were waited for; matrix products, arithmetic and copies ran while one was open for 6% of the time, Pallas kernels for 6%

profile of v6, /device:TPU:1, one launch (start us, length us, event | category | flops | bytes accessed | tf_op | source)
XLA Modules:
  0.0 193.0 jit_solution(1015120022206127229)
XLA Ops:
  0.6 0.0 copy-start
  0.6 1.0 copy-done
  1.7 0.7 copy-done.12
  2.4 2.1 %pair_bias.1 = bf16[8,2,2,64,128]{4,3,2,1,0:T(8,128)(2,1)} custom-call(bf16[32,64,128]{2,1,0:T(8,128)(2,1)S(1)} %copy-done, bf16[8,128]{1,0:T(8,128)(2,1)S(1)} %bitcast.59), custom_call_target="tpu_custom_call" | custom-call | tf_op jit(solution)/shard_map/pair_bias/pallas_call | solution.py:61
  4.5 9.6 %all-to-all-start = ((bf16[32,64,128]{2,1,0:T(8,128)(2,1)}), bf16[32,64,128]{2,1,0:T(8,128)(2,1)S(1)}, u32[]{:S(2)}, u32[]{:S(2)}) async-start(bf16[32,64,128]{2,1,0:T(8,128)(2,1)} %bitcast.3), calls=%async_computation | async-start | bytes 1048576 | tf_op jit(solution)/shard_map/all_to_all | solution.py:452
  14.1 0.1 dynamic_slice.10
  14.2 0.1 dynamic_slice.9
  14.3 0.1 mul.73
  14.4 0.1 mul.80
  14.5 0.1 copy.41
  14.5 0.1 mul.75
  14.6 0.1 mul.76
  14.7 0.7 copy.40
  15.4 0.1 copy.39
  15.6 0.8 copy.38
  16.4 0.3 copy.42
  16.7 0.6 dynamic_slice.11.seq_ref
  17.3 0.6 convert_reduce_fusion
  17.9 1.3 maximum_divide_fusion
  19.2 6.6 %all-to-all-done.in_ref = bf16[32,64,128]{2,1,0:T(8,128)(2,1)S(1)} async-done(((bf16[32,64,128]{2,1,0:T(8,128)(2,1)}), bf16[32,64,128]{2,1,0:T(8,128)(2,1)S(1)}, u32[]{:S(2)}, u32[]{:S(2)}) %all-to-all-start) | async-done | bytes 524320 | tf_op jit(solution)/shard_map/all_to_all | solution.py:452
  25.8 0.6 tile.11
  26.4 0.8 broadcast_in_dim.2.live_col_ref
  27.2 0.5 bias_plane.1.own0_ref
  27.7 1.4 collective-permute-start
  29.1 1.5 collective-permute-start.2
  30.6 4.7 %all-to-all-start.1 = ((bf16[16,5,32,256]{3,2,1,0:T(8,128)(2,1)}), bf16[16,5,32,256]{3,2,1,0:T(8,128)(2,1)S(1)}, u32[]{:S(2)}, u32[]{:S(2)}) async-start(bf16[16,5,32,256]{3,2,1,0:T(8,128)(2,1)} %bitcast.64), calls=%async_computation.1 | async-start | bytes 2621440 | tf_op jit(solution)/shard_map/all_to_all | solution.py:500
  35.3 6.4 %collective-permute-done.own1_ref = bf16[4,128,512]{2,1,0:T(8,128)(2,1)S(1)} collective-permute-done((bf16[4,128,512]{2,1,0:T(8,128)(2,1)S(1)}, bf16[4,128,512]{2,1,0:T(8,128)(2,1)S(1)}, u32[]{:S(2)}, u32[]{:S(2)}) %collective-permute-start) | collective-permute-done | bytes 524320 | tf_op jit(solution)/shard_map/ppermute | solution.py:493
  41.8 0.1 collective-permute-start.1
  41.9 2.7 %collective-permute-start.3 = (bf16[2,128,512]{2,1,0:T(8,128)(2,1)S(1)}, bf16[2,128,512]{2,1,0:T(8,128)(2,1)S(1)}, u32[]{:S(2)}, u32[]{:S(2)}) collective-permute-start(bf16[2,128,512]{2,1,0:T(8,128)(2,1)S(1)} %slice.25), channel_id=1, source_target_pairs={{0,3},{1,0},{2,1},{3,2},{4,7},{5,4},{6,5},{7,6},{8,11},{9,8},{10,9... | collective-permute-start | bytes 786440 | tf_op jit(solution)/shard_map/ppermute | solution.py:496
  44.6 2.2 %collective-permute-start.4 = (bf16[4,128,512]{2,1,0:T(8,128)(2,1)S(1)}, bf16[4,128,512]{2,1,0:T(8,128)(2,1)}, u32[]{:S(2)}, u32[]{:S(2)}) collective-permute-start(bf16[4,128,512]{2,1,0:T(8,128)(2,1)S(1)} %bias_plane.1.own0_ref), channel_id=1, source_target_pairs={{0,8},{8,0},{1,9},{9,1},{2,10},{10,2},{3,11},{11,3},{4,12},{12,4},... | collective-permute-start | bytes 1572872 | tf_op jit(solution)/shard_map/ppermute | solution.py:499
  46.8 0.5 collective-permute-start.5
  47.3 1.9 collective-permute-done.1
  49.2 0.7 constant_dynamic-update-slice_fusion.1
  50.0 0.7 constant_dynamic-update-slice_fusion.own2_ref
  50.7 2.6 %collective-permute-start.6 = (bf16[4,128,512]{2,1,0:T(8,128)(2,1)}, bf16[4,128,512]{2,1,0:T(8,128)(2,1)}, u32[]{:S(2)}, u32[]{:S(2)}) collective-permute-start(bf16[4,128,512]{2,1,0:T(8,128)(2,1)} %constant_dynamic-update-slice_fusion.own2_ref), channel_id=1, source_target_pairs={{0,8},{8,0},{1,9},{9,1},{2,10},{10,2},{3,11},{11,3},{4,12},{12,4},... | collective-permute-start | bytes 1572872 | tf_op jit(solution)/shard_map/ppermute | solution.py:499
  53.2 0.6 pad_add_fusion.place_ref
  53.8 1.6 copy.43.wl_ref
  55.4 0.0 copy-start.3
  55.5 0.9 copy-done.3
  56.4 0.8 copy-done.4
  57.2 0.9 copy-done.5
  58.1 0.7 copy-done.11
  58.8 0.6 copy-done.13
  59.4 0.6 copy-done.14
  60.0 20.1 %row_attention.1 = (bf16[16,5,32,256]{3,2,1,0:T(8,128)(2,1)S(1)}, bf16[8,2,8,5,16,128]{5,4,3,2,1,0:T(8,128)(2,1)S(1)}) custom-call(s32[2]{0:T(128)S(1)} %copy-done.14, f32[5]{0:T(128)S(1)} %copy-done.13, bf16[4,128,512]{2,1,0:T(8,128)(2,1)S(1)} %bias_plane.1.own0_ref, bf16[4,128,512]{2,1,0:T(8,128)(2,1)S(1)} %collective-permute-done.own1_ref, ...), custom_call_target="tpu_custom_call" | custom-call | tf_op jit(solution)/shard_map/row_attention/pallas_call | solution.py:222
  80.1 0.0 copy-start.2
  80.1 40.5 %all_to_all.30 = bf16[128,80,128]{2,1,0:T(8,128)(2,1)S(1)} all-to-all(bf16[128,80,128]{2,1,0:T(8,128)(2,1)S(1)} %bitcast.49), channel_id=1, replica_groups=mesh['x'=4,'zl'=2,'core'=2,'zh'=2,'y'=4] {'x','zl','core','zh','y'}, dimensions={0} | all-to-all | bytes 5242880 | tf_op jit(solution)/shard_map/all_to_all | solution.py:513
  120.7 1.2 fusion
  121.9 0.4 copy.53
  122.3 1.6 collective-permute-start.8
  123.9 3.8 %all-to-all-start.3 = ((bf16[16,5,32,256]{3,2,1,0:T(8,128)(2,1)}), bf16[16,5,32,256]{3,2,1,0:T(8,128)(2,1)S(1)}, u32[]{:S(2)}, u32[]{:S(2)}) async-start(bf16[16,5,32,256]{3,2,1,0:T(8,128)(2,1)} %copy-done.2), calls=%async_computation.3 | async-start | bytes 2621440 | tf_op jit(solution)/shard_map/all_to_all | solution.py:521
  127.7 0.1 copy.44.w_ref
  127.9 1.7 copy.54
  129.7 9.6 %outer_update.1 = (bf16[4,8,64,128]{3,2,1,0:T(8,128)(2,1)S(1)}, bf16[2,8,256,128]{3,2,1,0:T(8,128)(2,1)S(1)}) custom-call(s32[1]{0:T(128)} %bitcast.core_ref, bf16[640,1024]{1,0:T(8,128)(2,1)S(1)} %bitcast.47, bf16[640,1024]{1,0:T(8,128)(2,1)S(1)} %bitcast.46, bf16[640,1024]{1,0:T(8,128)(2,1)} %collective-permute-done.8.other_ref, ...), custom_call_target="tpu_custom_call" | custom-call | tf_op jit(solution)/shard_map/outer_update/pallas_call | solution.py:323
  139.3 0.7 copy.55
  139.9 6.1 %all-to-all-done.3 = bf16[16,5,32,256]{3,2,1,0:T(8,128)(2,1)S(1)} async-done(((bf16[16,5,32,256]{3,2,1,0:T(8,128)(2,1)}), bf16[16,5,32,256]{3,2,1,0:T(8,128)(2,1)S(1)}, u32[]{:S(2)}, u32[]{:S(2)}) %all-to-all-start.3) | async-done | bytes 1310752 | tf_op jit(solution)/shard_map/all_to_all | solution.py:521
  146.0 23.0 %all_to_all.31.in_ref = bf16[128,2,16,128]{3,2,1,0:T(8,128)(2,1)S(1)} all-to-all(bf16[128,2,16,128]{3,2,1,0:T(8,128)(2,1)S(1)} %bitcast.63), channel_id=1, replica_groups=mesh['x'=4,'zl'=2,'core'=2,'zh'=2,'y'=4] {'x','zl','core','zh','y'}, dimensions={0} | all-to-all | bytes 2097152 | tf_op jit(solution)/shard_map/all_to_all | solution.py:539
  169.0 3.7 %triangle.1 = bf16[128,16,128]{2,1,0:T(8,128)(2,1)} custom-call(bf16[128,2,16,128]{3,2,1,0:T(8,128)(2,1)S(1)} %all_to_all.31.in_ref), custom_call_target="tpu_custom_call" | custom-call | tf_op jit(solution)/shard_map/triangle/pallas_call | solution.py:367
  172.7 4.7 %all-to-all-start.5 = ((bf16[128,16,128]{2,1,0:T(8,128)(2,1)}), bf16[128,16,128]{2,1,0:T(8,128)(2,1)S(1)}, u32[]{:S(2)}, u32[]{:S(2)}) async-start(bf16[128,16,128]{2,1,0:T(8,128)(2,1)} %triangle.1), calls=%async_computation.5 | async-start | bytes 1048576 | tf_op jit(solution)/shard_map/all_to_all | solution.py:541
  177.5 1.1 copied.1
  178.6 1.2 pair_gate.1.gate_ref
  179.8 11.6 %all-to-all-done.5 = bf16[128,16,128]{2,1,0:T(8,128)(2,1)S(1)} async-done(((bf16[128,16,128]{2,1,0:T(8,128)(2,1)}), bf16[128,16,128]{2,1,0:T(8,128)(2,1)S(1)}, u32[]{:S(2)}, u32[]{:S(2)}) %all-to-all-start.5) | async-done | bytes 524320 | tf_op jit(solution)/shard_map/all_to_all | solution.py:541
  191.4 0.1 copy.56
  191.6 1.4 pair_final.1
  (50 shorter events, 0.1 us)
Async XLA Ops:
  0.6 1.0 copy-start
  1.7 0.7 copy-start.12
  2.4 11.7 %copy-start.22 = (s32[512]{0:T(512)S(1)}, s32[512]{0:T(512)}, u32[]{:S(2)}) copy-start(s32[512]{0:T(512)} %param.14) | copy-start | bytes 6148
  2.4 12.1 %copy-start.21 = (s32[640]{0:T(1024)S(1)}, s32[640]{0:T(1024)}, u32[]{:S(2)}) copy-start(s32[640]{0:T(1024)} %param.15) | copy-start | bytes 7684
  2.4 12.4 %copy-start.19 = (bf16[128,128]{1,0:T(8,128)(2,1)S(1)}, bf16[128,128]{1,0:T(8,128)(2,1)}, u32[]{:S(2)}) copy-start(bf16[128,128]{1,0:T(8,128)(2,1)} %param.23) | copy-start | bytes 98308
  2.4 13.1 %copy-start.18 = (bf16[128,4,128]{2,1,0:T(4,128)(2,1)S(1)}, bf16[128,4,128]{2,1,0:T(4,128)(2,1)}, u32[]{:S(2)}) copy-start(bf16[128,4,128]{2,1,0:T(4,128)(2,1)} %param.21) | copy-start | bytes 393220
  2.4 13.2 %copy-start.17 = (bf16[1024,128]{1,0:T(8,128)(2,1)S(1)}, bf16[1024,128]{1,0:T(8,128)(2,1)}, u32[]{:S(2)}) copy-start(bf16[1024,128]{1,0:T(8,128)(2,1)} %param.20) | copy-start | bytes 786436
  2.4 14.0 %copy-start.16 = (bf16[256,4,256]{2,1,0:T(4,128)(2,1)S(1)}, bf16[256,4,256]{2,1,0:T(4,128)(2,1)}, u32[]{:S(2)}) copy-start(bf16[256,4,256]{2,1,0:T(4,128)(2,1)} %param.16) | copy-start | bytes 1572868
  4.5 14.7 %copy-start.20 = (bf16[256,2,32]{0,2,1:T(8,128)(2,1)S(1)}, bf16[256,2,32]{0,2,1:T(8,128)(2,1)}, u32[]{:S(2)}) copy-start(bf16[256,2,32]{0,2,1:T(8,128)(2,1)} %param.19) | copy-start | bytes 98308
  4.5 21.3 %all-to-all-start = ((bf16[32,64,128]{2,1,0:T(8,128)(2,1)}), bf16[32,64,128]{2,1,0:T(8,128)(2,1)S(1)}, u32[]{:S(2)}, u32[]{:S(2)}) async-start(bf16[32,64,128]{2,1,0:T(8,128)(2,1)} %bitcast.3), calls=%async_computation | async-start | bytes 1048576 | tf_op jit(solution)/shard_map/all_to_all | solution.py:452
  14.1 13.1 %copy-start.10 = (f32[512]{0:T(512)}, f32[512]{0:T(512)S(1)}, u32[]{:S(2)}) copy-start(f32[512]{0:T(512)S(1)} %convert_element_type.7) | copy-start | bytes 6148
  27.7 14.0 %collective-permute-start = (bf16[4,128,512]{2,1,0:T(8,128)(2,1)S(1)}, bf16[4,128,512]{2,1,0:T(8,128)(2,1)S(1)}, u32[]{:S(2)}, u32[]{:S(2)}) collective-permute-start(bf16[4,128,512]{2,1,0:T(8,128)(2,1)S(1)} %bias_plane.1.own0_ref), channel_id=1, source_target_pairs={{0,1},{1,2},{2,3},{3,0},{4,5},{5,6},{6,7},{7,4},{8,9},{9,10},{10,1... | collective-permute-start | bytes 1572872 | tf_op jit(solution)/shard_map/ppermute | solution.py:493
  29.1 12.8 %collective-permute-start.2 = (bf16[4,128,512]{2,1,0:T(8,128)(2,1)S(1)}, bf16[4,128,512]{2,1,0:T(8,128)(2,1)S(1)}, u32[]{:S(2)}, u32[]{:S(2)}) collective-permute-start(bf16[4,128,512]{2,1,0:T(8,128)(2,1)S(1)} %bias_plane.1.own0_ref), channel_id=1, source_target_pairs={{0,3},{1,0},{2,1},{3,2},{4,7},{5,4},{6,5},{7,6},{8,11},{9,8},{10,9... | collective-permute-start | bytes 1572872 | tf_op jit(solution)/shard_map/ppermute | solution.py:494
  30.6 24.8 %all-to-all-start.1 = ((bf16[16,5,32,256]{3,2,1,0:T(8,128)(2,1)}), bf16[16,5,32,256]{3,2,1,0:T(8,128)(2,1)S(1)}, u32[]{:S(2)}, u32[]{:S(2)}) async-start(bf16[16,5,32,256]{3,2,1,0:T(8,128)(2,1)} %bitcast.64), calls=%async_computation.1 | async-start | bytes 2621440 | tf_op jit(solution)/shard_map/all_to_all | solution.py:500
  41.8 7.4 %collective-permute-start.1 = (bf16[2,128,512]{2,1,0:T(8,128)(2,1)S(1)}, bf16[2,128,512]{2,1,0:T(8,128)(2,1)S(1)}, u32[]{:S(2)}, u32[]{:S(2)}) collective-permute-start(bf16[2,128,512]{2,1,0:T(8,128)(2,1)S(1)} %slice.24), channel_id=1, source_target_pairs={{0,1},{1,2},{2,3},{3,0},{4,5},{5,6},{6,7},{7,4},{8,9},{9,10},{10,1... | collective-permute-start | bytes 786440 | tf_op jit(solution)/shard_map/ppermute | solution.py:496
  41.9 8.0 %collective-permute-start.3 = (bf16[2,128,512]{2,1,0:T(8,128)(2,1)S(1)}, bf16[2,128,512]{2,1,0:T(8,128)(2,1)S(1)}, u32[]{:S(2)}, u32[]{:S(2)}) collective-permute-start(bf16[2,128,512]{2,1,0:T(8,128)(2,1)S(1)} %slice.25), channel_id=1, source_target_pairs={{0,3},{1,0},{2,1},{3,2},{4,7},{5,4},{6,5},{7,6},{8,11},{9,8},{10,9... | collective-permute-start | bytes 786440 | tf_op jit(solution)/shard_map/ppermute | solution.py:496
  44.6 10.8 %collective-permute-start.4 = (bf16[4,128,512]{2,1,0:T(8,128)(2,1)S(1)}, bf16[4,128,512]{2,1,0:T(8,128)(2,1)}, u32[]{:S(2)}, u32[]{:S(2)}) collective-permute-start(bf16[4,128,512]{2,1,0:T(8,128)(2,1)S(1)} %bias_plane.1.own0_ref), channel_id=1, source_target_pairs={{0,8},{8,0},{1,9},{9,1},{2,10},{10,2},{3,11},{11,3},{4,12},{12,4},... | collective-permute-start | bytes 1572872 | tf_op jit(solution)/shard_map/ppermute | solution.py:499
  46.8 8.6 %collective-permute-start.7 = (bf16[4,128,512]{2,1,0:T(8,128)(2,1)S(1)}, bf16[4,128,512]{2,1,0:T(8,128)(2,1)}, u32[]{:S(2)}, u32[]{:S(2)}) collective-permute-start(bf16[4,128,512]{2,1,0:T(8,128)(2,1)S(1)} %collective-permute-done.2.own3_ref), channel_id=1, source_target_pairs={{0,8},{8,0},{1,9},{9,1},{2,10},{10,2},{3,11},{11,3},{4,12},{12,4},... | collective-permute-start | bytes 1572872 | tf_op jit(solution)/shard_map/ppermute | solution.py:499
  46.8 8.6 %collective-permute-start.5 = (bf16[4,128,512]{2,1,0:T(8,128)(2,1)S(1)}, bf16[4,128,512]{2,1,0:T(8,128)(2,1)}, u32[]{:S(2)}, u32[]{:S(2)}) collective-permute-start(bf16[4,128,512]{2,1,0:T(8,128)(2,1)S(1)} %collective-permute-done.own1_ref), channel_id=1, source_target_pairs={{0,8},{8,0},{1,9},{9,1},{2,10},{10,2},{3,11},{11,3},{4,12},{12,4},... | collective-permute-start | bytes 1572872 | tf_op jit(solution)/shard_map/ppermute | solution.py:499
  50.7 4.8 %collective-permute-start.6 = (bf16[4,128,512]{2,1,0:T(8,128)(2,1)}, bf16[4,128,512]{2,1,0:T(8,128)(2,1)}, u32[]{:S(2)}, u32[]{:S(2)}) collective-permute-start(bf16[4,128,512]{2,1,0:T(8,128)(2,1)} %constant_dynamic-update-slice_fusion.own2_ref), channel_id=1, source_target_pairs={{0,8},{8,0},{1,9},{9,1},{2,10},{10,2},{3,11},{11,3},{4,12},{12,4},... | collective-permute-start | bytes 1572872 | tf_op jit(solution)/shard_map/ppermute | solution.py:499
  55.4 1.0 copy-start.3
  56.4 0.8 copy-start.4
  57.2 0.9 copy-start.5
  58.1 0.7 copy-start.11
  58.8 0.6 copy-start.13
  59.4 0.6 copy-start.14
  80.1 40.6 %copy-start.2 = (bf16[16,5,32,256]{3,2,1,0:T(8,128)(2,1)}, bf16[16,5,32,256]{3,2,1,0:T(8,128)(2,1)S(1)}, u32[]{:S(2)}) copy-start(bf16[16,5,32,256]{3,2,1,0:T(8,128)(2,1)S(1)} %get-tuple-element.41) | copy-start | bytes 3932164
  122.3 5.4 %copy-start.15 = (bf16[128,16,2,32]{0,3,2,1:T(8,128)(2,1)S(1)}, bf16[128,16,2,32]{0,3,2,1:T(8,128)(2,1)}, u32[]{:S(2)}) copy-start(bf16[128,16,2,32]{0,3,2,1:T(8,128)(2,1)} %copy.38) | copy-start | bytes 786436
  122.3 7.4 %collective-permute-start.8 = (bf16[640,1024]{1,0:T(8,128)(2,1)S(1)}, bf16[640,1024]{1,0:T(8,128)(2,1)}, u32[]{:S(2)}, u32[]{:S(2)}) collective-permute-start(bf16[640,1024]{1,0:T(8,128)(2,1)S(1)} %bitcast.45), channel_id=1, source_target_pairs={{0,8},{8,0},{1,9},{9,1},{2,10},{10,2},{3,11},{11,3},{4,12},{12,4},... | collective-permute-start | bytes 3932168 | tf_op jit(solution)/shard_map/ppermute | solution.py:519
  123.9 22.1 %all-to-all-start.3 = ((bf16[16,5,32,256]{3,2,1,0:T(8,128)(2,1)}), bf16[16,5,32,256]{3,2,1,0:T(8,128)(2,1)S(1)}, u32[]{:S(2)}, u32[]{:S(2)}) async-start(bf16[16,5,32,256]{3,2,1,0:T(8,128)(2,1)} %copy-done.2), calls=%async_computation.3 | async-start | bytes 2621440 | tf_op jit(solution)/shard_map/all_to_all | solution.py:521
  127.9 1.8 copy-start.1
  127.9 1.8 copy-start.7
  127.9 1.8 copy-start.8
  172.7 18.7 %all-to-all-start.5 = ((bf16[128,16,128]{2,1,0:T(8,128)(2,1)}), bf16[128,16,128]{2,1,0:T(8,128)(2,1)S(1)}, u32[]{:S(2)}, u32[]{:S(2)}) async-start(bf16[128,16,128]{2,1,0:T(8,128)(2,1)} %triangle.1), calls=%async_computation.5 | async-start | bytes 1048576 | tf_op jit(solution)/shard_map/all_to_all | solution.py:541
  177.5 1.2 copy-start.9
  178.6 12.9 %copy-start.6 = (bf16[128,128]{0,1:T(8,128)(2,1)S(1)}, bf16[128,128]{0,1:T(8,128)(2,1)}, u32[]{:S(2)}) copy-start(bf16[128,128]{0,1:T(8,128)(2,1)} %copy.40) | copy-start | bytes 98308

commit v7 on v6

--- a/solution.py
+++ b/solution.py
@@ -101,7 +101,6 @@
 
 def attention_kernel(
     place_ref,
-    seq_ref,
     own0_ref,
     own1_ref,
     own2_ref,
@@ -112,10 +111,6 @@
     other3_ref,
     x_ref,
     win_ref,
-    wo_ref,
-    wl_ref,
-    wr_ref,
-    live_ref,
     live_col_ref,
     out_ref,
     factor_ref,
@@ -124,12 +119,14 @@
     k_ref,
     vt_ref,
     acc_ref,
+    live_ref,
 ):
     heads = bias_ref.shape[0]
     step = pl.program_id(0)
 
     @pl.when(step == 0)
     def _():
+        live_ref[...] = live_col_ref[...].T[:8]
         core, y = place_ref[0], place_ref[1]
         own = (own0_ref, own1_ref, own2_ref, own3_ref)
         other = (other0_ref, other1_ref, other2_ref, other3_ref)
@@ -185,19 +182,19 @@
     values(heads - 1, p)
     attended = (acc_ref[...] * jax.nn.sigmoid(project(3))).T.astype(BF16)
     out = (
-        x.astype(F32) + jnp.dot(attended, wo_ref[...], preferred_element_type=F32)
+        x.astype(F32) + jnp.dot(attended, win_ref[1024:1280], preferred_element_type=F32)
     ).astype(BF16)
     out_ref[:, 0] = out.reshape(16, 32, 256)
     second = layer_norm(out).astype(BF16)
-    seq_live = seq_ref[step]
-    left = jnp.dot(second, wl_ref[...], preferred_element_type=F32)
+    seq_live = place_ref[2 + step].astype(F32)
+    left = lax.dot_general(second, win_ref[1280:1408], NT, preferred_element_type=F32)
     left = (left * (live_col_ref[...] * seq_live)).reshape(16, 4, 8, 128)
     group = lax.broadcasted_iota(jnp.int32, (16, 8, 128), 2) // 32
     packed = left[:, 0]
     for q in range(1, 4):
         packed = jnp.where(group == q, left[:, q], packed)
-    right = lax.dot_general(wr_ref[...], second, NT, preferred_element_type=F32)
-    right = right * (live_ref[...] * seq_live)
+    right = lax.dot_general(win_ref[1408:1440], second, NT, preferred_element_type=F32)
+    right = right * (live_ref[:1] * seq_live)
     for m in range(4):
         tile = right[:, 128 * m : 128 * m + 128]
         for c, chunk in enumerate(mix(tile[:16], tile[16:])):
@@ -209,7 +206,7 @@
                     ).astype(BF16)
 
 
-def attention(place, seq_live, biases, x, win, wo, wl, wr, live, live_col):
+def attention(place, biases, x, win, live_col):
     count = x.shape[1]
     smem = pl.BlockSpec(memory_space=pltpu.SMEM)
 
@@ -224,14 +221,9 @@
         grid=(count,),
         in_specs=[
             smem,
-            smem,
             *(whole(b) for b in biases),
             per_seq(16, 1, 32, 256),
             whole(win),
-            whole(wo),
-            whole(wl),
-            whole(wr),
-            whole(live),
             whole(live_col),
         ],
         out_specs=[
@@ -248,10 +240,11 @@
             pltpu.VMEM((512, 256), BF16),
             pltpu.VMEM((8, 48, 512), BF16),
             pltpu.VMEM((256, 512), F32),
+            pltpu.VMEM((8, 512), F32),
         ],
-        compiler_params=params(32),
+        compiler_params=params(52),
         name="row_attention",
-    )(place, seq_live, *biases, x, win, wo, wl, wr, live, live_col)
+    )(place, *biases, x, win, live_col)
 
 
 def outer_kernel(
@@ -447,7 +440,8 @@
     seq_live = sequence_mask.astype(F32)
     row_live = lax.dynamic_slice_in_dim(res_live, row * 32, 32)
     col_live = lax.dynamic_slice_in_dim(res_live, col * 64, 64)
-    my_seqs = lax.dynamic_slice_in_dim(seq_live, col * 80 + row * 5, 5)
+    my_seqs = lax.dynamic_slice_in_dim(sequence_mask, col * 80 + row * 5, 5)
+    scalars = jnp.concatenate([jnp.stack([core, lax.axis_index("y")]), my_seqs])
 
     blocks = lax.all_to_all(
         pair_bias(pairwise, bias_project.T).reshape(32, 64, 128),
@@ -463,13 +457,23 @@
         return a.reshape(2, 16, 64).transpose(1, 0, 2).reshape(2, 8, 1, 128)
 
     weight = outer_output.reshape(32, 2, 16, 128).transpose(3, 2, 1, 0).reshape(128, 1024)
-    win = attention_input_weight.reshape(256, 1024).T
     wp = tri_project.reshape(128, 512).T
     wt = tri_output.T
-    wl = jnp.tile(outer_factor_weight[:, 0], (1, 4))
-    wr = outer_factor_weight[:, 1].T
+    wl = outer_factor_weight[:, 0].T
+    win = jnp.concatenate(
+        [
+            attention_input_weight.reshape(256, 1024).T,
+            attention_output_weight,
+            wl,
+            wl,
+            wl,
+            wl,
+            outer_factor_weight[:, 1].T,
+        ],
+        axis=0,
+    )
     live_cols = jnp.broadcast_to(res_live[:, None], (512, 128))
-    blocks, weight, wp, wt, inv, live_plane, win, wl, wr, live_cols, my_seqs = (
+    blocks, weight, wp, wt, inv, live_plane, win, live_cols, scalars = (
         lax.optimization_barrier(
             (
                 blocks,
@@ -479,10 +483,8 @@
                 pairs(inv),
                 pairs(live_plane),
                 win,
-                wl,
-                wr,
                 live_cols,
-                my_seqs,
+                scalars,
             )
         )
     )
@@ -498,18 +500,7 @@
     own = [bias_plane, left_plane, far_plane, right_plane]
     other = [lax.ppermute(b, "core", swap) for b in own]
     sequences = lax.all_to_all(outgoing, ROW, split_axis=0, concat_axis=0, tiled=True)
-    out_seq, factors = attention(
-        jnp.stack([core, lax.axis_index("y")]),
-        my_seqs,
-        own + other,
-        sequences,
-        win,
-        attention_output_weight,
-        wl,
-        wr,
-        res_live.reshape(1, 512),
-        live_cols,
-    )
+    out_seq, factors = attention(scalars, own + other, sequences, win, live_cols)
     factors = lax.all_to_all(
         factors.reshape(128, 80, 128), ALL, split_axis=0, concat_axis=0, tiled=True
     )

time: 194 us -> 190 us (0.979)
  waiting for transfers between devices: 32.6 us -> 28.3 us
  blocking collectives: 63.5 us -> 65.7 us
    all_to_all x1, waiting for transfers between devices: 6.58 us -> 3.08 us  [body(): lax.all_to_all(pair_bias(pairwise, bias_project.T).reshape(32, 64, 128),...]
    all_to_all x1, blocking collectives: 40.5 us -> 42.8 us  [body(): lax.all_to_all(factors.reshape(128, 80, 128), ALL, split_axis=0, concat_a...]
    unnamed x52 -> x46, local copies, waits for them, and re-layouts: 10.3 us -> 11.6 us
  transfers between devices with their start and end apart: 13 -> 13, of which waited for: 5 -> 6; matrix products, arithmetic and copies ran while one was open for 6% -> 6% of each run, Pallas kernels for 6% -> 6%
where the time goes in v7:
time: 190 us
  blocking collectives  65.7 us (35%)
  Pallas kernels  40.6 us (21%)
  starting transfers between devices  35.6 us (19%)
  waiting for transfers between devices  28.3 us (15%)
  local copies, waits for them, and re-layouts  17 us (9%)
    all_to_all x1, blocking collectives, body(): lax.all_to_all(factors.reshape(128, 80, 128), ALL, split_axis=0, concat_a...  42.8 us
    all_to_all x1, blocking collectives, body(): blocks = lax.all_to_all(tri, ALL, split_axis=0, concat_axis=0, tiled=True)  23 us
    pallas_call x1, Pallas kernels, attention(): pl.pallas_call(attention_kernel, grid=(count,), in_specs=[smem, *(whole(b...  21 us
    all_to_all x1, waiting for transfers between devices, body(): lax.all_to_all(product, ALL, split_axis=0, concat_axis=0, tiled=True)  11.6 us
    unnamed x46, local copies, waits for them, and re-layouts  11.6 us
    pallas_call x1, Pallas kernels, outer_update(): pl.pallas_call(outer_kernel, in_specs=[pl.BlockSpec(memory_space=pltpu.SM...  9.56 us
    all_to_all x1, starting transfers between devices, body(): lax.all_to_all(pair_bias(pairwise, bias_project.T).reshape(32, 64, 128),...  9.43 us
    ppermute x1, waiting for transfers between devices, body(): left_plane = lax.ppermute(bias_plane, 'y', up)  6.42 us
  transfers between devices with their start and end apart: 13, of which 6 were waited for; matrix products, arithmetic and copies ran while one was open for 6% of the time, Pallas kernels for 6%

profile of v7, /device:TPU:1, one launch (start us, length us, event | category | flops | bytes accessed | tf_op | source)
XLA Modules:
  0.0 189.6 jit_solution(4215576220504243349)
XLA Ops:
  0.6 1.0 copy-done
  1.7 0.7 copy-done.4
  2.4 2.1 %pair_bias.1 = bf16[8,2,2,64,128]{4,3,2,1,0:T(8,128)(2,1)} custom-call(bf16[32,64,128]{2,1,0:T(8,128)(2,1)S(1)} %copy-done, bf16[8,128]{1,0:T(8,128)(2,1)S(1)} %bitcast.59), custom_call_target="tpu_custom_call" | custom-call | tf_op jit(solution)/shard_map/pair_bias/pallas_call | solution.py:61
  4.5 9.4 %all-to-all-start = ((bf16[32,64,128]{2,1,0:T(8,128)(2,1)}), bf16[32,64,128]{2,1,0:T(8,128)(2,1)S(1)}, u32[]{:S(2)}, u32[]{:S(2)}) async-start(bf16[32,64,128]{2,1,0:T(8,128)(2,1)} %bitcast.2), calls=%async_computation | async-start | bytes 1048576 | tf_op jit(solution)/shard_map/all_to_all | solution.py:446
  14.0 0.7 convert_reduce_fusion
  14.6 0.1 dynamic_slice.11
  14.7 0.1 dynamic_slice.10
  14.8 0.1 dynamic_slice.9
  14.9 0.1 mul.73
  15.0 0.1 mul.80
  15.0 0.1 copy.38
  15.1 0.1 mul.75
  15.2 0.1 mul.76
  15.3 0.7 copy.37
  16.0 0.1 copy.36
  16.2 0.8 copy.35
  17.0 0.3 copy.39
  17.3 0.8 constant_dynamic-update-slice_fusion.6
  18.2 0.7 constant_dynamic-update-slice_fusion.5
  18.8 0.6 constant_dynamic-update-slice_fusion.4
  19.4 0.6 constant_dynamic-update-slice_fusion.3
  20.0 0.6 constant_dynamic-update-slice_fusion.2
  20.6 0.7 maximum_divide_fusion
  21.3 0.1 pad_add_fusion.place_ref
  21.4 0.6 constant_dynamic-update-slice_fusion.1
  22.0 0.6 constant_dynamic-update-slice_fusion.win_ref
  22.6 3.1 %all-to-all-done.in_ref = bf16[32,64,128]{2,1,0:T(8,128)(2,1)S(1)} async-done(((bf16[32,64,128]{2,1,0:T(8,128)(2,1)}), bf16[32,64,128]{2,1,0:T(8,128)(2,1)S(1)}, u32[]{:S(2)}, u32[]{:S(2)}) %all-to-all-start) | async-done | bytes 524320 | tf_op jit(solution)/shard_map/all_to_all | solution.py:446
  25.6 0.1 broadcast_in_dim.2.live_col_ref
  25.8 0.5 bias_plane.1.own0_ref
  26.2 1.4 collective-permute-start
  27.6 1.5 collective-permute-start.2
  29.1 4.7 %all-to-all-start.1 = ((bf16[16,5,32,256]{3,2,1,0:T(8,128)(2,1)}), bf16[16,5,32,256]{3,2,1,0:T(8,128)(2,1)S(1)}, u32[]{:S(2)}, u32[]{:S(2)}) async-start(bf16[16,5,32,256]{3,2,1,0:T(8,128)(2,1)} %bitcast.66), calls=%async_computation.1 | async-start | bytes 2621440 | tf_op jit(solution)/shard_map/all_to_all | solution.py:502
  33.9 6.4 %collective-permute-done.own1_ref = bf16[4,128,512]{2,1,0:T(8,128)(2,1)S(1)} collective-permute-done((bf16[4,128,512]{2,1,0:T(8,128)(2,1)S(1)}, bf16[4,128,512]{2,1,0:T(8,128)(2,1)S(1)}, u32[]{:S(2)}, u32[]{:S(2)}) %collective-permute-start) | collective-permute-done | bytes 524320 | tf_op jit(solution)/shard_map/ppermute | solution.py:495
  40.3 0.1 collective-permute-start.1
  40.4 1.0 slice.25
  41.4 2.7 %collective-permute-start.3 = (bf16[2,128,512]{2,1,0:T(8,128)(2,1)S(1)}, bf16[2,128,512]{2,1,0:T(8,128)(2,1)S(1)}, u32[]{:S(2)}, u32[]{:S(2)}) collective-permute-start(bf16[2,128,512]{2,1,0:T(8,128)(2,1)S(1)} %slice.25), channel_id=1, source_target_pairs={{0,3},{1,0},{2,1},{3,2},{4,7},{5,4},{6,5},{7,6},{8,11},{9,8},{10,9... | collective-permute-start | bytes 786440 | tf_op jit(solution)/shard_map/ppermute | solution.py:498
  44.1 2.2 %collective-permute-start.4 = (bf16[4,128,512]{2,1,0:T(8,128)(2,1)S(1)}, bf16[4,128,512]{2,1,0:T(8,128)(2,1)S(1)}, u32[]{:S(2)}, u32[]{:S(2)}) collective-permute-start(bf16[4,128,512]{2,1,0:T(8,128)(2,1)S(1)} %bias_plane.1.own0_ref), channel_id=1, source_target_pairs={{0,8},{8,0},{1,9},{9,1},{2,10},{10,2},{3,11},{11,3},{4,12},{12,4},... | collective-permute-start | bytes 1572872 | tf_op jit(solution)/shard_map/ppermute | solution.py:501
  46.3 0.5 collective-permute-start.5
  46.8 0.9 collective-permute-done.1
  47.8 0.0 collective-permute-done.3
  47.8 2.9 %collective-permute-start.6 = (bf16[4,128,512]{2,1,0:T(8,128)(2,1)S(1)}, bf16[4,128,512]{2,1,0:T(8,128)(2,1)}, u32[]{:S(2)}, u32[]{:S(2)}) collective-permute-start(bf16[4,128,512]{2,1,0:T(8,128)(2,1)S(1)} %constant_dynamic-update-slice_fusion.7.own2_ref), channel_id=1, source_target_pairs={{0,8},{8,0},{1,9},{9,1},{2,10},{10,2},{3,11},{11,3},{4,12},{12,4},... | collective-permute-start | bytes 1572872 | tf_op jit(solution)/shard_map/ppermute | solution.py:501
  50.7 0.8 copy-done.7
  51.5 0.8 copy-done.8
  52.3 0.1 all-to-all-done.1.x_ref
  52.5 1.1 copy-done.5
  53.5 21.0 %row_attention.1 = (bf16[16,5,32,256]{3,2,1,0:T(8,128)(2,1)}, bf16[8,2,8,5,16,128]{5,4,3,2,1,0:T(8,128)(2,1)}) custom-call(s32[7]{0:T(128)S(1)} %pad_add_fusion.place_ref, bf16[4,128,512]{2,1,0:T(8,128)(2,1)S(1)} %bias_plane.1.own0_ref, bf16[4,128,512]{2,1,0:T(8,128)(2,1)S(1)} %collective-permute-done.own1_ref, ...), custom_call_target="tpu_custom_call" | custom-call | tf_op jit(solution)/shard_map/row_attention/pallas_call | solution.py:219
  74.5 42.8 %all_to_all.30 = bf16[128,80,128]{2,1,0:T(8,128)(2,1)S(1)} all-to-all(bf16[128,80,128]{2,1,0:T(8,128)(2,1)} %bitcast.64), channel_id=1, replica_groups=mesh['x'=4,'zl'=2,'core'=2,'zh'=2,'y'=4] {'x','zl','core','zh','y'}, dimensions={0} | all-to-all | bytes 5242880 | tf_op jit(solution)/shard_map/all_to_all | solution.py:504
  117.3 1.2 fusion
  118.5 0.4 copy.49
  118.9 1.6 collective-permute-start.8
  120.5 3.8 %all-to-all-start.3 = ((bf16[16,5,32,256]{3,2,1,0:T(8,128)(2,1)}), bf16[16,5,32,256]{3,2,1,0:T(8,128)(2,1)S(1)}, u32[]{:S(2)}, u32[]{:S(2)}) async-start(bf16[16,5,32,256]{3,2,1,0:T(8,128)(2,1)} %get-tuple-element.37), calls=%async_computation.3 | async-start | bytes 2621440 | tf_op jit(solution)/shard_map/all_to_all | solution.py:512
  124.3 0.1 copy.40.w_ref
  124.5 1.7 copy.50
  126.3 9.6 %outer_update.1 = (bf16[4,8,64,128]{3,2,1,0:T(8,128)(2,1)S(1)}, bf16[2,8,256,128]{3,2,1,0:T(8,128)(2,1)S(1)}) custom-call(s32[1]{0:T(128)} %bitcast.core_ref, bf16[640,1024]{1,0:T(8,128)(2,1)S(1)} %bitcast.50, bf16[640,1024]{1,0:T(8,128)(2,1)S(1)} %bitcast.49, bf16[640,1024]{1,0:T(8,128)(2,1)} %collective-permute-done.8.other_ref, ...), custom_call_target="tpu_custom_call" | custom-call | tf_op jit(solution)/shard_map/outer_update/pallas_call | solution.py:316
  135.8 0.7 copy.51
  136.5 6.1 %all-to-all-done.3 = bf16[16,5,32,256]{3,2,1,0:T(8,128)(2,1)S(1)} async-done(((bf16[16,5,32,256]{3,2,1,0:T(8,128)(2,1)}), bf16[16,5,32,256]{3,2,1,0:T(8,128)(2,1)S(1)}, u32[]{:S(2)}, u32[]{:S(2)}) %all-to-all-start.3) | async-done | bytes 1310752 | tf_op jit(solution)/shard_map/all_to_all | solution.py:512
  142.7 23.0 %all_to_all.31.in_ref = bf16[128,2,16,128]{3,2,1,0:T(8,128)(2,1)S(1)} all-to-all(bf16[128,2,16,128]{3,2,1,0:T(8,128)(2,1)S(1)} %bitcast.63), channel_id=1, replica_groups=mesh['x'=4,'zl'=2,'core'=2,'zh'=2,'y'=4] {'x','zl','core','zh','y'}, dimensions={0} | all-to-all | bytes 2097152 | tf_op jit(solution)/shard_map/all_to_all | solution.py:530
  165.6 3.7 %triangle.1 = bf16[128,16,128]{2,1,0:T(8,128)(2,1)} custom-call(bf16[128,2,16,128]{3,2,1,0:T(8,128)(2,1)S(1)} %all_to_all.31.in_ref), custom_call_target="tpu_custom_call" | custom-call | tf_op jit(solution)/shard_map/triangle/pallas_call | solution.py:360
  169.4 4.7 %all-to-all-start.5 = ((bf16[128,16,128]{2,1,0:T(8,128)(2,1)}), bf16[128,16,128]{2,1,0:T(8,128)(2,1)S(1)}, u32[]{:S(2)}, u32[]{:S(2)}) async-start(bf16[128,16,128]{2,1,0:T(8,128)(2,1)} %triangle.1), calls=%async_computation.5 | async-start | bytes 1048576 | tf_op jit(solution)/shard_map/all_to_all | solution.py:532
  174.1 1.1 copied.1
  175.2 1.2 pair_gate.1.gate_ref
  176.4 11.6 %all-to-all-done.5 = bf16[128,16,128]{2,1,0:T(8,128)(2,1)S(1)} async-done(((bf16[128,16,128]{2,1,0:T(8,128)(2,1)}), bf16[128,16,128]{2,1,0:T(8,128)(2,1)S(1)}, u32[]{:S(2)}, u32[]{:S(2)}) %all-to-all-start.5) | async-done | bytes 524320 | tf_op jit(solution)/shard_map/all_to_all | solution.py:532
  188.0 0.1 copy.52
  188.2 1.4 pair_final.1
  (41 shorter events, 0.1 us)
Async XLA Ops:
  0.6 1.0 copy-start
  1.7 0.7 copy-start.4
  2.4 11.6 %copy-start.15 = (s32[640]{0:T(1024)S(1)}, s32[640]{0:T(1024)}, u32[]{:S(2)}) copy-start(s32[640]{0:T(1024)} %param.15) | copy-start | bytes 7684
  2.4 12.4 %copy-start.16 = (s32[512]{0:T(512)S(1)}, s32[512]{0:T(512)}, u32[]{:S(2)}) copy-start(s32[512]{0:T(512)} %param.14) | copy-start | bytes 6148
  2.4 12.9 %copy-start.14 = (bf16[128,128]{1,0:T(8,128)(2,1)S(1)}, bf16[128,128]{1,0:T(8,128)(2,1)}, u32[]{:S(2)}) copy-start(bf16[128,128]{1,0:T(8,128)(2,1)} %param.23) | copy-start | bytes 98308
  2.4 13.7 %copy-start.12 = (bf16[128,4,128]{2,1,0:T(4,128)(2,1)S(1)}, bf16[128,4,128]{2,1,0:T(4,128)(2,1)}, u32[]{:S(2)}) copy-start(bf16[128,4,128]{2,1,0:T(4,128)(2,1)} %param.21) | copy-start | bytes 393220
  2.4 13.8 %copy-start.10 = (bf16[1024,128]{1,0:T(8,128)(2,1)S(1)}, bf16[1024,128]{1,0:T(8,128)(2,1)}, u32[]{:S(2)}) copy-start(bf16[1024,128]{1,0:T(8,128)(2,1)} %param.20) | copy-start | bytes 786436
  2.4 14.6 %copy-start.9 = (bf16[256,4,256]{2,1,0:T(4,128)(2,1)S(1)}, bf16[256,4,256]{2,1,0:T(4,128)(2,1)}, u32[]{:S(2)}) copy-start(bf16[256,4,256]{2,1,0:T(4,128)(2,1)} %param.16) | copy-start | bytes 1572868
  4.5 21.1 %all-to-all-start = ((bf16[32,64,128]{2,1,0:T(8,128)(2,1)}), bf16[32,64,128]{2,1,0:T(8,128)(2,1)S(1)}, u32[]{:S(2)}, u32[]{:S(2)}) async-start(bf16[32,64,128]{2,1,0:T(8,128)(2,1)} %bitcast.2), calls=%async_computation | async-start | bytes 1048576 | tf_op jit(solution)/shard_map/all_to_all | solution.py:446
  16.2 2.0 %copy-start.13 = (bf16[256,256]{1,0:T(8,128)(2,1)S(1)}, bf16[256,256]{1,0:T(8,128)(2,1)}, u32[]{:S(2)}) copy-start(bf16[256,256]{1,0:T(8,128)(2,1)} %param.17) | copy-start | bytes 393220
  17.0 1.8 copy-start.11
  26.2 14.0 %collective-permute-start = (bf16[4,128,512]{2,1,0:T(8,128)(2,1)S(1)}, bf16[4,128,512]{2,1,0:T(8,128)(2,1)S(1)}, u32[]{:S(2)}, u32[]{:S(2)}) collective-permute-start(bf16[4,128,512]{2,1,0:T(8,128)(2,1)S(1)} %bias_plane.1.own0_ref), channel_id=1, source_target_pairs={{0,1},{1,2},{2,3},{3,0},{4,5},{5,6},{6,7},{7,4},{8,9},{9,10},{10,1... | collective-permute-start | bytes 1572872 | tf_op jit(solution)/shard_map/ppermute | solution.py:495
  27.6 12.8 %collective-permute-start.2 = (bf16[4,128,512]{2,1,0:T(8,128)(2,1)S(1)}, bf16[4,128,512]{2,1,0:T(8,128)(2,1)}, u32[]{:S(2)}, u32[]{:S(2)}) collective-permute-start(bf16[4,128,512]{2,1,0:T(8,128)(2,1)S(1)} %bias_plane.1.own0_ref), channel_id=1, source_target_pairs={{0,3},{1,0},{2,1},{3,2},{4,7},{5,4},{6,5},{7,6},{8,11},{9,8},{10,9... | collective-permute-start | bytes 1572872 | tf_op jit(solution)/shard_map/ppermute | solution.py:496
  29.1 23.3 %all-to-all-start.1 = ((bf16[16,5,32,256]{3,2,1,0:T(8,128)(2,1)}), bf16[16,5,32,256]{3,2,1,0:T(8,128)(2,1)S(1)}, u32[]{:S(2)}, u32[]{:S(2)}) async-start(bf16[16,5,32,256]{3,2,1,0:T(8,128)(2,1)} %bitcast.66), calls=%async_computation.1 | async-start | bytes 2621440 | tf_op jit(solution)/shard_map/all_to_all | solution.py:502
  40.3 7.4 %collective-permute-start.1 = (bf16[2,128,512]{2,1,0:T(8,128)(2,1)S(1)}, bf16[2,128,512]{2,1,0:T(8,128)(2,1)S(1)}, u32[]{:S(2)}, u32[]{:S(2)}) collective-permute-start(bf16[2,128,512]{2,1,0:T(8,128)(2,1)S(1)} %slice.24), channel_id=1, source_target_pairs={{0,1},{1,2},{2,3},{3,0},{4,5},{5,6},{6,7},{7,4},{8,9},{9,10},{10,1... | collective-permute-start | bytes 786440 | tf_op jit(solution)/shard_map/ppermute | solution.py:498
  41.4 6.4 %collective-permute-start.3 = (bf16[2,128,512]{2,1,0:T(8,128)(2,1)S(1)}, bf16[2,128,512]{2,1,0:T(8,128)(2,1)S(1)}, u32[]{:S(2)}, u32[]{:S(2)}) collective-permute-start(bf16[2,128,512]{2,1,0:T(8,128)(2,1)S(1)} %slice.25), channel_id=1, source_target_pairs={{0,3},{1,0},{2,1},{3,2},{4,7},{5,4},{6,5},{7,6},{8,11},{9,8},{10,9... | collective-permute-start | bytes 786440 | tf_op jit(solution)/shard_map/ppermute | solution.py:498
  44.1 6.6 %collective-permute-start.4 = (bf16[4,128,512]{2,1,0:T(8,128)(2,1)S(1)}, bf16[4,128,512]{2,1,0:T(8,128)(2,1)S(1)}, u32[]{:S(2)}, u32[]{:S(2)}) collective-permute-start(bf16[4,128,512]{2,1,0:T(8,128)(2,1)S(1)} %bias_plane.1.own0_ref), channel_id=1, source_target_pairs={{0,8},{8,0},{1,9},{9,1},{2,10},{10,2},{3,11},{11,3},{4,12},{12,4},... | collective-permute-start | bytes 1572872 | tf_op jit(solution)/shard_map/ppermute | solution.py:501
  46.3 4.4 %collective-permute-start.7 = (bf16[4,128,512]{2,1,0:T(8,128)(2,1)}, bf16[4,128,512]{2,1,0:T(8,128)(2,1)S(1)}, u32[]{:S(2)}, u32[]{:S(2)}) collective-permute-start(bf16[4,128,512]{2,1,0:T(8,128)(2,1)} %collective-permute-done.2.own3_ref), channel_id=1, source_target_pairs={{0,8},{8,0},{1,9},{9,1},{2,10},{10,2},{3,11},{11,3},{4,12},{12,4},... | collective-permute-start | bytes 1572872 | tf_op jit(solution)/shard_map/ppermute | solution.py:501
  46.3 6.0 %collective-permute-start.5 = (bf16[4,128,512]{2,1,0:T(8,128)(2,1)S(1)}, bf16[4,128,512]{2,1,0:T(8,128)(2,1)}, u32[]{:S(2)}, u32[]{:S(2)}) collective-permute-start(bf16[4,128,512]{2,1,0:T(8,128)(2,1)S(1)} %collective-permute-done.own1_ref), channel_id=1, source_target_pairs={{0,8},{8,0},{1,9},{9,1},{2,10},{10,2},{3,11},{11,3},{4,12},{12,4},... | collective-permute-start | bytes 1572872 | tf_op jit(solution)/shard_map/ppermute | solution.py:501
  47.8 4.7 %collective-permute-start.6 = (bf16[4,128,512]{2,1,0:T(8,128)(2,1)S(1)}, bf16[4,128,512]{2,1,0:T(8,128)(2,1)}, u32[]{:S(2)}, u32[]{:S(2)}) collective-permute-start(bf16[4,128,512]{2,1,0:T(8,128)(2,1)S(1)} %constant_dynamic-update-slice_fusion.7.own2_ref), channel_id=1, source_target_pairs={{0,8},{8,0},{1,9},{9,1},{2,10},{10,2},{3,11},{11,3},{4,12},{12,4},... | collective-permute-start | bytes 1572872 | tf_op jit(solution)/shard_map/ppermute | solution.py:501
  50.7 0.8 copy-start.7
  51.5 0.8 copy-start.8
  52.5 1.1 copy-start.5
  118.9 5.4 %copy-start.6 = (bf16[128,16,2,32]{0,3,2,1:T(8,128)(2,1)S(1)}, bf16[128,16,2,32]{0,3,2,1:T(8,128)(2,1)}, u32[]{:S(2)}) copy-start(bf16[128,16,2,32]{0,3,2,1:T(8,128)(2,1)} %copy.35) | copy-start | bytes 786436
  118.9 7.4 %collective-permute-start.8 = (bf16[640,1024]{1,0:T(8,128)(2,1)S(1)}, bf16[640,1024]{1,0:T(8,128)(2,1)}, u32[]{:S(2)}, u32[]{:S(2)}) collective-permute-start(bf16[640,1024]{1,0:T(8,128)(2,1)S(1)} %bitcast.48), channel_id=1, source_target_pairs={{0,8},{8,0},{1,9},{9,1},{2,10},{10,2},{3,11},{11,3},{4,12},{12,4},... | collective-permute-start | bytes 3932168 | tf_op jit(solution)/shard_map/ppermute | solution.py:510
  120.5 22.1 %all-to-all-start.3 = ((bf16[16,5,32,256]{3,2,1,0:T(8,128)(2,1)}), bf16[16,5,32,256]{3,2,1,0:T(8,128)(2,1)S(1)}, u32[]{:S(2)}, u32[]{:S(2)}) async-start(bf16[16,5,32,256]{3,2,1,0:T(8,128)(2,1)} %get-tuple-element.37), calls=%async_computation.3 | async-start | bytes 2621440 | tf_op jit(solution)/shard_map/all_to_all | solution.py:512
  124.5 1.8 copy-start.1
  169.4 18.7 %all-to-all-start.5 = ((bf16[128,16,128]{2,1,0:T(8,128)(2,1)}), bf16[128,16,128]{2,1,0:T(8,128)(2,1)S(1)}, u32[]{:S(2)}, u32[]{:S(2)}) async-start(bf16[128,16,128]{2,1,0:T(8,128)(2,1)} %triangle.1), calls=%async_computation.5 | async-start | bytes 1048576 | tf_op jit(solution)/shard_map/all_to_all | solution.py:532
  174.1 1.2 copy-start.3
  175.2 12.9 %copy-start.2 = (bf16[128,128]{0,1:T(8,128)(2,1)S(1)}, bf16[128,128]{0,1:T(8,128)(2,1)}, u32[]{:S(2)}) copy-start(bf16[128,128]{0,1:T(8,128)(2,1)} %copy.37) | copy-start | bytes 98308

commit v8 on v7

--- a/solution.py
+++ b/solution.py
@@ -338,7 +338,7 @@
                 ref[pl.ds(base + 16, 16), 128 * m : 128 * m + 128] = high.astype(BF16)
         return carry
 
-    lax.fori_loop(0, 16, assemble, 0)
+    lax.fori_loop(0, 16, assemble, 0, unroll=True)
 
     def multiply(g, carry):
         base = pl.multiple_of(g * 128, 128)
@@ -353,7 +353,7 @@
                 out_ref[(g * 4 + part) * 8 + 2 * m + 1] = odd.astype(BF16)
         return carry
 
-    lax.fori_loop(0, 4, multiply, 0)
+    lax.fori_loop(0, 4, multiply, 0, unroll=True)
 
 
 def triangle(blocks):
@@ -505,10 +505,13 @@
         factors.reshape(128, 80, 128), ALL, split_axis=0, concat_axis=0, tiled=True
     )
     out_seq, factors = lax.optimization_barrier((out_seq, factors))
+    factors, far_factors = lax.optimization_barrier(
+        (factors, lax.ppermute(factors, "core", swap))
+    )
     factors = factors.reshape(640, 16, 128)
+    left = factors[:, :8].reshape(640, 1024)
     right_own = factors[:, 8:].reshape(640, 1024)
-    right_other = lax.ppermute(right_own, "core", swap)
-    left = factors[:, :8].reshape(640, 1024)
+    right_other = far_factors.reshape(640, 16, 128)[:, 8:].reshape(640, 1024)
     alignment_output = lax.all_to_all(
         out_seq, ROW, split_axis=0, concat_axis=0, tiled=True
     ).reshape(80, 32, 256)

time: 190 us -> 185 us (0.974)
  local copies, waits for them, and re-layouts: 17 us -> 10.2 us
  waiting for transfers between devices: 28.3 us -> 34.4 us
  Pallas kernels: 40.6 us -> 37.4 us
    unnamed x46 -> x43, local copies, waits for them, and re-layouts: 11.6 us -> 4.34 us
    all_to_all x1, waiting for transfers between devices: 3.08 us -> 8.49 us  [body(): lax.all_to_all(pair_bias(pairwise, bias_project.T).reshape(32, 64, 128),...]
    all_to_all x1, waiting for transfers between devices: 6.13 us -> 3.56 us  [body(): lax.all_to_all(out_seq, ROW, split_axis=0, concat_axis=0, tiled=True)]
  transfers between devices with their start and end apart: 13 -> 13, of which waited for: 6 -> 7; matrix products, arithmetic and copies ran while one was open for 6% -> 4% of each run, Pallas kernels for 6% -> 6%
where the time goes in v8:
time: 185 us; the launch traced here: 184 us
  blocking collectives  64.2 us (35%)
  Pallas kernels  37.4 us (20%)
  starting transfers between devices  35.7 us (19%)
  waiting for transfers between devices  34.4 us (19%)
  local copies, waits for them, and re-layouts  10.2 us (6%)
    all_to_all x1, blocking collectives, body(): lax.all_to_all(factors.reshape(128, 80, 128), ALL, split_axis=0, concat_a...  41.2 us
    all_to_all x1, blocking collectives, body(): blocks = lax.all_to_all(tri, ALL, split_axis=0, concat_axis=0, tiled=True)  23 us
    pallas_call x1, Pallas kernels, attention(): pl.pallas_call(attention_kernel, grid=(count,), in_specs=[smem, *(whole(b...  21 us
    all_to_all x1, waiting for transfers between devices, body(): lax.all_to_all(product, ALL, split_axis=0, concat_axis=0, tiled=True)  11.6 us
    all_to_all x1, starting transfers between devices, body(): lax.all_to_all(pair_bias(pairwise, bias_project.T).reshape(32, 64, 128),...  9.43 us
    all_to_all x1, waiting for transfers between devices, body(): lax.all_to_all(pair_bias(pairwise, bias_project.T).reshape(32, 64, 128),...  8.49 us
    pallas_call x1, Pallas kernels, outer_update(): pl.pallas_call(outer_kernel, in_specs=[pl.BlockSpec(memory_space=pltpu.SM...  8.24 us
    ppermute x1, waiting for transfers between devices, body(): left_plane = lax.ppermute(bias_plane, 'y', up)  5.89 us
  transfers between devices with their start and end apart: 13, of which 7 were waited for; matrix products, arithmetic and copies ran while one was open for 4% of the time, Pallas kernels for 6%

profile of v8, /device:TPU:1, one launch (start us, length us, event | category | flops | bytes accessed | tf_op | source)
XLA Modules:
  0.0 184.2 jit_solution(15664081917443947866)
XLA Ops:
  0.6 0.0 copy-start
  0.6 1.0 copy-done
  1.7 0.7 copy-done.3
  2.4 2.1 %pair_bias.1 = bf16[8,2,2,64,128]{4,3,2,1,0:T(8,128)(2,1)} custom-call(bf16[32,64,128]{2,1,0:T(8,128)(2,1)S(1)} %copy-done, bf16[8,128]{1,0:T(8,128)(2,1)S(1)} %bitcast.60), custom_call_target="tpu_custom_call" | custom-call | tf_op jit(solution)/shard_map/pair_bias/pallas_call | solution.py:61
  4.5 9.4 %all-to-all-start = ((bf16[32,64,128]{2,1,0:T(8,128)(2,1)}), bf16[32,64,128]{2,1,0:T(8,128)(2,1)S(1)}, u32[]{:S(2)}, u32[]{:S(2)}) async-start(bf16[32,64,128]{2,1,0:T(8,128)(2,1)} %bitcast.2), calls=%async_computation | async-start | bytes 1048576 | tf_op jit(solution)/shard_map/all_to_all | solution.py:446
  14.0 0.6 convert_reduce_fusion
  14.6 0.1 dynamic_slice.11
  14.6 0.1 dynamic_slice.10
  14.7 0.1 dynamic_slice.9
  14.8 0.1 mul.73
  14.9 0.1 mul.80
  15.0 0.1 copy.38
  15.1 0.1 mul.75
  15.1 0.1 mul.76
  15.2 0.1 copy.37
  15.4 0.1 copy.36
  15.5 0.0 copy-start.12
  15.5 0.1 copy.35
  15.6 0.0 copy-start.10
  15.7 0.3 copy.39
  16.0 0.4 copy-done.12
  16.5 0.6 maximum_divide_fusion
  17.1 0.1 pad_add_fusion.place_ref
  17.1 8.5 %all-to-all-done.in_ref = bf16[32,64,128]{2,1,0:T(8,128)(2,1)S(1)} async-done(((bf16[32,64,128]{2,1,0:T(8,128)(2,1)}), bf16[32,64,128]{2,1,0:T(8,128)(2,1)S(1)}, u32[]{:S(2)}, u32[]{:S(2)}) %all-to-all-start) | async-done | bytes 524320 | tf_op jit(solution)/shard_map/all_to_all | solution.py:446
  25.6 0.1 broadcast_in_dim.2.live_col_ref
  25.8 0.5 bias_plane.1.own0_ref
  26.2 1.4 collective-permute-start
  27.6 1.5 collective-permute-start.2
  29.1 5.4 %all-to-all-start.1 = ((bf16[16,5,32,256]{3,2,1,0:T(8,128)(2,1)}), bf16[16,5,32,256]{3,2,1,0:T(8,128)(2,1)}, u32[]{:S(2)}, u32[]{:S(2)}) async-start(bf16[16,5,32,256]{3,2,1,0:T(8,128)(2,1)} %bitcast.17), calls=%async_computation.1 | async-start | bytes 2621440 | tf_op jit(solution)/shard_map/all_to_all | solution.py:502
  34.5 5.9 %collective-permute-done.own1_ref = bf16[4,128,512]{2,1,0:T(8,128)(2,1)S(1)} collective-permute-done((bf16[4,128,512]{2,1,0:T(8,128)(2,1)S(1)}, bf16[4,128,512]{2,1,0:T(8,128)(2,1)S(1)}, u32[]{:S(2)}, u32[]{:S(2)}) %collective-permute-start) | collective-permute-done | bytes 524320 | tf_op jit(solution)/shard_map/ppermute | solution.py:495
  40.4 0.1 collective-permute-start.1
  40.5 0.0 collective-permute-done.2.own3_ref
  40.5 0.0 copy-start.5
  40.6 2.7 %collective-permute-start.3 = (bf16[2,128,512]{2,1,0:T(8,128)(2,1)S(1)}, bf16[2,128,512]{2,1,0:T(8,128)(2,1)S(1)}, u32[]{:S(2)}, u32[]{:S(2)}) collective-permute-start(bf16[2,128,512]{2,1,0:T(8,128)(2,1)S(1)} %slice.29), channel_id=1, source_target_pairs={{0,3},{1,0},{2,1},{3,2},{4,7},{5,4},{6,5},{7,6},{8,11},{9,8},{10,9... | collective-permute-start | bytes 786440 | tf_op jit(solution)/shard_map/ppermute | solution.py:498
  43.3 2.1 %collective-permute-start.4 = (bf16[4,128,512]{2,1,0:T(8,128)(2,1)S(1)}, bf16[4,128,512]{2,1,0:T(8,128)(2,1)S(1)}, u32[]{:S(2)}, u32[]{:S(2)}) collective-permute-start(bf16[4,128,512]{2,1,0:T(8,128)(2,1)S(1)} %bias_plane.1.own0_ref), channel_id=1, source_target_pairs={{0,8},{8,0},{1,9},{9,1},{2,10},{10,2},{3,11},{11,3},{4,12},{12,4},... | collective-permute-start | bytes 1572872 | tf_op jit(solution)/shard_map/ppermute | solution.py:501
  45.4 0.5 collective-permute-start.5
  45.9 2.1 %collective-permute-done.1 = bf16[2,128,512]{2,1,0:T(8,128)(2,1)S(1)} collective-permute-done((bf16[2,128,512]{2,1,0:T(8,128)(2,1)S(1)}, bf16[2,128,512]{2,1,0:T(8,128)(2,1)S(1)}, u32[]{:S(2)}, u32[]{:S(2)}) %collective-permute-start.1) | collective-permute-done | bytes 262176 | tf_op jit(solution)/shard_map/ppermute | solution.py:498
  48.0 2.5 %collective-permute-start.6 = (bf16[4,128,512]{2,1,0:T(8,128)(2,1)S(1)}, bf16[4,128,512]{2,1,0:T(8,128)(2,1)}, u32[]{:S(2)}, u32[]{:S(2)}) collective-permute-start(bf16[4,128,512]{2,1,0:T(8,128)(2,1)S(1)} %constant_dynamic-update-slice_fusion.7.own2_ref), channel_id=1, source_target_pairs={{0,8},{8,0},{1,9},{9,1},{2,10},{10,2},{3,11},{11,3},{4,12},{12,4},... | collective-permute-start | bytes 1572872 | tf_op jit(solution)/shard_map/ppermute | solution.py:501
  50.6 0.8 copy-done.7
  51.4 1.8 all-to-all-done.1.x_ref
  53.2 21.0 %row_attention.1 = (bf16[16,5,32,256]{3,2,1,0:T(8,128)(2,1)}, bf16[8,2,8,5,16,128]{5,4,3,2,1,0:T(8,128)(2,1)}) custom-call(s32[7]{0:T(128)S(1)} %pad_add_fusion.place_ref, bf16[4,128,512]{2,1,0:T(8,128)(2,1)S(1)} %bias_plane.1.own0_ref, bf16[4,128,512]{2,1,0:T(8,128)(2,1)S(1)} %collective-permute-done.own1_ref, ...), custom_call_target="tpu_custom_call" | custom-call | tf_op jit(solution)/shard_map/row_attention/pallas_call | solution.py:219
  74.2 41.2 %all_to_all.30 = bf16[128,80,128]{2,1,0:T(8,128)(2,1)} all-to-all(bf16[128,80,128]{2,1,0:T(8,128)(2,1)} %bitcast.65), channel_id=1, replica_groups=mesh['x'=4,'zl'=2,'core'=2,'zh'=2,'y'=4] {'x','zl','core','zh','y'}, dimensions={0} | all-to-all | bytes 5242880 | tf_op jit(solution)/shard_map/all_to_all | solution.py:504
  115.4 1.6 collective-permute-start.8
  117.0 3.8 %all-to-all-start.3 = ((bf16[16,5,32,256]{3,2,1,0:T(8,128)(2,1)}), bf16[16,5,32,256]{3,2,1,0:T(8,128)(2,1)S(1)}, u32[]{:S(2)}, u32[]{:S(2)}) async-start(bf16[16,5,32,256]{3,2,1,0:T(8,128)(2,1)} %get-tuple-element.41), calls=%async_computation.3 | async-start | bytes 2621440 | tf_op jit(solution)/shard_map/all_to_all | solution.py:515
  120.8 0.1 copy.40.w_ref
  120.9 0.9 collective-permute-done.8
  121.9 1.4 slice.32
  123.3 1.9 %fusion = (bf16[640,8,128]{2,1,0:T(8,128)(2,1)S(1)}, bf16[640,8,128]{2,1,0:T(8,128)(2,1)S(1)}) fusion(bf16[640,16,128]{2,1,0:T(8,128)(2,1)} %bitcast.19), kind=kLoop, calls=%fused_computation.18 | loop fusion | bytes 5242880 | tf_op jit(solution)/shard_map/slice | solution.py:513
  125.2 0.4 copy.51
  125.5 0.0 copy-start.1
  125.6 0.7 copy_bitcast_fusion
  126.3 0.3 copy-done.1
  126.6 8.2 %outer_update.1 = (bf16[4,8,64,128]{3,2,1,0:T(8,128)(2,1)S(1)}, bf16[2,8,256,128]{3,2,1,0:T(8,128)(2,1)S(1)}) custom-call(s32[1]{0:T(128)} %bitcast.core_ref, bf16[640,1024]{1,0:T(8,128)(2,1)S(1)} %bitcast.51, bf16[640,1024]{1,0:T(8,128)(2,1)S(1)} %get-tuple-element.53.own_ref, bf16[640,1024]{1,0:T(8,128)(2,1)S(1)} %get-tuple-element.52.other_ref, ...), custom_call_target="tpu_custom_call" | custom-call | tf_op jit(solution)/shard_map/outer_update/pallas_call | solution.py:316
  134.8 0.7 copy.52
  135.5 3.6 %all-to-all-done.3 = bf16[16,5,32,256]{3,2,1,0:T(8,128)(2,1)S(1)} async-done(((bf16[16,5,32,256]{3,2,1,0:T(8,128)(2,1)}), bf16[16,5,32,256]{3,2,1,0:T(8,128)(2,1)S(1)}, u32[]{:S(2)}, u32[]{:S(2)}) %all-to-all-start.3) | async-done | bytes 1310752 | tf_op jit(solution)/shard_map/all_to_all | solution.py:515
  139.1 23.0 %all_to_all.31.in_ref = bf16[128,2,16,128]{3,2,1,0:T(8,128)(2,1)S(1)} all-to-all(bf16[128,2,16,128]{3,2,1,0:T(8,128)(2,1)S(1)} %bitcast.64), channel_id=1, replica_groups=mesh['x'=4,'zl'=2,'core'=2,'zh'=2,'y'=4] {'x','zl','core','zh','y'}, dimensions={0} | all-to-all | bytes 2097152 | tf_op jit(solution)/shard_map/all_to_all | solution.py:533
  162.1 1.9 %triangle.1 = bf16[128,16,128]{2,1,0:T(8,128)(2,1)} custom-call(bf16[128,2,16,128]{3,2,1,0:T(8,128)(2,1)S(1)} %all_to_all.31.in_ref), custom_call_target="tpu_custom_call" | custom-call | tf_op jit(solution)/shard_map/triangle/pallas_call | solution.py:360
  163.9 4.7 %all-to-all-start.5 = ((bf16[128,16,128]{2,1,0:T(8,128)(2,1)}), bf16[128,16,128]{2,1,0:T(8,128)(2,1)S(1)}, u32[]{:S(2)}, u32[]{:S(2)}) async-start(bf16[128,16,128]{2,1,0:T(8,128)(2,1)} %triangle.1), calls=%async_computation.5 | async-start | bytes 1048576 | tf_op jit(solution)/shard_map/all_to_all | solution.py:535
  168.7 0.0 copy-start.2
  168.7 1.1 copied.1
  169.8 1.2 pair_gate.1.gate_ref
  171.0 11.6 %all-to-all-done.5 = bf16[128,16,128]{2,1,0:T(8,128)(2,1)S(1)} async-done(((bf16[128,16,128]{2,1,0:T(8,128)(2,1)}), bf16[128,16,128]{2,1,0:T(8,128)(2,1)S(1)}, u32[]{:S(2)}, u32[]{:S(2)}) %all-to-all-start.5) | async-done | bytes 524320 | tf_op jit(solution)/shard_map/all_to_all | solution.py:535
  182.6 0.1 copy.53
  182.7 1.4 pair_final.1
  (40 shorter events, 0.2 us)
Async XLA Ops:
  0.6 1.0 copy-start
  1.7 0.7 copy-start.3
  2.4 11.6 %copy-start.14 = (s32[640]{0:T(1024)S(1)}, s32[640]{0:T(1024)}, u32[]{:S(2)}) copy-start(s32[640]{0:T(1024)} %param.15) | copy-start | bytes 7684
  2.4 12.3 %copy-start.15 = (s32[512]{0:T(512)S(1)}, s32[512]{0:T(512)}, u32[]{:S(2)}) copy-start(s32[512]{0:T(512)} %param.14) | copy-start | bytes 6148
  2.4 12.9 %copy-start.13 = (bf16[128,128]{1,0:T(8,128)(2,1)S(1)}, bf16[128,128]{1,0:T(8,128)(2,1)}, u32[]{:S(2)}) copy-start(bf16[128,128]{1,0:T(8,128)(2,1)} %param.23) | copy-start | bytes 98308
  2.4 13.0 %copy-start.11 = (bf16[128,4,128]{2,1,0:T(4,128)(2,1)S(1)}, bf16[128,4,128]{2,1,0:T(4,128)(2,1)}, u32[]{:S(2)}) copy-start(bf16[128,4,128]{2,1,0:T(4,128)(2,1)} %param.21) | copy-start | bytes 393220
  2.4 13.1 %copy-start.9 = (bf16[1024,128]{1,0:T(8,128)(2,1)S(1)}, bf16[1024,128]{1,0:T(8,128)(2,1)}, u32[]{:S(2)}) copy-start(bf16[1024,128]{1,0:T(8,128)(2,1)} %param.20) | copy-start | bytes 786436
  2.4 13.3 %copy-start.8 = (bf16[256,4,256]{2,1,0:T(4,128)(2,1)S(1)}, bf16[256,4,256]{2,1,0:T(4,128)(2,1)}, u32[]{:S(2)}) copy-start(bf16[256,4,256]{2,1,0:T(4,128)(2,1)} %param.16) | copy-start | bytes 1572868
  4.5 21.1 %all-to-all-start = ((bf16[32,64,128]{2,1,0:T(8,128)(2,1)}), bf16[32,64,128]{2,1,0:T(8,128)(2,1)S(1)}, u32[]{:S(2)}, u32[]{:S(2)}) async-start(bf16[32,64,128]{2,1,0:T(8,128)(2,1)} %bitcast.2), calls=%async_computation | async-start | bytes 1048576 | tf_op jit(solution)/shard_map/all_to_all | solution.py:446
  15.5 0.9 copy-start.12
  15.6 0.8 copy-start.10
  17.1 12.0 %copy-start.4 = (bf16[1440,256]{1,0:T(8,128)(2,1)}, bf16[1440,256]{1,0:T(8,128)(2,1)S(1)}, u32[]{:S(2)}) copy-start(bf16[1440,256]{1,0:T(8,128)(2,1)S(1)} %constant_dynamic-update-slice_fusion.win_ref) | copy-start | bytes 2211844
  26.2 14.1 %collective-permute-start = (bf16[4,128,512]{2,1,0:T(8,128)(2,1)S(1)}, bf16[4,128,512]{2,1,0:T(8,128)(2,1)S(1)}, u32[]{:S(2)}, u32[]{:S(2)}) collective-permute-start(bf16[4,128,512]{2,1,0:T(8,128)(2,1)S(1)} %bias_plane.1.own0_ref), channel_id=1, source_target_pairs={{0,1},{1,2},{2,3},{3,0},{4,5},{5,6},{6,7},{7,4},{8,9},{9,10},{10,1... | collective-permute-start | bytes 1572872 | tf_op jit(solution)/shard_map/ppermute | solution.py:495
  27.6 12.9 %collective-permute-start.2 = (bf16[4,128,512]{2,1,0:T(8,128)(2,1)S(1)}, bf16[4,128,512]{2,1,0:T(8,128)(2,1)S(1)}, u32[]{:S(2)}, u32[]{:S(2)}) collective-permute-start(bf16[4,128,512]{2,1,0:T(8,128)(2,1)S(1)} %bias_plane.1.own0_ref), channel_id=1, source_target_pairs={{0,3},{1,0},{2,1},{3,2},{4,7},{5,4},{6,5},{7,6},{8,11},{9,8},{10,9... | collective-permute-start | bytes 1572872 | tf_op jit(solution)/shard_map/ppermute | solution.py:496
  29.1 24.1 %all-to-all-start.1 = ((bf16[16,5,32,256]{3,2,1,0:T(8,128)(2,1)}), bf16[16,5,32,256]{3,2,1,0:T(8,128)(2,1)}, u32[]{:S(2)}, u32[]{:S(2)}) async-start(bf16[16,5,32,256]{3,2,1,0:T(8,128)(2,1)} %bitcast.17), calls=%async_computation.1 | async-start | bytes 2621440 | tf_op jit(solution)/shard_map/all_to_all | solution.py:502
  40.4 7.5 %collective-permute-start.1 = (bf16[2,128,512]{2,1,0:T(8,128)(2,1)S(1)}, bf16[2,128,512]{2,1,0:T(8,128)(2,1)S(1)}, u32[]{:S(2)}, u32[]{:S(2)}) collective-permute-start(bf16[2,128,512]{2,1,0:T(8,128)(2,1)S(1)} %slice.28), channel_id=1, source_target_pairs={{0,1},{1,2},{2,3},{3,0},{4,5},{5,6},{6,7},{7,4},{8,9},{9,10},{10,1... | collective-permute-start | bytes 786440 | tf_op jit(solution)/shard_map/ppermute | solution.py:498
  40.5 12.7 %copy-start.5 = (bf16[4,128,512]{2,1,0:T(8,128)(2,1)}, bf16[4,128,512]{2,1,0:T(8,128)(2,1)S(1)}, u32[]{:S(2)}) copy-start(bf16[4,128,512]{2,1,0:T(8,128)(2,1)S(1)} %collective-permute-done.2.own3_ref) | copy-start | bytes 1572868
  40.6 7.4 %collective-permute-start.3 = (bf16[2,128,512]{2,1,0:T(8,128)(2,1)S(1)}, bf16[2,128,512]{2,1,0:T(8,128)(2,1)S(1)}, u32[]{:S(2)}, u32[]{:S(2)}) collective-permute-start(bf16[2,128,512]{2,1,0:T(8,128)(2,1)S(1)} %slice.29), channel_id=1, source_target_pairs={{0,3},{1,0},{2,1},{3,2},{4,7},{5,4},{6,5},{7,6},{8,11},{9,8},{10,9... | collective-permute-start | bytes 786440 | tf_op jit(solution)/shard_map/ppermute | solution.py:498
  43.3 7.3 %collective-permute-start.4 = (bf16[4,128,512]{2,1,0:T(8,128)(2,1)S(1)}, bf16[4,128,512]{2,1,0:T(8,128)(2,1)S(1)}, u32[]{:S(2)}, u32[]{:S(2)}) collective-permute-start(bf16[4,128,512]{2,1,0:T(8,128)(2,1)S(1)} %bias_plane.1.own0_ref), channel_id=1, source_target_pairs={{0,8},{8,0},{1,9},{9,1},{2,10},{10,2},{3,11},{11,3},{4,12},{12,4},... | collective-permute-start | bytes 1572872 | tf_op jit(solution)/shard_map/ppermute | solution.py:501
  45.4 5.2 %collective-permute-start.7 = (bf16[4,128,512]{2,1,0:T(8,128)(2,1)S(1)}, bf16[4,128,512]{2,1,0:T(8,128)(2,1)S(1)}, u32[]{:S(2)}, u32[]{:S(2)}) collective-permute-start(bf16[4,128,512]{2,1,0:T(8,128)(2,1)S(1)} %collective-permute-done.2.own3_ref), channel_id=1, source_target_pairs={{0,8},{8,0},{1,9},{9,1},{2,10},{10,2},{3,11},{11,3},{4,12},{12,4},... | collective-permute-start | bytes 1572872 | tf_op jit(solution)/shard_map/ppermute | solution.py:501
  45.4 6.1 %collective-permute-start.5 = (bf16[4,128,512]{2,1,0:T(8,128)(2,1)S(1)}, bf16[4,128,512]{2,1,0:T(8,128)(2,1)}, u32[]{:S(2)}, u32[]{:S(2)}) collective-permute-start(bf16[4,128,512]{2,1,0:T(8,128)(2,1)S(1)} %collective-permute-done.own1_ref), channel_id=1, source_target_pairs={{0,8},{8,0},{1,9},{9,1},{2,10},{10,2},{3,11},{11,3},{4,12},{12,4},... | collective-permute-start | bytes 1572872 | tf_op jit(solution)/shard_map/ppermute | solution.py:501
  48.0 5.2 %collective-permute-start.6 = (bf16[4,128,512]{2,1,0:T(8,128)(2,1)S(1)}, bf16[4,128,512]{2,1,0:T(8,128)(2,1)}, u32[]{:S(2)}, u32[]{:S(2)}) collective-permute-start(bf16[4,128,512]{2,1,0:T(8,128)(2,1)S(1)} %constant_dynamic-update-slice_fusion.7.own2_ref), channel_id=1, source_target_pairs={{0,8},{8,0},{1,9},{9,1},{2,10},{10,2},{3,11},{11,3},{4,12},{12,4},... | collective-permute-start | bytes 1572872 | tf_op jit(solution)/shard_map/ppermute | solution.py:501
  50.6 2.7 %copy-start.6 = (bf16[4,128,512]{2,1,0:T(8,128)(2,1)}, bf16[4,128,512]{2,1,0:T(8,128)(2,1)S(1)}, u32[]{:S(2)}) copy-start(bf16[4,128,512]{2,1,0:T(8,128)(2,1)S(1)} %collective-permute-done.4.other0_ref) | copy-start | bytes 1572868
  50.6 0.9 copy-start.7
  115.4 6.4 %collective-permute-start.8 = (bf16[128,80,128]{2,1,0:T(8,128)(2,1)}, bf16[128,80,128]{2,1,0:T(8,128)(2,1)}, u32[]{:S(2)}, u32[]{:S(2)}) collective-permute-start(bf16[128,80,128]{2,1,0:T(8,128)(2,1)} %all_to_all.30), channel_id=1, source_target_pairs={{0,8},{8,0},{1,9},{9,1},{2,10},{10,2},{3,11},{11,3},{4,12},{12,4},... | collective-permute-start | bytes 7864328 | tf_op jit(solution)/shard_map/ppermute | solution.py:509
  117.0 22.1 %all-to-all-start.3 = ((bf16[16,5,32,256]{3,2,1,0:T(8,128)(2,1)}), bf16[16,5,32,256]{3,2,1,0:T(8,128)(2,1)S(1)}, u32[]{:S(2)}, u32[]{:S(2)}) async-start(bf16[16,5,32,256]{3,2,1,0:T(8,128)(2,1)} %get-tuple-element.41), calls=%async_computation.3 | async-start | bytes 2621440 | tf_op jit(solution)/shard_map/all_to_all | solution.py:515
  125.5 1.0 copy-start.1
  163.9 18.7 %all-to-all-start.5 = ((bf16[128,16,128]{2,1,0:T(8,128)(2,1)}), bf16[128,16,128]{2,1,0:T(8,128)(2,1)S(1)}, u32[]{:S(2)}, u32[]{:S(2)}) async-start(bf16[128,16,128]{2,1,0:T(8,128)(2,1)} %triangle.1), calls=%async_computation.5 | async-start | bytes 1048576 | tf_op jit(solution)/shard_map/all_to_all | solution.py:535
  168.7 1.2 copy-start.2

commit v9 on v8

--- a/solution.py
+++ b/solution.py
@@ -120,29 +120,32 @@
     vt_ref,
     acc_ref,
     live_ref,
+    plane_ref,
+    sem_ref,
 ):
     heads = bias_ref.shape[0]
     step = pl.program_id(0)
 
+    copies = [
+        pltpu.make_async_copy(ref, plane_ref.at[n], sem_ref.at[n])
+        for n, ref in enumerate(
+            (
+                own0_ref,
+                own1_ref,
+                own2_ref,
+                own3_ref,
+                other0_ref,
+                other1_ref,
+                other2_ref,
+                other3_ref,
+            )
+        )
+    ]
+
     @pl.when(step == 0)
     def _():
-        live_ref[...] = live_col_ref[...].T[:8]
-        core, y = place_ref[0], place_ref[1]
-        own = (own0_ref, own1_ref, own2_ref, own3_ref)
-        other = (other0_ref, other1_ref, other2_ref, other3_ref)
-        for refs, side in ((own, core), (other, 1 - core)):
-            for d in range(4):
-                source = lax.rem(y + 4 - d, 4)
-                for zh in range(2):
-                    rows = pl.ds(pl.multiple_of(256 * zh + 64 * source, 64), 64)
-                    penalty = (live_col_ref[rows, :] - 1.0) * BIG
-                    for m in range(4):
-                        lanes = slice(128 * m, 128 * m + 128)
-                        for hh in range(4):
-                            bias_ref[4 * side + hh, rows, lanes] = (
-                                refs[d][hh, 64 * zh : 64 * zh + 64, lanes].astype(F32) * LOG2E
-                                + penalty
-                            )
+        for copy in copies:
+            copy.start()
 
     x = x_ref[:, 0].reshape(512, 256)
     normed = layer_norm(x).astype(BF16)
@@ -158,6 +161,23 @@
     ).astype(BF16)
     vt_ref[:, :32] = project(2).astype(BF16).reshape(heads, 32, 512)
     vt_ref[:, 32:] = jnp.ones((heads, 16, 512), BF16)
+    @pl.when(step == 0)
+    def _():
+        live_ref[...] = live_col_ref[...].T[:8]
+        core, y = place_ref[0], place_ref[1]
+        for n, copy in enumerate(copies):
+            copy.wait()
+            side = core if n < 4 else 1 - core
+            source = lax.rem(y + 4 - n % 4, 4)
+            for zh in range(2):
+                rows = pl.ds(pl.multiple_of(256 * zh + 64 * source, 64), 64)
+                penalty = (live_col_ref[rows, :] - 1.0) * BIG
+                for m in range(4):
+                    lanes = slice(128 * m, 128 * m + 128)
+                    for hh in range(4):
+                        part = plane_ref[n, hh, 64 * zh : 64 * zh + 64, lanes]
+                        bias_ref[4 * side + hh, rows, lanes] = part.astype(F32) * LOG2E + penalty
+
     row_head = lax.broadcasted_iota(jnp.int32, (128, 512), 0) // 32
 
     def scores(h):
@@ -221,7 +241,7 @@
         grid=(count,),
         in_specs=[
             smem,
-            *(whole(b) for b in biases),
+            *(pl.BlockSpec(memory_space=pl.ANY) for _ in biases),
             per_seq(16, 1, 32, 256),
             whole(win),
             whole(live_col),
@@ -241,6 +261,8 @@
             pltpu.VMEM((8, 48, 512), BF16),
             pltpu.VMEM((256, 512), F32),
             pltpu.VMEM((8, 512), F32),
+            pltpu.VMEM((8, 4, 128, 512), BF16),
+            pltpu.SemaphoreType.DMA((8,)),
         ],
         compiler_params=params(52),
         name="row_attention",

time: 185 us -> 189 us (1.022)
  Pallas kernels: 37.4 us -> 41.8 us
    pallas_call x1, Pallas kernels: 21 us -> 25.4 us  [attention(): pl.pallas_call(attention_kernel, grid=(count,), in_specs=[smem, *(pl.Bloc...]
where the time goes in v9:
time: 189 us
  blocking collectives  64.2 us (34%)
  Pallas kernels  41.8 us (22%)
  starting transfers between devices  35.7 us (19%)
  waiting for transfers between devices  34.6 us (18%)
  local copies, waits for them, and re-layouts  10.2 us (5%)
    all_to_all x1, blocking collectives, body(): lax.all_to_all(factors.reshape(128, 80, 128), ALL, split_axis=0, concat_a...  41.2 us
    pallas_call x1, Pallas kernels, attention(): pl.pallas_call(attention_kernel, grid=(count,), in_specs=[smem, *(pl.Bloc...  25.4 us
    all_to_all x1, blocking collectives, body(): blocks = lax.all_to_all(tri, ALL, split_axis=0, concat_axis=0, tiled=True)  23 us
    all_to_all x1, waiting for transfers between devices, body(): lax.all_to_all(product, ALL, split_axis=0, concat_axis=0, tiled=True)  11.6 us
    all_to_all x1, starting transfers between devices, body(): lax.all_to_all(pair_bias(pairwise, bias_project.T).reshape(32, 64, 128),...  9.43 us
    all_to_all x1, waiting for transfers between devices, body(): lax.all_to_all(pair_bias(pairwise, bias_project.T).reshape(32, 64, 128),...  8.49 us
    pallas_call x1, Pallas kernels, outer_update(): pl.pallas_call(outer_kernel, in_specs=[pl.BlockSpec(memory_space=pltpu.SM...  8.25 us
    ppermute x1, waiting for transfers between devices, body(): left_plane = lax.ppermute(bias_plane, 'y', up)  5.89 us
  transfers between devices with their start and end apart: 13, of which 7 were waited for; matrix products, arithmetic and copies ran while one was open for 4% of the time, Pallas kernels for 6%

profile of v9, /device:TPU:1, one launch (start us, length us, event | category | flops | bytes accessed | tf_op | source)
XLA Modules:
  0.0 188.7 jit_solution(138830595686406841)
XLA Ops:
  0.6 0.0 copy-start
  0.6 1.0 copy-done
  1.7 0.7 copy-done.3
  2.4 2.1 %pair_bias.1 = bf16[8,2,2,64,128]{4,3,2,1,0:T(8,128)(2,1)} custom-call(bf16[32,64,128]{2,1,0:T(8,128)(2,1)S(1)} %copy-done, bf16[8,128]{1,0:T(8,128)(2,1)S(1)} %bitcast.60), custom_call_target="tpu_custom_call" | custom-call | tf_op jit(solution)/shard_map/pair_bias/pallas_call | solution.py:61
  4.5 9.4 %all-to-all-start = ((bf16[32,64,128]{2,1,0:T(8,128)(2,1)}), bf16[32,64,128]{2,1,0:T(8,128)(2,1)S(1)}, u32[]{:S(2)}, u32[]{:S(2)}) async-start(bf16[32,64,128]{2,1,0:T(8,128)(2,1)} %bitcast.2), calls=%async_computation | async-start | bytes 1048576 | tf_op jit(solution)/shard_map/all_to_all | solution.py:468
  14.0 0.6 convert_reduce_fusion
  14.6 0.1 dynamic_slice.11
  14.6 0.1 dynamic_slice.10
  14.7 0.1 dynamic_slice.9
  14.8 0.1 mul.73
  14.9 0.1 mul.80
  15.0 0.1 copy.38
  15.1 0.1 mul.75
  15.1 0.1 mul.76
  15.2 0.1 copy.37
  15.4 0.1 copy.36
  15.5 0.0 copy-start.12
  15.5 0.1 copy.35
  15.6 0.0 copy-start.10
  15.7 0.3 copy.39
  16.0 0.4 copy-done.12
  16.5 0.6 maximum_divide_fusion
  17.1 0.1 pad_add_fusion.place_ref
  17.1 8.5 %all-to-all-done.in_ref = bf16[32,64,128]{2,1,0:T(8,128)(2,1)S(1)} async-done(((bf16[32,64,128]{2,1,0:T(8,128)(2,1)}), bf16[32,64,128]{2,1,0:T(8,128)(2,1)S(1)}, u32[]{:S(2)}, u32[]{:S(2)}) %all-to-all-start) | async-done | bytes 524320 | tf_op jit(solution)/shard_map/all_to_all | solution.py:468
  25.6 0.1 broadcast_in_dim.2.live_col_ref
  25.8 0.5 bias_plane.1.own0_ref
  26.2 1.4 collective-permute-start
  27.6 1.5 collective-permute-start.2
  29.1 5.4 %all-to-all-start.1 = ((bf16[16,5,32,256]{3,2,1,0:T(8,128)(2,1)}), bf16[16,5,32,256]{3,2,1,0:T(8,128)(2,1)}, u32[]{:S(2)}, u32[]{:S(2)}) async-start(bf16[16,5,32,256]{3,2,1,0:T(8,128)(2,1)} %bitcast.17), calls=%async_computation.1 | async-start | bytes 2621440 | tf_op jit(solution)/shard_map/all_to_all | solution.py:524
  34.5 5.9 %collective-permute-done.own1_ref = bf16[4,128,512]{2,1,0:T(8,128)(2,1)S(1)} collective-permute-done((bf16[4,128,512]{2,1,0:T(8,128)(2,1)S(1)}, bf16[4,128,512]{2,1,0:T(8,128)(2,1)S(1)}, u32[]{:S(2)}, u32[]{:S(2)}) %collective-permute-start) | collective-permute-done | bytes 524320 | tf_op jit(solution)/shard_map/ppermute | solution.py:517
  40.4 0.1 collective-permute-start.1
  40.5 0.0 collective-permute-done.2.own3_ref
  40.5 0.0 copy-start.5
  40.6 2.7 %collective-permute-start.3 = (bf16[2,128,512]{2,1,0:T(8,128)(2,1)S(1)}, bf16[2,128,512]{2,1,0:T(8,128)(2,1)S(1)}, u32[]{:S(2)}, u32[]{:S(2)}) collective-permute-start(bf16[2,128,512]{2,1,0:T(8,128)(2,1)S(1)} %slice.29), channel_id=1, source_target_pairs={{0,3},{1,0},{2,1},{3,2},{4,7},{5,4},{6,5},{7,6},{8,11},{9,8},{10,9... | collective-permute-start | bytes 786440 | tf_op jit(solution)/shard_map/ppermute | solution.py:520
  43.3 2.1 %collective-permute-start.4 = (bf16[4,128,512]{2,1,0:T(8,128)(2,1)S(1)}, bf16[4,128,512]{2,1,0:T(8,128)(2,1)S(1)}, u32[]{:S(2)}, u32[]{:S(2)}) collective-permute-start(bf16[4,128,512]{2,1,0:T(8,128)(2,1)S(1)} %bias_plane.1.own0_ref), channel_id=1, source_target_pairs={{0,8},{8,0},{1,9},{9,1},{2,10},{10,2},{3,11},{11,3},{4,12},{12,4},... | collective-permute-start | bytes 1572872 | tf_op jit(solution)/shard_map/ppermute | solution.py:523
  45.4 0.5 collective-permute-start.5
  45.9 2.1 %collective-permute-done.1 = bf16[2,128,512]{2,1,0:T(8,128)(2,1)S(1)} collective-permute-done((bf16[2,128,512]{2,1,0:T(8,128)(2,1)S(1)}, bf16[2,128,512]{2,1,0:T(8,128)(2,1)S(1)}, u32[]{:S(2)}, u32[]{:S(2)}) %collective-permute-start.1) | collective-permute-done | bytes 262176 | tf_op jit(solution)/shard_map/ppermute | solution.py:520
  48.0 2.5 %collective-permute-start.6 = (bf16[4,128,512]{2,1,0:T(8,128)(2,1)S(1)}, bf16[4,128,512]{2,1,0:T(8,128)(2,1)}, u32[]{:S(2)}, u32[]{:S(2)}) collective-permute-start(bf16[4,128,512]{2,1,0:T(8,128)(2,1)S(1)} %constant_dynamic-update-slice_fusion.7.own2_ref), channel_id=1, source_target_pairs={{0,8},{8,0},{1,9},{9,1},{2,10},{10,2},{3,11},{11,3},{4,12},{12,4},... | collective-permute-start | bytes 1572872 | tf_op jit(solution)/shard_map/ppermute | solution.py:523
  50.6 0.8 copy-done.7
  51.4 1.8 all-to-all-done.1.x_ref
  53.2 25.4 %row_attention.1 = (bf16[16,5,32,256]{3,2,1,0:T(8,128)(2,1)}, bf16[8,2,8,5,16,128]{5,4,3,2,1,0:T(8,128)(2,1)}) custom-call(s32[7]{0:T(128)S(1)} %pad_add_fusion.place_ref, bf16[4,128,512]{2,1,0:T(8,128)(2,1)S(1)} %bias_plane.1.own0_ref, bf16[4,128,512]{2,1,0:T(8,128)(2,1)S(1)} %collective-permute-done.own1_ref, ...), custom_call_target="tpu_custom_call" | custom-call | tf_op jit(solution)/shard_map/row_attention/pallas_call | solution.py:239
  78.6 41.2 %all_to_all.30 = bf16[128,80,128]{2,1,0:T(8,128)(2,1)} all-to-all(bf16[128,80,128]{2,1,0:T(8,128)(2,1)} %bitcast.65), channel_id=1, replica_groups=mesh['x'=4,'zl'=2,'core'=2,'zh'=2,'y'=4] {'x','zl','core','zh','y'}, dimensions={0} | all-to-all | bytes 5242880 | tf_op jit(solution)/shard_map/all_to_all | solution.py:526
  119.8 1.6 collective-permute-start.8
  121.4 3.8 %all-to-all-start.3 = ((bf16[16,5,32,256]{3,2,1,0:T(8,128)(2,1)}), bf16[16,5,32,256]{3,2,1,0:T(8,128)(2,1)S(1)}, u32[]{:S(2)}, u32[]{:S(2)}) async-start(bf16[16,5,32,256]{3,2,1,0:T(8,128)(2,1)} %get-tuple-element.41), calls=%async_computation.3 | async-start | bytes 2621440 | tf_op jit(solution)/shard_map/all_to_all | solution.py:537
  125.2 0.1 copy.40.w_ref
  125.3 0.9 collective-permute-done.8
  126.3 1.4 slice.32
  127.7 1.9 fusion
  129.5 0.4 copy.51
  129.9 0.0 copy-start.1
  129.9 0.7 copy_bitcast_fusion
  130.7 0.3 copy-done.1
  131.0 8.2 %outer_update.1 = (bf16[4,8,64,128]{3,2,1,0:T(8,128)(2,1)S(1)}, bf16[2,8,256,128]{3,2,1,0:T(8,128)(2,1)S(1)}) custom-call(s32[1]{0:T(128)} %bitcast.core_ref, bf16[640,1024]{1,0:T(8,128)(2,1)S(1)} %bitcast.51, bf16[640,1024]{1,0:T(8,128)(2,1)S(1)} %get-tuple-element.53.own_ref, bf16[640,1024]{1,0:T(8,128)(2,1)S(1)} %get-tuple-element.52.other_ref, ...), custom_call_target="tpu_custom_call" | custom-call | tf_op jit(solution)/shard_map/outer_update/pallas_call | solution.py:338
  139.2 0.7 copy.52
  139.9 3.7 %all-to-all-done.3 = bf16[16,5,32,256]{3,2,1,0:T(8,128)(2,1)S(1)} async-done(((bf16[16,5,32,256]{3,2,1,0:T(8,128)(2,1)}), bf16[16,5,32,256]{3,2,1,0:T(8,128)(2,1)S(1)}, u32[]{:S(2)}, u32[]{:S(2)}) %all-to-all-start.3) | async-done | bytes 1310752 | tf_op jit(solution)/shard_map/all_to_all | solution.py:537
  143.7 23.0 %all_to_all.31.in_ref = bf16[128,2,16,128]{3,2,1,0:T(8,128)(2,1)S(1)} all-to-all(bf16[128,2,16,128]{3,2,1,0:T(8,128)(2,1)S(1)} %bitcast.64), channel_id=1, replica_groups=mesh['x'=4,'zl'=2,'core'=2,'zh'=2,'y'=4] {'x','zl','core','zh','y'}, dimensions={0} | all-to-all | bytes 2097152 | tf_op jit(solution)/shard_map/all_to_all | solution.py:555
  166.6 1.9 triangle.1
  168.5 4.7 %all-to-all-start.5 = ((bf16[128,16,128]{2,1,0:T(8,128)(2,1)}), bf16[128,16,128]{2,1,0:T(8,128)(2,1)S(1)}, u32[]{:S(2)}, u32[]{:S(2)}) async-start(bf16[128,16,128]{2,1,0:T(8,128)(2,1)} %triangle.1), calls=%async_computation.5 | async-start | bytes 1048576 | tf_op jit(solution)/shard_map/all_to_all | solution.py:557
  173.2 0.0 copy-start.2
  173.2 1.1 copied.1
  174.4 1.2 pair_gate.1.gate_ref
  175.5 11.6 %all-to-all-done.5 = bf16[128,16,128]{2,1,0:T(8,128)(2,1)S(1)} async-done(((bf16[128,16,128]{2,1,0:T(8,128)(2,1)}), bf16[128,16,128]{2,1,0:T(8,128)(2,1)S(1)}, u32[]{:S(2)}, u32[]{:S(2)}) %all-to-all-start.5) | async-done | bytes 524320 | tf_op jit(solution)/shard_map/all_to_all | solution.py:557
  187.2 0.1 copy.53
  187.3 1.4 pair_final.1
  (40 shorter events, 0.2 us)
Async XLA Ops:
  0.6 1.0 copy-start
  1.7 0.7 copy-start.3
  2.4 11.6 %copy-start.14 = (s32[640]{0:T(1024)S(1)}, s32[640]{0:T(1024)}, u32[]{:S(2)}) copy-start(s32[640]{0:T(1024)} %param.15) | copy-start | bytes 7684
  2.4 12.3 %copy-start.15 = (s32[512]{0:T(512)S(1)}, s32[512]{0:T(512)}, u32[]{:S(2)}) copy-start(s32[512]{0:T(512)} %param.14) | copy-start | bytes 6148
  2.4 12.9 %copy-start.13 = (bf16[128,128]{1,0:T(8,128)(2,1)S(1)}, bf16[128,128]{1,0:T(8,128)(2,1)}, u32[]{:S(2)}) copy-start(bf16[128,128]{1,0:T(8,128)(2,1)} %param.23) | copy-start | bytes 98308
  2.4 13.0 %copy-start.11 = (bf16[128,4,128]{2,1,0:T(4,128)(2,1)S(1)}, bf16[128,4,128]{2,1,0:T(4,128)(2,1)}, u32[]{:S(2)}) copy-start(bf16[128,4,128]{2,1,0:T(4,128)(2,1)} %param.21) | copy-start | bytes 393220
  2.4 13.1 %copy-start.9 = (bf16[1024,128]{1,0:T(8,128)(2,1)S(1)}, bf16[1024,128]{1,0:T(8,128)(2,1)}, u32[]{:S(2)}) copy-start(bf16[1024,128]{1,0:T(8,128)(2,1)} %param.20) | copy-start | bytes 786436
  2.4 13.3 %copy-start.8 = (bf16[256,4,256]{2,1,0:T(4,128)(2,1)S(1)}, bf16[256,4,256]{2,1,0:T(4,128)(2,1)}, u32[]{:S(2)}) copy-start(bf16[256,4,256]{2,1,0:T(4,128)(2,1)} %param.16) | copy-start | bytes 1572868
  4.5 21.1 %all-to-all-start = ((bf16[32,64,128]{2,1,0:T(8,128)(2,1)}), bf16[32,64,128]{2,1,0:T(8,128)(2,1)S(1)}, u32[]{:S(2)}, u32[]{:S(2)}) async-start(bf16[32,64,128]{2,1,0:T(8,128)(2,1)} %bitcast.2), calls=%async_computation | async-start | bytes 1048576 | tf_op jit(solution)/shard_map/all_to_all | solution.py:468
  15.5 0.9 copy-start.12
  15.6 0.8 copy-start.10
  17.1 12.0 %copy-start.4 = (bf16[1440,256]{1,0:T(8,128)(2,1)}, bf16[1440,256]{1,0:T(8,128)(2,1)S(1)}, u32[]{:S(2)}) copy-start(bf16[1440,256]{1,0:T(8,128)(2,1)S(1)} %constant_dynamic-update-slice_fusion.win_ref) | copy-start | bytes 2211844
  26.2 14.1 %collective-permute-start = (bf16[4,128,512]{2,1,0:T(8,128)(2,1)S(1)}, bf16[4,128,512]{2,1,0:T(8,128)(2,1)S(1)}, u32[]{:S(2)}, u32[]{:S(2)}) collective-permute-start(bf16[4,128,512]{2,1,0:T(8,128)(2,1)S(1)} %bias_plane.1.own0_ref), channel_id=1, source_target_pairs={{0,1},{1,2},{2,3},{3,0},{4,5},{5,6},{6,7},{7,4},{8,9},{9,10},{10,1... | collective-permute-start | bytes 1572872 | tf_op jit(solution)/shard_map/ppermute | solution.py:517
  27.6 12.9 %collective-permute-start.2 = (bf16[4,128,512]{2,1,0:T(8,128)(2,1)S(1)}, bf16[4,128,512]{2,1,0:T(8,128)(2,1)S(1)}, u32[]{:S(2)}, u32[]{:S(2)}) collective-permute-start(bf16[4,128,512]{2,1,0:T(8,128)(2,1)S(1)} %bias_plane.1.own0_ref), channel_id=1, source_target_pairs={{0,3},{1,0},{2,1},{3,2},{4,7},{5,4},{6,5},{7,6},{8,11},{9,8},{10,9... | collective-permute-start | bytes 1572872 | tf_op jit(solution)/shard_map/ppermute | solution.py:518
  29.1 24.1 %all-to-all-start.1 = ((bf16[16,5,32,256]{3,2,1,0:T(8,128)(2,1)}), bf16[16,5,32,256]{3,2,1,0:T(8,128)(2,1)}, u32[]{:S(2)}, u32[]{:S(2)}) async-start(bf16[16,5,32,256]{3,2,1,0:T(8,128)(2,1)} %bitcast.17), calls=%async_computation.1 | async-start | bytes 2621440 | tf_op jit(solution)/shard_map/all_to_all | solution.py:524
  40.4 7.5 %collective-permute-start.1 = (bf16[2,128,512]{2,1,0:T(8,128)(2,1)S(1)}, bf16[2,128,512]{2,1,0:T(8,128)(2,1)S(1)}, u32[]{:S(2)}, u32[]{:S(2)}) collective-permute-start(bf16[2,128,512]{2,1,0:T(8,128)(2,1)S(1)} %slice.28), channel_id=1, source_target_pairs={{0,1},{1,2},{2,3},{3,0},{4,5},{5,6},{6,7},{7,4},{8,9},{9,10},{10,1... | collective-permute-start | bytes 786440 | tf_op jit(solution)/shard_map/ppermute | solution.py:520
  40.5 12.7 %copy-start.5 = (bf16[4,128,512]{2,1,0:T(8,128)(2,1)}, bf16[4,128,512]{2,1,0:T(8,128)(2,1)S(1)}, u32[]{:S(2)}) copy-start(bf16[4,128,512]{2,1,0:T(8,128)(2,1)S(1)} %collective-permute-done.2.own3_ref) | copy-start | bytes 1572868
  40.6 7.4 %collective-permute-start.3 = (bf16[2,128,512]{2,1,0:T(8,128)(2,1)S(1)}, bf16[2,128,512]{2,1,0:T(8,128)(2,1)S(1)}, u32[]{:S(2)}, u32[]{:S(2)}) collective-permute-start(bf16[2,128,512]{2,1,0:T(8,128)(2,1)S(1)} %slice.29), channel_id=1, source_target_pairs={{0,3},{1,0},{2,1},{3,2},{4,7},{5,4},{6,5},{7,6},{8,11},{9,8},{10,9... | collective-permute-start | bytes 786440 | tf_op jit(solution)/shard_map/ppermute | solution.py:520
  43.3 7.3 %collective-permute-start.4 = (bf16[4,128,512]{2,1,0:T(8,128)(2,1)S(1)}, bf16[4,128,512]{2,1,0:T(8,128)(2,1)S(1)}, u32[]{:S(2)}, u32[]{:S(2)}) collective-permute-start(bf16[4,128,512]{2,1,0:T(8,128)(2,1)S(1)} %bias_plane.1.own0_ref), channel_id=1, source_target_pairs={{0,8},{8,0},{1,9},{9,1},{2,10},{10,2},{3,11},{11,3},{4,12},{12,4},... | collective-permute-start | bytes 1572872 | tf_op jit(solution)/shard_map/ppermute | solution.py:523
  45.4 5.2 %collective-permute-start.7 = (bf16[4,128,512]{2,1,0:T(8,128)(2,1)S(1)}, bf16[4,128,512]{2,1,0:T(8,128)(2,1)S(1)}, u32[]{:S(2)}, u32[]{:S(2)}) collective-permute-start(bf16[4,128,512]{2,1,0:T(8,128)(2,1)S(1)} %collective-permute-done.2.own3_ref), channel_id=1, source_target_pairs={{0,8},{8,0},{1,9},{9,1},{2,10},{10,2},{3,11},{11,3},{4,12},{12,4},... | collective-permute-start | bytes 1572872 | tf_op jit(solution)/shard_map/ppermute | solution.py:523
  45.4 6.1 %collective-permute-start.5 = (bf16[4,128,512]{2,1,0:T(8,128)(2,1)S(1)}, bf16[4,128,512]{2,1,0:T(8,128)(2,1)}, u32[]{:S(2)}, u32[]{:S(2)}) collective-permute-start(bf16[4,128,512]{2,1,0:T(8,128)(2,1)S(1)} %collective-permute-done.own1_ref), channel_id=1, source_target_pairs={{0,8},{8,0},{1,9},{9,1},{2,10},{10,2},{3,11},{11,3},{4,12},{12,4},... | collective-permute-start | bytes 1572872 | tf_op jit(solution)/shard_map/ppermute | solution.py:523
  48.0 5.2 %collective-permute-start.6 = (bf16[4,128,512]{2,1,0:T(8,128)(2,1)S(1)}, bf16[4,128,512]{2,1,0:T(8,128)(2,1)}, u32[]{:S(2)}, u32[]{:S(2)}) collective-permute-start(bf16[4,128,512]{2,1,0:T(8,128)(2,1)S(1)} %constant_dynamic-update-slice_fusion.7.own2_ref), channel_id=1, source_target_pairs={{0,8},{8,0},{1,9},{9,1},{2,10},{10,2},{3,11},{11,3},{4,12},{12,4},... | collective-permute-start | bytes 1572872 | tf_op jit(solution)/shard_map/ppermute | solution.py:523
  50.6 2.7 %copy-start.6 = (bf16[4,128,512]{2,1,0:T(8,128)(2,1)}, bf16[4,128,512]{2,1,0:T(8,128)(2,1)S(1)}, u32[]{:S(2)}) copy-start(bf16[4,128,512]{2,1,0:T(8,128)(2,1)S(1)} %collective-permute-done.4.other0_ref) | copy-start | bytes 1572868
  50.6 0.9 copy-start.7
  119.8 6.4 %collective-permute-start.8 = (bf16[128,80,128]{2,1,0:T(8,128)(2,1)}, bf16[128,80,128]{2,1,0:T(8,128)(2,1)}, u32[]{:S(2)}, u32[]{:S(2)}) collective-permute-start(bf16[128,80,128]{2,1,0:T(8,128)(2,1)} %all_to_all.30), channel_id=1, source_target_pairs={{0,8},{8,0},{1,9},{9,1},{2,10},{10,2},{3,11},{11,3},{4,12},{12,4},... | collective-permute-start | bytes 7864328 | tf_op jit(solution)/shard_map/ppermute | solution.py:531
  121.4 22.3 %all-to-all-start.3 = ((bf16[16,5,32,256]{3,2,1,0:T(8,128)(2,1)}), bf16[16,5,32,256]{3,2,1,0:T(8,128)(2,1)S(1)}, u32[]{:S(2)}, u32[]{:S(2)}) async-start(bf16[16,5,32,256]{3,2,1,0:T(8,128)(2,1)} %get-tuple-element.41), calls=%async_computation.3 | async-start | bytes 2621440 | tf_op jit(solution)/shard_map/all_to_all | solution.py:537
  129.9 1.0 copy-start.1
  168.5 18.7 %all-to-all-start.5 = ((bf16[128,16,128]{2,1,0:T(8,128)(2,1)}), bf16[128,16,128]{2,1,0:T(8,128)(2,1)S(1)}, u32[]{:S(2)}, u32[]{:S(2)}) async-start(bf16[128,16,128]{2,1,0:T(8,128)(2,1)} %triangle.1), calls=%async_computation.5 | async-start | bytes 1048576 | tf_op jit(solution)/shard_map/all_to_all | solution.py:557
  173.2 1.2 copy-start.2

commit v10 on v8

--- a/solution.py
+++ b/solution.py
@@ -43,8 +43,18 @@
     return pltpu.CompilerParams(vmem_limit_bytes=mib * MB)
 
 
-def bias_kernel(pair_ref, weight_ref, out_ref, normed_ref, bias_ref):
-    normed_ref[...] = layer_norm(pair_ref[...])
+def bias_kernel(pair_ref, weight_ref, out_ref, normed_ref, bias_ref, held_ref, sem_ref):
+    copies = [
+        pltpu.make_async_copy(
+            pair_ref.at[pl.ds(8 * n, 8)], held_ref.at[pl.ds(8 * n, 8)], sem_ref.at[n]
+        )
+        for n in range(4)
+    ]
+    for copy in copies:
+        copy.start()
+    for n, copy in enumerate(copies):
+        copy.wait()
+        normed_ref[8 * n : 8 * n + 8] = layer_norm(held_ref[8 * n : 8 * n + 8])
     for w in range(16):
         block = jnp.concatenate([normed_ref[:, jq * 16 + w, :] for jq in range(4)], axis=0)
         bias_ref[:, w, :] = lax.dot_general(
@@ -61,8 +71,17 @@
     return pl.pallas_call(
         bias_kernel,
         out_shape=jax.ShapeDtypeStruct((8, 2, 2, 64, 128), BF16),
-        scratch_shapes=[pltpu.VMEM((32, 64, 128), F32), pltpu.VMEM((8, 16, 128), F32)],
-        compiler_params=params(16),
+        in_specs=[
+            pl.BlockSpec(memory_space=pl.ANY),
+            pl.BlockSpec(memory_space=pltpu.VMEM),
+        ],
+        scratch_shapes=[
+            pltpu.VMEM((32, 64, 128), F32),
+            pltpu.VMEM((8, 16, 128), F32),
+            pltpu.VMEM((32, 64, 128), BF16),
+            pltpu.SemaphoreType.DMA((4,)),
+        ],
+        compiler_params=params(60),
         name="pair_bias",
     )(pairwise, weight)
 

time: 185 us -> 185 us (level)
  Pallas kernels: 37.4 us -> 39.4 us
    pallas_call x1, Pallas kernels: 2.11 us -> 4.1 us  [pair_bias(): pl.pallas_call(bias_kernel, out_shape=jax.ShapeDtypeStruct((8, 2, 2, 64,...]
    unnamed x43 -> x39, local copies, waits for them, and re-layouts: 4.34 us -> 2.62 us
where the time goes in v10:
time: 185 us; the launch traced here: 184 us
  blocking collectives  64.2 us (35%)
  Pallas kernels  39.4 us (21%)
  starting transfers between devices  35.7 us (19%)
  waiting for transfers between devices  34.2 us (18%)
  local copies, waits for them, and re-layouts  8.51 us (5%)
    all_to_all x1, blocking collectives, body(): lax.all_to_all(factors.reshape(128, 80, 128), ALL, split_axis=0, concat_a...  41.2 us
    all_to_all x1, blocking collectives, body(): blocks = lax.all_to_all(tri, ALL, split_axis=0, concat_axis=0, tiled=True)  23 us
    pallas_call x1, Pallas kernels, attention(): pl.pallas_call(attention_kernel, grid=(count,), in_specs=[smem, *(whole(b...  21 us
    all_to_all x1, waiting for transfers between devices, body(): lax.all_to_all(product, ALL, split_axis=0, concat_axis=0, tiled=True)  11.6 us
    all_to_all x1, starting transfers between devices, body(): lax.all_to_all(pair_bias(pairwise, bias_project.T).reshape(32, 64, 128),...  9.44 us
    all_to_all x1, waiting for transfers between devices, body(): lax.all_to_all(pair_bias(pairwise, bias_project.T).reshape(32, 64, 128),...  8.33 us
    pallas_call x1, Pallas kernels, outer_update(): pl.pallas_call(outer_kernel, in_specs=[pl.BlockSpec(memory_space=pltpu.SM...  8.24 us
    ppermute x1, waiting for transfers between devices, body(): left_plane = lax.ppermute(bias_plane, 'y', up)  5.89 us
  transfers between devices with their start and end apart: 13, of which 7 were waited for; matrix products, arithmetic and copies ran while one was open for 4% of the time, Pallas kernels for 6%

profile of v10, /device:TPU:1, one launch (start us, length us, event | category | flops | bytes accessed | tf_op | source)
XLA Modules:
  0.0 184.5 jit_solution(3247989286980462531)
XLA Ops:
  0.7 4.1 %pair_bias.1 = bf16[8,2,2,64,128]{4,3,2,1,0:T(8,128)(2,1)} custom-call(bf16[32,64,128]{2,1,0:T(8,128)(2,1)} %pair_ref.1, bf16[8,128]{1,0:T(8,128)(2,1)} %bitcast.69), custom_call_target="tpu_custom_call" | custom-call | tf_op jit(solution)/shard_map/pair_bias/pallas_call | solution.py:71
  4.8 9.4 %all-to-all-start = ((bf16[32,64,128]{2,1,0:T(8,128)(2,1)}), bf16[32,64,128]{2,1,0:T(8,128)(2,1)S(1)}, u32[]{:S(2)}, u32[]{:S(2)}) async-start(bf16[32,64,128]{2,1,0:T(8,128)(2,1)} %bitcast.65), calls=%async_computation | async-start | bytes 1048576 | tf_op jit(solution)/shard_map/all_to_all | solution.py:465
  14.3 0.7 convert_reduce_fusion
  15.0 0.1 dynamic_slice.11
  15.0 0.1 dynamic_slice.10
  15.1 0.1 dynamic_slice.9
  15.2 0.1 mul.73
  15.3 0.1 mul.80
  15.4 0.1 copy.38
  15.4 0.1 mul.75
  15.5 0.1 mul.76
  15.6 0.1 copy.37
  15.7 0.1 copy.36
  15.9 0.0 copy-start.10
  15.9 0.1 copy.35
  16.0 0.0 copy-start.8
  16.1 0.3 copy.39
  16.4 0.4 copy-done.10
  16.9 0.7 maximum_divide_fusion
  17.5 0.1 pad_add_fusion.place_ref
  17.6 8.3 %all-to-all-done.in_ref = bf16[32,64,128]{2,1,0:T(8,128)(2,1)S(1)} async-done(((bf16[32,64,128]{2,1,0:T(8,128)(2,1)}), bf16[32,64,128]{2,1,0:T(8,128)(2,1)S(1)}, u32[]{:S(2)}, u32[]{:S(2)}) %all-to-all-start) | async-done | bytes 524320 | tf_op jit(solution)/shard_map/all_to_all | solution.py:465
  26.0 0.1 broadcast_in_dim.2.live_col_ref
  26.1 0.5 bias_plane.1.own0_ref
  26.6 1.4 collective-permute-start
  27.9 1.5 collective-permute-start.2
  29.5 5.4 %all-to-all-start.1 = ((bf16[16,5,32,256]{3,2,1,0:T(8,128)(2,1)}), bf16[16,5,32,256]{3,2,1,0:T(8,128)(2,1)}, u32[]{:S(2)}, u32[]{:S(2)}) async-start(bf16[16,5,32,256]{3,2,1,0:T(8,128)(2,1)} %bitcast.17), calls=%async_computation.1 | async-start | bytes 2621440 | tf_op jit(solution)/shard_map/all_to_all | solution.py:521
  34.8 5.9 %collective-permute-done.own1_ref = bf16[4,128,512]{2,1,0:T(8,128)(2,1)S(1)} collective-permute-done((bf16[4,128,512]{2,1,0:T(8,128)(2,1)S(1)}, bf16[4,128,512]{2,1,0:T(8,128)(2,1)S(1)}, u32[]{:S(2)}, u32[]{:S(2)}) %collective-permute-start) | collective-permute-done | bytes 524320 | tf_op jit(solution)/shard_map/ppermute | solution.py:514
  40.7 0.1 collective-permute-start.1
  40.8 0.0 collective-permute-done.2.own3_ref
  40.8 0.0 copy-start.3
  40.9 2.7 %collective-permute-start.3 = (bf16[2,128,512]{2,1,0:T(8,128)(2,1)S(1)}, bf16[2,128,512]{2,1,0:T(8,128)(2,1)S(1)}, u32[]{:S(2)}, u32[]{:S(2)}) collective-permute-start(bf16[2,128,512]{2,1,0:T(8,128)(2,1)S(1)} %slice.29), channel_id=1, source_target_pairs={{0,3},{1,0},{2,1},{3,2},{4,7},{5,4},{6,5},{7,6},{8,11},{9,8},{10,9... | collective-permute-start | bytes 786440 | tf_op jit(solution)/shard_map/ppermute | solution.py:517
  43.6 2.1 %collective-permute-start.4 = (bf16[4,128,512]{2,1,0:T(8,128)(2,1)S(1)}, bf16[4,128,512]{2,1,0:T(8,128)(2,1)S(1)}, u32[]{:S(2)}, u32[]{:S(2)}) collective-permute-start(bf16[4,128,512]{2,1,0:T(8,128)(2,1)S(1)} %bias_plane.1.own0_ref), channel_id=1, source_target_pairs={{0,8},{8,0},{1,9},{9,1},{2,10},{10,2},{3,11},{11,3},{4,12},{12,4},... | collective-permute-start | bytes 1572872 | tf_op jit(solution)/shard_map/ppermute | solution.py:520
  45.7 0.0 collective-permute-start.7
  45.7 0.5 collective-permute-start.5
  46.2 2.1 %collective-permute-done.1 = bf16[2,128,512]{2,1,0:T(8,128)(2,1)S(1)} collective-permute-done((bf16[2,128,512]{2,1,0:T(8,128)(2,1)S(1)}, bf16[2,128,512]{2,1,0:T(8,128)(2,1)S(1)}, u32[]{:S(2)}, u32[]{:S(2)}) %collective-permute-start.1) | collective-permute-done | bytes 262176 | tf_op jit(solution)/shard_map/ppermute | solution.py:517
  48.3 2.5 %collective-permute-start.6 = (bf16[4,128,512]{2,1,0:T(8,128)(2,1)S(1)}, bf16[4,128,512]{2,1,0:T(8,128)(2,1)}, u32[]{:S(2)}, u32[]{:S(2)}) collective-permute-start(bf16[4,128,512]{2,1,0:T(8,128)(2,1)S(1)} %constant_dynamic-update-slice_fusion.7.own2_ref), channel_id=1, source_target_pairs={{0,8},{8,0},{1,9},{9,1},{2,10},{10,2},{3,11},{11,3},{4,12},{12,4},... | collective-permute-start | bytes 1572872 | tf_op jit(solution)/shard_map/ppermute | solution.py:520
  50.9 0.0 collective-permute-done.7.other3_ref
  50.9 0.8 copy-done.5
  51.7 1.8 all-to-all-done.1.x_ref
  53.5 0.0 collective-permute-done.6.other2_ref
  53.5 21.0 %row_attention.1 = (bf16[16,5,32,256]{3,2,1,0:T(8,128)(2,1)}, bf16[8,2,8,5,16,128]{5,4,3,2,1,0:T(8,128)(2,1)}) custom-call(s32[7]{0:T(128)S(1)} %pad_add_fusion.place_ref, bf16[4,128,512]{2,1,0:T(8,128)(2,1)S(1)} %bias_plane.1.own0_ref, bf16[4,128,512]{2,1,0:T(8,128)(2,1)S(1)} %collective-permute-done.own1_ref, ...), custom_call_target="tpu_custom_call" | custom-call | tf_op jit(solution)/shard_map/row_attention/pallas_call | solution.py:238
  74.5 41.2 %all_to_all.30 = bf16[128,80,128]{2,1,0:T(8,128)(2,1)} all-to-all(bf16[128,80,128]{2,1,0:T(8,128)(2,1)} %bitcast.64), channel_id=1, replica_groups=mesh['x'=4,'zl'=2,'core'=2,'zh'=2,'y'=4] {'x','zl','core','zh','y'}, dimensions={0} | all-to-all | bytes 5242880 | tf_op jit(solution)/shard_map/all_to_all | solution.py:523
  115.8 1.6 collective-permute-start.8
  117.3 3.8 %all-to-all-start.3 = ((bf16[16,5,32,256]{3,2,1,0:T(8,128)(2,1)}), bf16[16,5,32,256]{3,2,1,0:T(8,128)(2,1)S(1)}, u32[]{:S(2)}, u32[]{:S(2)}) async-start(bf16[16,5,32,256]{3,2,1,0:T(8,128)(2,1)} %get-tuple-element.41), calls=%async_computation.3 | async-start | bytes 2621440 | tf_op jit(solution)/shard_map/all_to_all | solution.py:534
  121.1 0.1 copy.40.w_ref
  121.3 0.9 collective-permute-done.8
  122.2 1.4 slice.32
  123.6 1.9 %fusion = (bf16[640,8,128]{2,1,0:T(8,128)(2,1)S(1)}, bf16[640,8,128]{2,1,0:T(8,128)(2,1)S(1)}) fusion(bf16[640,16,128]{2,1,0:T(8,128)(2,1)} %bitcast.19), kind=kLoop, calls=%fused_computation.18 | loop fusion | bytes 5242880 | tf_op jit(solution)/shard_map/slice | solution.py:532
  125.5 0.4 copy.51
  125.9 0.0 copy-start
  125.9 0.7 copy_bitcast_fusion
  126.6 0.3 copy-done
  126.9 8.2 %outer_update.1 = (bf16[4,8,64,128]{3,2,1,0:T(8,128)(2,1)S(1)}, bf16[2,8,256,128]{3,2,1,0:T(8,128)(2,1)S(1)}) custom-call(s32[1]{0:T(128)} %bitcast.core_ref, bf16[640,1024]{1,0:T(8,128)(2,1)S(1)} %bitcast.51, bf16[640,1024]{1,0:T(8,128)(2,1)S(1)} %get-tuple-element.53.own_ref, bf16[640,1024]{1,0:T(8,128)(2,1)S(1)} %get-tuple-element.52.other_ref, ...), custom_call_target="tpu_custom_call" | custom-call | tf_op jit(solution)/shard_map/outer_update/pallas_call | solution.py:335
  135.2 0.7 copy.52
  135.8 3.6 %all-to-all-done.3 = bf16[16,5,32,256]{3,2,1,0:T(8,128)(2,1)S(1)} async-done(((bf16[16,5,32,256]{3,2,1,0:T(8,128)(2,1)}), bf16[16,5,32,256]{3,2,1,0:T(8,128)(2,1)S(1)}, u32[]{:S(2)}, u32[]{:S(2)}) %all-to-all-start.3) | async-done | bytes 1310752 | tf_op jit(solution)/shard_map/all_to_all | solution.py:534
  139.4 23.0 %all_to_all.31.in_ref = bf16[128,2,16,128]{3,2,1,0:T(8,128)(2,1)S(1)} all-to-all(bf16[128,2,16,128]{3,2,1,0:T(8,128)(2,1)S(1)} %bitcast.63), channel_id=1, replica_groups=mesh['x'=4,'zl'=2,'core'=2,'zh'=2,'y'=4] {'x','zl','core','zh','y'}, dimensions={0} | all-to-all | bytes 2097152 | tf_op jit(solution)/shard_map/all_to_all | solution.py:552
  162.4 1.9 %triangle.1 = bf16[128,16,128]{2,1,0:T(8,128)(2,1)} custom-call(bf16[128,2,16,128]{3,2,1,0:T(8,128)(2,1)S(1)} %all_to_all.31.in_ref), custom_call_target="tpu_custom_call" | custom-call | tf_op jit(solution)/shard_map/triangle/pallas_call | solution.py:379
  164.3 4.7 %all-to-all-start.5 = ((bf16[128,16,128]{2,1,0:T(8,128)(2,1)}), bf16[128,16,128]{2,1,0:T(8,128)(2,1)S(1)}, u32[]{:S(2)}, u32[]{:S(2)}) async-start(bf16[128,16,128]{2,1,0:T(8,128)(2,1)} %triangle.1), calls=%async_computation.5 | async-start | bytes 1048576 | tf_op jit(solution)/shard_map/all_to_all | solution.py:554
  169.0 0.0 copy-start.1
  169.0 1.1 copied.1
  170.1 1.2 pair_gate.1.gate_ref
  171.3 11.6 %all-to-all-done.5 = bf16[128,16,128]{2,1,0:T(8,128)(2,1)S(1)} async-done(((bf16[128,16,128]{2,1,0:T(8,128)(2,1)}), bf16[128,16,128]{2,1,0:T(8,128)(2,1)S(1)}, u32[]{:S(2)}, u32[]{:S(2)}) %all-to-all-start.5) | async-done | bytes 524320 | tf_op jit(solution)/shard_map/all_to_all | solution.py:554
  182.9 0.1 copy.53
  183.1 1.4 pair_final.1
  (36 shorter events, 0.2 us)
Async XLA Ops:
  0.6 13.6 %copy-start.12 = (s32[640]{0:T(1024)S(1)}, s32[640]{0:T(1024)}, u32[]{:S(2)}) copy-start(s32[640]{0:T(1024)} %param.15) | copy-start | bytes 7684
  0.6 14.4 %copy-start.13 = (s32[512]{0:T(512)S(1)}, s32[512]{0:T(512)}, u32[]{:S(2)}) copy-start(s32[512]{0:T(512)} %param.14) | copy-start | bytes 6148
  0.7 15.0 %copy-start.11 = (bf16[128,128]{1,0:T(8,128)(2,1)S(1)}, bf16[128,128]{1,0:T(8,128)(2,1)}, u32[]{:S(2)}) copy-start(bf16[128,128]{1,0:T(8,128)(2,1)} %param.23) | copy-start | bytes 98308
  0.7 15.1 %copy-start.9 = (bf16[128,4,128]{2,1,0:T(4,128)(2,1)S(1)}, bf16[128,4,128]{2,1,0:T(4,128)(2,1)}, u32[]{:S(2)}) copy-start(bf16[128,4,128]{2,1,0:T(4,128)(2,1)} %param.21) | copy-start | bytes 393220
  0.7 15.2 %copy-start.7 = (bf16[1024,128]{1,0:T(8,128)(2,1)S(1)}, bf16[1024,128]{1,0:T(8,128)(2,1)}, u32[]{:S(2)}) copy-start(bf16[1024,128]{1,0:T(8,128)(2,1)} %param.20) | copy-start | bytes 786436
  0.7 15.3 %copy-start.6 = (bf16[256,4,256]{2,1,0:T(4,128)(2,1)S(1)}, bf16[256,4,256]{2,1,0:T(4,128)(2,1)}, u32[]{:S(2)}) copy-start(bf16[256,4,256]{2,1,0:T(4,128)(2,1)} %param.16) | copy-start | bytes 1572868
  4.8 21.1 %all-to-all-start = ((bf16[32,64,128]{2,1,0:T(8,128)(2,1)}), bf16[32,64,128]{2,1,0:T(8,128)(2,1)S(1)}, u32[]{:S(2)}, u32[]{:S(2)}) async-start(bf16[32,64,128]{2,1,0:T(8,128)(2,1)} %bitcast.65), calls=%async_computation | async-start | bytes 1048576 | tf_op jit(solution)/shard_map/all_to_all | solution.py:465
  15.9 0.9 copy-start.10
  16.0 0.8 copy-start.8
  17.6 11.8 %copy-start.2 = (bf16[1440,256]{1,0:T(8,128)(2,1)}, bf16[1440,256]{1,0:T(8,128)(2,1)S(1)}, u32[]{:S(2)}) copy-start(bf16[1440,256]{1,0:T(8,128)(2,1)S(1)} %constant_dynamic-update-slice_fusion.win_ref) | copy-start | bytes 2211844
  26.6 14.1 %collective-permute-start = (bf16[4,128,512]{2,1,0:T(8,128)(2,1)S(1)}, bf16[4,128,512]{2,1,0:T(8,128)(2,1)S(1)}, u32[]{:S(2)}, u32[]{:S(2)}) collective-permute-start(bf16[4,128,512]{2,1,0:T(8,128)(2,1)S(1)} %bias_plane.1.own0_ref), channel_id=1, source_target_pairs={{0,1},{1,2},{2,3},{3,0},{4,5},{5,6},{6,7},{7,4},{8,9},{9,10},{10,1... | collective-permute-start | bytes 1572872 | tf_op jit(solution)/shard_map/ppermute | solution.py:514
  27.9 12.9 %collective-permute-start.2 = (bf16[4,128,512]{2,1,0:T(8,128)(2,1)S(1)}, bf16[4,128,512]{2,1,0:T(8,128)(2,1)S(1)}, u32[]{:S(2)}, u32[]{:S(2)}) collective-permute-start(bf16[4,128,512]{2,1,0:T(8,128)(2,1)S(1)} %bias_plane.1.own0_ref), channel_id=1, source_target_pairs={{0,3},{1,0},{2,1},{3,2},{4,7},{5,4},{6,5},{7,6},{8,11},{9,8},{10,9... | collective-permute-start | bytes 1572872 | tf_op jit(solution)/shard_map/ppermute | solution.py:515
  29.5 24.1 %all-to-all-start.1 = ((bf16[16,5,32,256]{3,2,1,0:T(8,128)(2,1)}), bf16[16,5,32,256]{3,2,1,0:T(8,128)(2,1)}, u32[]{:S(2)}, u32[]{:S(2)}) async-start(bf16[16,5,32,256]{3,2,1,0:T(8,128)(2,1)} %bitcast.17), calls=%async_computation.1 | async-start | bytes 2621440 | tf_op jit(solution)/shard_map/all_to_all | solution.py:521
  40.7 7.5 %collective-permute-start.1 = (bf16[2,128,512]{2,1,0:T(8,128)(2,1)S(1)}, bf16[2,128,512]{2,1,0:T(8,128)(2,1)S(1)}, u32[]{:S(2)}, u32[]{:S(2)}) collective-permute-start(bf16[2,128,512]{2,1,0:T(8,128)(2,1)S(1)} %slice.28), channel_id=1, source_target_pairs={{0,1},{1,2},{2,3},{3,0},{4,5},{5,6},{6,7},{7,4},{8,9},{9,10},{10,1... | collective-permute-start | bytes 786440 | tf_op jit(solution)/shard_map/ppermute | solution.py:517
  40.8 12.7 %copy-start.3 = (bf16[4,128,512]{2,1,0:T(8,128)(2,1)}, bf16[4,128,512]{2,1,0:T(8,128)(2,1)S(1)}, u32[]{:S(2)}) copy-start(bf16[4,128,512]{2,1,0:T(8,128)(2,1)S(1)} %collective-permute-done.2.own3_ref) | copy-start | bytes 1572868
  40.9 7.4 %collective-permute-start.3 = (bf16[2,128,512]{2,1,0:T(8,128)(2,1)S(1)}, bf16[2,128,512]{2,1,0:T(8,128)(2,1)S(1)}, u32[]{:S(2)}, u32[]{:S(2)}) collective-permute-start(bf16[2,128,512]{2,1,0:T(8,128)(2,1)S(1)} %slice.29), channel_id=1, source_target_pairs={{0,3},{1,0},{2,1},{3,2},{4,7},{5,4},{6,5},{7,6},{8,11},{9,8},{10,9... | collective-permute-start | bytes 786440 | tf_op jit(solution)/shard_map/ppermute | solution.py:517
  43.6 7.3 %collective-permute-start.4 = (bf16[4,128,512]{2,1,0:T(8,128)(2,1)S(1)}, bf16[4,128,512]{2,1,0:T(8,128)(2,1)S(1)}, u32[]{:S(2)}, u32[]{:S(2)}) collective-permute-start(bf16[4,128,512]{2,1,0:T(8,128)(2,1)S(1)} %bias_plane.1.own0_ref), channel_id=1, source_target_pairs={{0,8},{8,0},{1,9},{9,1},{2,10},{10,2},{3,11},{11,3},{4,12},{12,4},... | collective-permute-start | bytes 1572872 | tf_op jit(solution)/shard_map/ppermute | solution.py:520
  45.7 5.2 %collective-permute-start.7 = (bf16[4,128,512]{2,1,0:T(8,128)(2,1)S(1)}, bf16[4,128,512]{2,1,0:T(8,128)(2,1)S(1)}, u32[]{:S(2)}, u32[]{:S(2)}) collective-permute-start(bf16[4,128,512]{2,1,0:T(8,128)(2,1)S(1)} %collective-permute-done.2.own3_ref), channel_id=1, source_target_pairs={{0,8},{8,0},{1,9},{9,1},{2,10},{10,2},{3,11},{11,3},{4,12},{12,4},... | collective-permute-start | bytes 1572872 | tf_op jit(solution)/shard_map/ppermute | solution.py:520
  45.7 6.1 %collective-permute-start.5 = (bf16[4,128,512]{2,1,0:T(8,128)(2,1)S(1)}, bf16[4,128,512]{2,1,0:T(8,128)(2,1)}, u32[]{:S(2)}, u32[]{:S(2)}) collective-permute-start(bf16[4,128,512]{2,1,0:T(8,128)(2,1)S(1)} %collective-permute-done.own1_ref), channel_id=1, source_target_pairs={{0,8},{8,0},{1,9},{9,1},{2,10},{10,2},{3,11},{11,3},{4,12},{12,4},... | collective-permute-start | bytes 1572872 | tf_op jit(solution)/shard_map/ppermute | solution.py:520
  48.3 5.2 %collective-permute-start.6 = (bf16[4,128,512]{2,1,0:T(8,128)(2,1)S(1)}, bf16[4,128,512]{2,1,0:T(8,128)(2,1)}, u32[]{:S(2)}, u32[]{:S(2)}) collective-permute-start(bf16[4,128,512]{2,1,0:T(8,128)(2,1)S(1)} %constant_dynamic-update-slice_fusion.7.own2_ref), channel_id=1, source_target_pairs={{0,8},{8,0},{1,9},{9,1},{2,10},{10,2},{3,11},{11,3},{4,12},{12,4},... | collective-permute-start | bytes 1572872 | tf_op jit(solution)/shard_map/ppermute | solution.py:520
  50.9 2.7 %copy-start.4 = (bf16[4,128,512]{2,1,0:T(8,128)(2,1)}, bf16[4,128,512]{2,1,0:T(8,128)(2,1)S(1)}, u32[]{:S(2)}) copy-start(bf16[4,128,512]{2,1,0:T(8,128)(2,1)S(1)} %collective-permute-done.4.other0_ref) | copy-start | bytes 1572868
  50.9 0.8 copy-start.5
  115.8 6.4 %collective-permute-start.8 = (bf16[128,80,128]{2,1,0:T(8,128)(2,1)}, bf16[128,80,128]{2,1,0:T(8,128)(2,1)}, u32[]{:S(2)}, u32[]{:S(2)}) collective-permute-start(bf16[128,80,128]{2,1,0:T(8,128)(2,1)} %all_to_all.30), channel_id=1, source_target_pairs={{0,8},{8,0},{1,9},{9,1},{2,10},{10,2},{3,11},{11,3},{4,12},{12,4},... | collective-permute-start | bytes 7864328 | tf_op jit(solution)/shard_map/ppermute | solution.py:528
  117.3 22.1 %all-to-all-start.3 = ((bf16[16,5,32,256]{3,2,1,0:T(8,128)(2,1)}), bf16[16,5,32,256]{3,2,1,0:T(8,128)(2,1)S(1)}, u32[]{:S(2)}, u32[]{:S(2)}) async-start(bf16[16,5,32,256]{3,2,1,0:T(8,128)(2,1)} %get-tuple-element.41), calls=%async_computation.3 | async-start | bytes 2621440 | tf_op jit(solution)/shard_map/all_to_all | solution.py:534
  125.9 1.0 copy-start
  164.3 18.7 %all-to-all-start.5 = ((bf16[128,16,128]{2,1,0:T(8,128)(2,1)}), bf16[128,16,128]{2,1,0:T(8,128)(2,1)S(1)}, u32[]{:S(2)}, u32[]{:S(2)}) async-start(bf16[128,16,128]{2,1,0:T(8,128)(2,1)} %triangle.1), calls=%async_computation.5 | async-start | bytes 1048576 | tf_op jit(solution)/shard_map/all_to_all | solution.py:554
  169.0 1.2 copy-start.1
